TPU v7x, 32 devices: a whole 2x2x4 slice. The times are simulated.
32 devices in a mesh: seq: 8 (over z, y), head: 4 (over x, core).
Axes of the slice: x: 2, y: 2, z: 4, core: 2. Of those that a mesh axis runs over, the one named last changes fastest.
Arguments:
- features: bfloat16 [20480, 8192], P('seq', 'head'), may hold values from -75 to 75
- state_write: bfloat16 [20480, 128], P('seq'), may hold values from -6 to 6
- state_read: bfloat16 [20480, 128], P('seq'), may hold values from -1.5 to 1.5
- conv_feat: float32 [4, 8192], P(None, 'head'), may hold values from -3 to 3
- conv_state: float32 [4, 256], replicated, may hold values from -3 to 3
- log_decay: float32 [20480, 128], P('seq', 'head'), may hold values from -0.81 to 0, as said below
- skip_weight: float32 [128], P('head'), may hold values from 0.5 to 2
- norm_gain: float32 [8192], P('head'), may hold values from 0.5 to 1.5
Outputs:
- mixed_out: bfloat16 [20480, 8192], P('seq', 'head')
Inputs may be any that keep to these rules, and one draw needn't show every extreme that they name: `log_decay`: every log decay is strictly negative.
All inputs are finite; a program needn't handle non-finite values.
Results may differ from a plain program's by a relative error of at most 0.0094.
Values may be sent and summed in bfloat16 or wider, within the bound.
No kernel may reach another device: no remote copies, remote signals or barrier semaphores. Data moves between devices by JAX's collectives and lax.ppermute only.
A program may use at most 128 MiB of HBM per device.

v0:
```python
import jax
import jax.numpy as jnp
from jax import lax
from jax.sharding import PartitionSpec as P

MIXER_HEADS = 128
HEAD_DIM = 64
BLOCK = 256


EPSILON = 1e-05


def shifted(value, axis, steps):
    count = lax.axis_size(axis)
    leading, last = (max(0, -steps), min(count, count - steps))
    return lax.ppermute(value, axis, [(source, source + steps) for source in range(leading, last)])


def prefix_2(part, axis, combine, identity):
    place = lax.axis_index(axis)
    gathered = jax.tree.map(lambda a: lax.all_gather(a, axis), part)
    state = jax.tree.map(lambda a, e: jnp.zeros_like(a) + jnp.asarray(e, a.dtype), part, identity)

    def one(hop, state):
        return combine(
            state, jax.tree.map(lambda a: lax.dynamic_index_in_dim(a, hop, 0, False), gathered)
        )

    return lax.fori_loop(0, place, one, state)


def conv_silu(extended, kernel_taps, length):
    summed = extended[0:length].astype(jnp.float32) * kernel_taps[0]
    for place in range(1, kernel_taps.shape[0]):
        summed = summed + extended[place : place + length].astype(jnp.float32) * kernel_taps[place]
    return jax.nn.silu(summed).astype(jnp.bfloat16)


def chain_combine(earlier, later):
    return (earlier[0] + later[0], jnp.exp(later[0])[:, None, None] * earlier[1] + later[1])


def on_device(
    features, state_write, state_read, conv_feat, conv_state, log_decay, skip_weight, norm_gain
):
    length = features.shape[0]
    margin = conv_feat.shape[0] - 1
    received = shifted(
        (
            features[length - margin :],
            state_write[length - margin :],
            state_read[length - margin :],
        ),
        "seq",
        1,
    )
    feat_conv = conv_silu(jnp.concatenate([received[0], features], axis=0), conv_feat, length)
    joined = jnp.concatenate(
        [
            jnp.concatenate([received[1], received[2]], axis=1),
            jnp.concatenate([state_write, state_read], axis=1),
        ],
        axis=0,
    )
    state_conv = conv_silu(joined, conv_state, length)
    state_width = state_write.shape[1]
    heads_here = log_decay.shape[1]
    head_dim = features.shape[1] // heads_here
    groups = length // BLOCK
    decay_blocks = log_decay.reshape(groups, BLOCK, heads_here)
    cumulative = jnp.cumsum(decay_blocks, axis=1)
    group_total = cumulative[:, -1]
    scaling = jnp.sqrt(-jnp.expm1(2.0 * decay_blocks))
    feat_blocks = feat_conv.reshape(groups, BLOCK, heads_here, head_dim)
    write_blocks = state_conv[:, :state_width].reshape(groups, BLOCK, state_width)
    read_blocks = state_conv[:, state_width:].reshape(groups, BLOCK, state_width)
    decayed = (
        (jnp.exp(group_total[:, None, :] - cumulative) * scaling)[..., None] * feat_blocks
    ).astype(jnp.bfloat16)
    contrib = jnp.einsum(
        "kqn,kqhp->khpn", write_blocks, decayed, preferred_element_type=jnp.float32
    )

    def advance(carried, pieces):
        return (jnp.exp(pieces[0])[:, None, None] * carried + pieces[1], carried)

    empty_state = jnp.zeros((heads_here, head_dim, state_width), jnp.float32)
    end_state, starts = lax.scan(advance, empty_state, (group_total, contrib))
    device_total = jnp.sum(group_total, axis=0)
    prefix = prefix_2(
        (device_total, end_state), "seq", chain_combine, (jnp.zeros_like(device_total), empty_state)
    )
    carried_in = prefix[1]
    before = jnp.cumsum(group_total, axis=0) - group_total
    group_states = (starts + jnp.exp(before)[:, :, None, None] * carried_in[None]).astype(
        jnp.bfloat16
    )
    causal_mask = jnp.tril(jnp.ones((BLOCK, BLOCK), dtype=bool))

    def group_output(pieces):
        read_rows, write_rows, cumul_rows, scales, feature_rows, state_now = pieces
        scores = jnp.dot(read_rows, write_rows.T, preferred_element_type=jnp.float32)
        cum_heads = cumul_rows.T
        decay_gaps = jnp.where(
            causal_mask[None], cum_heads[:, :, None] - cum_heads[:, None, :], -1e30
        )
        mixing = (scores[None] * jnp.exp(decay_gaps) * scales.T[:, None, :]).astype(jnp.bfloat16)
        within = jnp.einsum(
            "hts,shp->thp", mixing, feature_rows, preferred_element_type=jnp.float32
        )
        from_state = (
            jnp.einsum("tn,hpn->thp", read_rows, state_now, preferred_element_type=jnp.float32)
            * jnp.exp(cumul_rows)[:, :, None]
        )
        return within + from_state + skip_weight[None, :, None] * feature_rows.astype(jnp.float32)

    outputs = lax.map(
        group_output, (read_blocks, write_blocks, cumulative, scaling, feat_blocks, group_states)
    )
    mixed_rows = outputs.reshape(length, heads_here * head_dim)
    totals = lax.psum(jnp.sum(mixed_rows * mixed_rows, axis=1), "head")
    scale_rows = lax.rsqrt(totals / (MIXER_HEADS * HEAD_DIM) + EPSILON)
    return (mixed_rows * scale_rows[:, None] * norm_gain[None, :]).astype(jnp.bfloat16)


def solution(mesh):
    placed = (
        P("seq", "head"),
        P("seq", None),
        P("seq", None),
        P(None, "head"),
        P(),
        P("seq", "head"),
        P("head"),
        P("head"),
    )
    return jax.shard_map(
        on_device, mesh=mesh, in_specs=placed, out_specs=P("seq", "head"), check_vma=False
    )
```

profile of v0, /device:TPU:28, one launch (start us, length us, event | category | flops | bytes accessed | tf_op | source)
XLA Modules:
  0.0 469.2 jit_solution(16500940386854284201)
XLA Ops:
  7.2 1.3 collective-permute-start.2
  9.2 1.3 collective-permute-start.1
  10.5 1.4 slice.66
  11.9 1.3 collective-permute-start
  14.4 1.5 fusion.33
  17.2 5.8 %reduce-window.6 = f32[10,32,2,128]{3,1,2,0:T(8,128)S(1)} reduce-window(f32[10,32,2,128]{3,1,2,0:T(8,128)S(1)} %copy.41, f32[]{:T(128)} %constant.73.clone.1), window={size=1x1x1x128 pad=0_0x0_0x0_0x127_0}, to_apply=%region_0.1 | reduce-window | flops 10403840 | bytes 655364 | tf_op jit(solution)/shard_map/reduce-window
  25.4 1.4 exponential_multiply_fusion
  28.6 1.6 multiply_convert_fusion.7
  30.3 26.1 %multiply_convert_fusion.6 = bf16[2560,2048]{1,0:T(8,128)(2,1)} fusion(bf16[2560,2048]{1,0:T(8,128)(2,1)} %param.14, bf16[3,2048]{1,0:T(4,128)(2,1)} %collective-permute-done, f32[2048]{0:T(1024)} %bitcast.126, f32[2048]{0:T(1024)} %bitcast.127, f32[2048]{0:T(1024)} %bitcast.125, f32[2048]{0:T(1024)S(1)} %bitcast.124), kind=kLoop, calls=%fused_computation.44 | loop fusion | flops 131072000 | bytes 21016576 | tf_op jit(solution)/shard_map/convert_element_type | solution.py:37
  56.4 13.8 %copy.39 = bf16[2560,2048]{0,1:T(8,128)(2,1)} copy(bf16[2560,2048]{1,0:T(8,128)(2,1)} %multiply_convert_fusion.6) | data formatting | bytes 20971520 | tf_op jit(solution)/shard_map/convert_element_type | solution.py:37
  70.3 20.9 %reshape.66 = bf16[10,256,32,64]{1,0,3,2:T(8,128)(2,1)} reshape(bf16[2560,2048]{0,1:T(8,128)(2,1)} %copy.39) | data formatting | bytes 20971520 | tf_op jit(solution)/shard_map/reshape | solution.py:75
  91.2 14.7 %multiply_convert_fusion.4 = bf16[10,256,32,64]{1,0,3,2:T(8,128)(2,1)} fusion(bf16[10,256,32,64]{1,0,3,2:T(8,128)(2,1)} %reshape.66, f32[10,256,32]{1,0,2:T(8,128)S(1)} %copy-done.2), kind=kLoop, calls=%fused_computation.41 | loop fusion | flops 15728640 | bytes 21299200 | tf_op jit(solution)/shard_map/convert_element_type | solution.py:80
  105.9 13.4 %fusion.30 = f32[10,32,64,128]{3,2,1,0:T(8,128)} fusion(bf16[10,256,128,1]{2,1,3,0:T(8,128)(2,1)S(1)} %bitcast.112, bf16[10,256,32,64]{1,0,3,2:T(8,128)(2,1)} %multiply_convert_fusion.4), kind=kOutput, calls=%fused_computation.50 | convolution fusion | flops 1342177280 | bytes 21626880 | tf_op jit(solution)/shard_map/kqn,kqhp->khpn/dot_general | solution.py:81
  119.3 25.1 %while.38 = (s32[]{:T(128)}, f32[32,64,128]{2,1,0:T(8,128)S(1)}, f32[10,32,64,128]{3,2,1,0:T(8,128)}, f32[10,32]{1,0:T(8,128)S(1)}, f32[10,32,64,128]{3,2,1,0:T(8,128)}, /*index=5*/s32[]{:T(128)}, s32[]{:T(128)}) while((s32[]{:T(128)}, f32[32,64,128]{2,1,0:T(8,128)S(1)}, f32[10,32,64,128]{3,2,1,0:T(8,128)}, ...), condition=%wide.region_3.4_spmd.clone, body=%wide.region_2.3_spmd.clone.sunk | while | flops 1048579 | bytes 5243372 | solution.py:89
  120.4 1.4 bitcast_add_fusion.6
  122.8 1.4 bitcast_add_fusion.6
  125.3 1.4 bitcast_add_fusion.6
  127.8 1.4 bitcast_add_fusion.6
  130.4 1.4 bitcast_add_fusion.6
  132.9 1.4 bitcast_add_fusion.6
  135.4 1.4 bitcast_add_fusion.6
  137.9 1.4 bitcast_add_fusion.6
  140.4 1.4 bitcast_add_fusion.6
  143.0 1.4 bitcast_add_fusion.6
  147.0 21.8 %all-reduce = f32[256]{0:T(256)S(1)} all-reduce(f32[256]{0:T(256)S(1)} %dynamic-update-slice), channel_id=2, replica_groups=mesh['seq'=8,'head'=4] {'seq'}, use_global_device_ids=true, to_apply=%add | all-reduce | flops 256 | bytes 2048
  168.9 12.6 %copy.47 = bf16[10,256,32,64]{1,3,2,0:T(8,128)(2,1)} copy(bf16[10,256,32,64]{1,0,3,2:T(8,128)(2,1)} %reshape.66) | data formatting | bytes 20971520
  181.5 92.0 %all-gather.4.cloned.1.call-done = f32[256,64,128]{2,1,0:T(8,128)} async-done(((f32[32,64,128]{2,1,0:T(8,128)}), f32[256,64,128]{2,1,0:T(8,128)}) %all-gather.4.cloned.1.call-update) | async-done | bytes 8388624 | tf_op jit(solution)/shard_map/all_gather | solution.py:22
  273.6 10.4 %while.36 = (s32[]{:T(128)}, f32[32,64,128]{2,1,0:T(8,128)S(1)}, s32[]{:T(128)}, f32[8,32]{1,0:T(8,128)S(1)}, f32[8,32,64,128]{3,2,1,0:T(8,128)}, /*index=5*/s32[]{:T(128)}, s32[]{:T(128)}, s32[]{:T(128)}) while((s32[]{:T(128)}, f32[32,64,128]{2,1,0:T(8,128)S(1)}, s32[]{:T(128)}, f32[8,32]{1,0:T(8,128)S(1)}, f32[8,32,64,128]{3,2,1,0:T(8,128)}, ...), condition=%wide.region_7.8_spmd, body=%wide.region_6.7_spmd.sunk | while | flops 524293 | bytes 3146247 | solution.py:30
  273.6 1.4 bitcast_add_fusion.5
  275.1 1.4 bitcast_add_fusion.5
  276.6 1.4 bitcast_add_fusion.5
  278.1 1.4 bitcast_add_fusion.5
  279.6 1.4 bitcast_add_fusion.5
  281.1 1.4 bitcast_add_fusion.5
  282.6 1.4 bitcast_add_fusion.5
  284.0 7.6 %add_convert_fusion = bf16[10,32,64,128]{3,2,1,0:T(8,128)(2,1)} fusion(f32[10,32,64,128]{3,2,1,0:T(8,128)} %get-tuple-element.129, f32[32,64,128]{2,1,0:T(8,128)S(1)} %get-tuple-element.131, f32[10,32]{1,0:T(8,128)S(1)} %subtract_exponential_fusion), kind=kLoop, calls=%fused_computation.52 | loop fusion | flops 7864320 | bytes 16778496 | tf_op jit(solution)/shard_map/convert_element_type | solution.py:96
  291.6 80.4 %while.37 = (s32[]{:T(128)}, f32[10,256,32,64]{1,3,2,0:T(8,128)}, bf16[10,256,32,64]{1,3,2,0:T(8,128)(2,1)}, bf16[10,256,128]{2,1,0:T(8,128)(2,1)S(1)}, bf16[10,...) while((s32[]{:T(128)}, f32[10,256,32,64]{1,3,2,0:T(8,128)}, ...), condition=%wide.region_9.10_spmd.clone, body=%wide.region_8.9_spmd.clone.sunk | while | flops 432603136 | bytes 10227313 | solution.py:118
  292.9 1.5 fusion.49
  294.4 5.3 %bitcast_dynamic-update-slice_fusion.4 = f32[10,256,32,64]{1,3,2,0:T(8,128)} fusion(f32[10,256,32,64]{1,3,2,0:T(8,128)} %get-tuple-element.444, s32[]{:T(128)S(6)} %copy.95, f32[256,32,64]{0,2,1:T(8,128)S(1)} %fusion.49, f32[32,256]{1,0:T(8,128)S(1)} %bitcast.119, f32[32,256]{1,0:T(8,128)S(1)} %bitcast.120, f32[256,256]{1,0:T(8,128)S(1)} %fusion.50, ...), kind=kOutput, calls=%fused_computation.11.clone.1 | convolution fusion | flops 281542656 | bytes 6751744 | tf_op jit(solution)/shard_map/while/body/eval_jaxpr/hts,shp->thp/dot_general | solution.py:109
  301.0 1.5 fusion.49
  302.4 5.2 %bitcast_dynamic-update-slice_fusion.4 = f32[10,256,32,64]{1,3,2,0:T(8,128)} fusion(f32[10,256,32,64]{1,3,2,0:T(8,128)} %get-tuple-element.444, s32[]{:T(128)S(6)} %copy.95, f32[256,32,64]{0,2,1:T(8,128)S(1)} %fusion.49, f32[32,256]{1,0:T(8,128)S(1)} %bitcast.119, f32[32,256]{1,0:T(8,128)S(1)} %bitcast.120, f32[256,256]{1,0:T(8,128)S(1)} %fusion.50, ...), kind=kOutput, calls=%fused_computation.11.clone.1 | convolution fusion | flops 281542656 | bytes 6751744 | tf_op jit(solution)/shard_map/while/body/eval_jaxpr/hts,shp->thp/dot_general | solution.py:109
  308.9 1.5 fusion.49
  310.4 5.3 %bitcast_dynamic-update-slice_fusion.4 = f32[10,256,32,64]{1,3,2,0:T(8,128)} fusion(f32[10,256,32,64]{1,3,2,0:T(8,128)} %get-tuple-element.444, s32[]{:T(128)S(6)} %copy.95, f32[256,32,64]{0,2,1:T(8,128)S(1)} %fusion.49, f32[32,256]{1,0:T(8,128)S(1)} %bitcast.119, f32[32,256]{1,0:T(8,128)S(1)} %bitcast.120, f32[256,256]{1,0:T(8,128)S(1)} %fusion.50, ...), kind=kOutput, calls=%fused_computation.11.clone.1 | convolution fusion | flops 281542656 | bytes 6751744 | tf_op jit(solution)/shard_map/while/body/eval_jaxpr/hts,shp->thp/dot_general | solution.py:109
  317.0 1.5 fusion.49
  318.5 5.3 %bitcast_dynamic-update-slice_fusion.4 = f32[10,256,32,64]{1,3,2,0:T(8,128)} fusion(f32[10,256,32,64]{1,3,2,0:T(8,128)} %get-tuple-element.444, s32[]{:T(128)S(6)} %copy.95, f32[256,32,64]{0,2,1:T(8,128)S(1)} %fusion.49, f32[32,256]{1,0:T(8,128)S(1)} %bitcast.119, f32[32,256]{1,0:T(8,128)S(1)} %bitcast.120, f32[256,256]{1,0:T(8,128)S(1)} %fusion.50, ...), kind=kOutput, calls=%fused_computation.11.clone.1 | convolution fusion | flops 281542656 | bytes 6751744 | tf_op jit(solution)/shard_map/while/body/eval_jaxpr/hts,shp->thp/dot_general | solution.py:109
  325.0 1.5 fusion.49
  326.5 5.2 %bitcast_dynamic-update-slice_fusion.4 = f32[10,256,32,64]{1,3,2,0:T(8,128)} fusion(f32[10,256,32,64]{1,3,2,0:T(8,128)} %get-tuple-element.444, s32[]{:T(128)S(6)} %copy.95, f32[256,32,64]{0,2,1:T(8,128)S(1)} %fusion.49, f32[32,256]{1,0:T(8,128)S(1)} %bitcast.119, f32[32,256]{1,0:T(8,128)S(1)} %bitcast.120, f32[256,256]{1,0:T(8,128)S(1)} %fusion.50, ...), kind=kOutput, calls=%fused_computation.11.clone.1 | convolution fusion | flops 281542656 | bytes 6751744 | tf_op jit(solution)/shard_map/while/body/eval_jaxpr/hts,shp->thp/dot_general | solution.py:109
  333.1 1.5 fusion.49
  334.5 5.2 %bitcast_dynamic-update-slice_fusion.4 = f32[10,256,32,64]{1,3,2,0:T(8,128)} fusion(f32[10,256,32,64]{1,3,2,0:T(8,128)} %get-tuple-element.444, s32[]{:T(128)S(6)} %copy.95, f32[256,32,64]{0,2,1:T(8,128)S(1)} %fusion.49, f32[32,256]{1,0:T(8,128)S(1)} %bitcast.119, f32[32,256]{1,0:T(8,128)S(1)} %bitcast.120, f32[256,256]{1,0:T(8,128)S(1)} %fusion.50, ...), kind=kOutput, calls=%fused_computation.11.clone.1 | convolution fusion | flops 281542656 | bytes 6751744 | tf_op jit(solution)/shard_map/while/body/eval_jaxpr/hts,shp->thp/dot_general | solution.py:109
  341.0 1.5 fusion.49
  342.5 5.4 %bitcast_dynamic-update-slice_fusion.4 = f32[10,256,32,64]{1,3,2,0:T(8,128)} fusion(f32[10,256,32,64]{1,3,2,0:T(8,128)} %get-tuple-element.444, s32[]{:T(128)S(6)} %copy.95, f32[256,32,64]{0,2,1:T(8,128)S(1)} %fusion.49, f32[32,256]{1,0:T(8,128)S(1)} %bitcast.119, f32[32,256]{1,0:T(8,128)S(1)} %bitcast.120, f32[256,256]{1,0:T(8,128)S(1)} %fusion.50, ...), kind=kOutput, calls=%fused_computation.11.clone.1 | convolution fusion | flops 281542656 | bytes 6751744 | tf_op jit(solution)/shard_map/while/body/eval_jaxpr/hts,shp->thp/dot_general | solution.py:109
  349.2 1.5 fusion.49
  350.6 5.3 %bitcast_dynamic-update-slice_fusion.4 = f32[10,256,32,64]{1,3,2,0:T(8,128)} fusion(f32[10,256,32,64]{1,3,2,0:T(8,128)} %get-tuple-element.444, s32[]{:T(128)S(6)} %copy.95, f32[256,32,64]{0,2,1:T(8,128)S(1)} %fusion.49, f32[32,256]{1,0:T(8,128)S(1)} %bitcast.119, f32[32,256]{1,0:T(8,128)S(1)} %bitcast.120, f32[256,256]{1,0:T(8,128)S(1)} %fusion.50, ...), kind=kOutput, calls=%fused_computation.11.clone.1 | convolution fusion | flops 281542656 | bytes 6751744 | tf_op jit(solution)/shard_map/while/body/eval_jaxpr/hts,shp->thp/dot_general | solution.py:109
  357.2 1.5 fusion.49
  358.7 5.3 %bitcast_dynamic-update-slice_fusion.4 = f32[10,256,32,64]{1,3,2,0:T(8,128)} fusion(f32[10,256,32,64]{1,3,2,0:T(8,128)} %get-tuple-element.444, s32[]{:T(128)S(6)} %copy.95, f32[256,32,64]{0,2,1:T(8,128)S(1)} %fusion.49, f32[32,256]{1,0:T(8,128)S(1)} %bitcast.119, f32[32,256]{1,0:T(8,128)S(1)} %bitcast.120, f32[256,256]{1,0:T(8,128)S(1)} %fusion.50, ...), kind=kOutput, calls=%fused_computation.11.clone.1 | convolution fusion | flops 281542656 | bytes 6751744 | tf_op jit(solution)/shard_map/while/body/eval_jaxpr/hts,shp->thp/dot_general | solution.py:109
  365.3 1.5 fusion.49
  366.8 5.2 %bitcast_dynamic-update-slice_fusion.4 = f32[10,256,32,64]{1,3,2,0:T(8,128)} fusion(f32[10,256,32,64]{1,3,2,0:T(8,128)} %get-tuple-element.444, s32[]{:T(128)S(6)} %copy.95, f32[256,32,64]{0,2,1:T(8,128)S(1)} %fusion.49, f32[32,256]{1,0:T(8,128)S(1)} %bitcast.119, f32[32,256]{1,0:T(8,128)S(1)} %bitcast.120, f32[256,256]{1,0:T(8,128)S(1)} %fusion.50, ...), kind=kOutput, calls=%fused_computation.11.clone.1 | convolution fusion | flops 281542656 | bytes 6751744 | tf_op jit(solution)/shard_map/while/body/eval_jaxpr/hts,shp->thp/dot_general | solution.py:109
  372.0 8.8 %multiply_reduce_fusion = f32[10,256]{1,0:T(8,128)S(1)} fusion(f32[10,256,32,64]{1,3,2,0:T(8,128)} %get-tuple-element.132), kind=kLoop, calls=%fused_computation.43 | loop fusion | flops 10483200 | bytes 20981760 | tf_op jit(solution)/shard_map/reduce_sum | solution.py:122
  380.7 4.2 copy-done.1
  385.0 21.5 %copy.50 = f32[10,256,32,64]{1,0,3,2:T(8,128)} copy(f32[10,256,32,64]{1,3,2,0:T(8,128)S(1)} %copy-done.1) | data formatting | bytes 41943040 | tf_op jit(solution)/shard_map/while | solution.py:118
  406.4 11.2 %psum.7 = f32[2560]{0:T(1024)S(1)} all-reduce(f32[2560]{0:T(1024)S(1)} %reduce_sum.22), channel_id=1, replica_groups=mesh['seq'=8,'head'=4] {'head'}, use_global_device_ids=true, to_apply=%region_11.12 | all-reduce | flops 2560 | bytes 20480 | tf_op jit(solution)/shard_map/psum | solution.py:122
  417.6 24.7 %copy.60 = f32[256,8,10,256]{3,1,2,0:T(8,128)S(1)} copy(f32[256,8,10,256]{3,2,1,0:T(8,128)} %bitcast.110) | data formatting | bytes 41943040
  442.4 5.5 %multiply_convert_fusion.5 = bf16[2560,2048]{0,1:T(8,128)(2,1)} fusion(f32[2560,2048]{0,1:T(8,128)S(1)} %bitcast.111, f32[2048]{0:T(1024)S(1)} %copy-done.3, f32[2560]{0:T(1024)S(1)} %add_rsqrt_fusion), kind=kLoop, calls=%fused_computation.42 | loop fusion | flops 15728640 | bytes 31475712 | tf_op jit(solution)/shard_map/convert_element_type | solution.py:124
  447.9 14.4 %copy.51 = bf16[2560,2048]{1,0:T(8,128)(2,1)} copy(bf16[2560,2048]{0,1:T(8,128)(2,1)} %multiply_convert_fusion.5) | data formatting | bytes 20971520 | tf_op jit(solution)/shard_map/convert_element_type | solution.py:124
  (138 shorter events, 33.5 us)
Async XLA Ops:
  6.5 21.5 %copy-start.4 = (f32[4,256]{1,0:T(4,128)S(1)}, f32[4,256]{1,0:T(4,128)}, u32[]{:S(2)}) copy-start(f32[4,256]{1,0:T(4,128)} %param.18) | copy-start | bytes 12292
  6.5 266.9 %all-gather.4.cloned.1.call-start = ((), (), s32[]{:S(2)}) async-start(), calls=%async_computation | async-start | bytes 9437184 | tf_op jit(solution)/shard_map/all_gather | solution.py:22
  7.2 21.1 %collective-permute-start.2 = (bf16[3,128]{1,0:T(4,128)(2,1)S(1)}, bf16[3,128]{1,0:T(4,128)(2,1)S(1)}, u32[]{:S(2)}, u32[]{:S(2)}) collective-permute-start(bf16[3,128]{1,0:T(4,128)(2,1)S(1)} %slice.75), channel_id=1, source_target_pairs={{0,4},{4,8},{8,12},{12,16},{16,20},{20,24},{24,28},{1,5},{5,9},{9,... | collective-permute-start | bytes 2312 | tf_op jit(solution)/shard_map/ppermute | solution.py:17
  9.2 19.1 %collective-permute-start.1 = (bf16[3,128]{1,0:T(4,128)(2,1)S(1)}, bf16[3,128]{1,0:T(4,128)(2,1)S(1)}, u32[]{:S(2)}, u32[]{:S(2)}) collective-permute-start(bf16[3,128]{1,0:T(4,128)(2,1)S(1)} %slice.74), channel_id=1, source_target_pairs={{0,4},{4,8},{8,12},{12,16},{16,20},{20,24},{24,28},{1,5},{5,9},{9,... | collective-permute-start | bytes 2312 | tf_op jit(solution)/shard_map/ppermute | solution.py:17
  11.9 18.4 %collective-permute-start = (bf16[3,2048]{1,0:T(4,128)(2,1)}, bf16[3,2048]{1,0:T(4,128)(2,1)}, u32[]{:S(2)}, u32[]{:S(2)}) collective-permute-start(bf16[3,2048]{1,0:T(4,128)(2,1)} %slice.66), channel_id=1, source_target_pairs={{0,4},{4,8},{8,12},{12,16},{16,20},{20,24},{24,28},{1,5},{5,9},{9,... | collective-permute-start | bytes 36872 | tf_op jit(solution)/shard_map/ppermute | solution.py:17
  70.3 21.0 %copy-start.2 = (f32[10,256,32]{1,0,2:T(8,128)S(1)}, f32[10,256,32]{1,0,2:T(8,128)}, u32[]{:S(2)}) copy-start(f32[10,256,32]{1,0,2:T(8,128)} %get-tuple-element.256) | copy-start | bytes 983044
  119.3 26.2 %copy-start.7 = (u32[32]{0:T(128)S(1)}, u32[32]{0:T(128)}, u32[]{:S(2)}) copy-start(u32[32]{0:T(128)} %constant.82) | copy-start | bytes 388
  119.3 27.4 %copy-start.5 = (f32[32]{0:T(128)S(1)}, f32[32]{0:T(128)}, u32[]{:S(2)}) copy-start(f32[32]{0:T(128)} %get-tuple-element.254) | copy-start | bytes 388
  144.4 1.0 copy-start
  284.0 7.6 %copy-start.6 = (f32[32]{0:T(128)S(1)}, f32[32]{0:T(128)}, u32[]{:S(2)}) copy-start(f32[32]{0:T(128)} %param.20) | copy-start | bytes 388
  372.0 13.0 %copy-start.1 = (f32[10,256,32,64]{1,3,2,0:T(8,128)S(1)}, f32[10,256,32,64]{1,3,2,0:T(8,128)}, u32[]{:S(2)}) copy-start(f32[10,256,32,64]{1,3,2,0:T(8,128)} %get-tuple-element.132) | copy-start | bytes 62914564
  417.6 24.7 %copy-start.3 = (f32[2048]{0:T(1024)S(1)}, f32[2048]{0:T(1024)}, u32[]{:S(2)}) copy-start(f32[2048]{0:T(1024)} %param.21) | copy-start | bytes 24580
Sparse Core Ops, SparseCore 0:
  145.5 127.8 all-gather.3
where the time goes:
time: 473 us; the launch traced here: 469 us
  local copies, waits for them, and re-layouts  134 us (28%)
  other arithmetic  108 us (23%)
  waiting for transfers between devices  92 us (19%)
  matrix products  82.8 us (18%)
  blocking collectives  33 us (7%)
  between operations  14.3 us (3%)
    all_gather x1, waiting for transfers between devices, prefix_2(): gathered = jax.tree.map(lambda a: lax.all_gather(a, axis), part)  92 us
    dot_general x10, matrix products, group_output(): jnp.einsum('hts,shp->thp', mixing, feature_rows, preferred_element_type=j...  52.7 us
    unnamed x22, local copies, waits for them, and re-layouts  44.6 us
    convert_element_type x2, other arithmetic, conv_silu(): return jax.nn.silu(summed).astype(jnp.bfloat16)  27.7 us
    unnamed x1, blocking collectives  21.8 us
    while x1, local copies, waits for them, and re-layouts, on_device(): lax.map(group_output, (read_blocks, write_blocks, cumulative, scaling, fe...  21.5 us
    reshape x1, local copies, waits for them, and re-layouts, on_device(): feat_blocks = feat_conv.reshape(groups, BLOCK, heads_here, head_dim)  20.9 us
    dot_general x10, matrix products, group_output(): jnp.einsum('tn,hpn->thp', read_rows, state_now, preferred_element_type=jn...  14.8 us
  transfers between devices with their start and end apart: 4, of which 1 were waited for; matrix products, arithmetic and copies ran while one was open for 7% of the time, Pallas kernels for 0%

commit v1 on v0

v1 whole, which is shorter than its diff:
```python
import functools

import jax
import jax.numpy as jnp
from jax import lax
from jax.experimental import pallas as pl
from jax.experimental.pallas import tpu as pltpu
from jax.sharding import PartitionSpec as P

EPSILON = 1e-05
SUB = 128
ROWS = 256
WIDE = 256
GROUP = 4
F32 = jnp.float32
BF16 = jnp.bfloat16
HIGHEST = lax.Precision.HIGHEST
MIB = 1 << 20

VMEM = pl.BlockSpec(memory_space=pltpu.VMEM)
SMEM = pl.BlockSpec(memory_space=pltpu.SMEM)
ANY = pl.BlockSpec(memory_space=pl.ANY)


def dot(a, b):
    return jnp.dot(a, b, preferred_element_type=F32)


def exact_dot(a, b):
    return jnp.dot(a, b, preferred_element_type=F32, precision=HIGHEST)


def iota(shape, dim):
    return lax.broadcasted_iota(jnp.int32, shape, dim)


def split_pair(value, low):
    high = value.astype(BF16).astype(F32)
    return jnp.where(low, value - high, high).astype(BF16)


def decay_kernel(heads, ld_ref, skip_ref, ab_ref, fe_ref, rows_ref, first_ref, second_ref, cum_ref, sc_ref):
    tokens = ld_ref.shape[0]
    channels = rows_ref.shape[1]
    blocks = tokens // SUB
    width = 4 * heads
    dim_shift = (channels // heads).bit_length() - 1
    lower = (iota((SUB, SUB), 0) >= iota((SUB, SUB), 1)).astype(F32)
    lane = iota((SUB, width), 1)
    low = (lane & heads) != 0
    second = lane >= 2 * heads
    totals, refs = [], []
    for b in range(blocks):
        at = pl.ds(b * SUB, SUB)
        part = ld_ref[at, :]
        decay = jnp.concatenate([part] * 4, axis=1)
        cumul = exact_dot(lower, decay)
        y = 2.0 * decay
        series = -y * (1.0 + y * (1 / 2) * (1.0 + y * (1 / 3) * (1.0 + y * (1 / 4) * (1.0 + y * (1 / 5)))))
        scale = jnp.sqrt(jnp.where(y > -0.1, series, 1.0 - jnp.exp(y)))
        ref = cumul[SUB // 2 - 1 : SUB // 2]
        gap = cumul - ref
        value = jnp.exp(jnp.where(second, -gap, gap)) * jnp.where(second, scale, 1.0)
        ab_ref[at, :] = split_pair(value, low)
        cum_ref[at, :] = cumul
        sc_ref[at, :] = scale
        totals.append(cumul[SUB - 1 : SUB])
        refs.append(ref)
    zero = jnp.zeros_like(totals[0])
    before = [zero]
    for b in range(blocks - 1):
        before.append(before[-1] + totals[b])
    after = [zero] * blocks
    for b in range(blocks - 2, -1, -1):
        after[b] = after[b + 1] + totals[b + 1]
    for b in range(blocks):
        at = pl.ds(b * SUB, SUB)
        cumul = cum_ref[at, :]
        power = jnp.where(second, cumul + before[b], (totals[b] - cumul) + after[b])
        value = jnp.exp(power) * jnp.where(second, 1.0, sc_ref[at, :])
        fe_ref[at, :] = split_pair(value, low)
    rows = [jnp.exp(totals[b] - refs[b] + refs[b + 1]) for b in range(blocks - 1)] + [zero]
    rows.append(jnp.exp(before[-1] + totals[-1]))
    rows.append(jnp.concatenate([skip_ref[...]] * 4, axis=1))
    rows += [zero] * (rows_ref.shape[0] - len(rows))
    head_of = lax.shift_right_logical(iota((width, channels), 1), dim_shift)
    row = iota((width, channels), 0)
    rows_ref[...] = exact_dot(jnp.concatenate(rows, axis=0), (row == head_of).astype(F32))
    match = (row & (heads - 1)) == head_of
    first_ref[...] = (match & (row < 2 * heads)).astype(F32).astype(BF16)
    second_ref[...] = (match & (row >= 2 * heads)).astype(F32).astype(BF16)


def decay_prep(log_decay, skip_weight, channels):
    tokens, heads = log_decay.shape
    blocks = tokens // SUB
    rows = -(-(blocks + 2) // 8) * 8
    width = 4 * heads
    return pl.pallas_call(
        functools.partial(decay_kernel, heads),
        in_specs=[VMEM, VMEM],
        out_specs=[VMEM] * 5,
        out_shape=[
            pltpu.VMEM((tokens, width), BF16),
            pltpu.VMEM((tokens, width), BF16),
            pltpu.VMEM((rows, channels), F32),
            pltpu.VMEM((width, channels), BF16),
            pltpu.VMEM((width, channels), BF16),
        ],
        scratch_shapes=[pltpu.VMEM((tokens, width), F32), pltpu.VMEM((tokens, width), F32)],
        compiler_params=pltpu.CompilerParams(vmem_limit_bytes=12 * MIB),
        cost_estimate=pl.CostEstimate(flops=10**9, bytes_accessed=5 * 10**6, transcendentals=10**6),
        name="decay_prep",
    )(log_decay, skip_weight.reshape(1, heads))


def conv_silu(ref, taps, cols):
    rows = ref.shape[0] - 8
    total = None
    for k in range(4):
        term = ref[pl.ds(5 + k, rows), cols] * (0.5 * taps[k : k + 1])
        total = term if total is None else total + term
    return total + total * jnp.tanh(total)


def conv_kernel(
    place_ref, halo_ref, feat_ref, write_ref, read_ref, taps_ref, state_taps_ref, fe_ref, first_ref, rows_ref,
    *refs,
):
    *x_refs, wt_ref, c_ref, msg_ref, buf, state_buf, carry = refs
    step = pl.program_id(0)
    rows = feat_ref.shape[0]
    channels = feat_ref.shape[1]
    state = write_ref.shape[1]
    quarter = channels // GROUP
    blocks = x_refs[0].shape[0] // SUB

    @pl.when(step == 0)
    def _():
        halo = halo_ref[...].astype(F32)[8:16]
        buf[0:8, :] = halo[:, :channels]
        state_buf[0:8, :] = halo[:, channels:]
        carry[...] = jnp.zeros_like(carry)

    @pl.when(step > 0)
    def _():
        buf[0:8, :] = buf[rows : rows + 8, :]
        state_buf[0:8, :] = state_buf[rows : rows + 8, :]

    state_buf[8:, :state] = write_ref[...].astype(F32)
    state_buf[8:, state:] = read_ref[...].astype(F32)
    conv = conv_silu(state_buf, state_taps_ref[...], slice(None))
    c_ref[...] = conv[:, state:].astype(BF16)
    wt = conv[:, :state].T.astype(BF16)
    wt_ref[...] = wt
    here = pl.ds(pl.multiple_of(step * rows, rows), rows)
    fe = fe_ref[...]
    homes = [(ref, n) for ref in x_refs for n in range(ref.shape[1] // WIDE)]
    for chunk, (x_ref, n) in enumerate(homes):
        cols = pl.ds(chunk * WIDE, WIDE)
        buf[8:, cols] = feat_ref[:, cols].astype(F32)
        x = conv_silu(buf, taps_ref[:, cols], cols)
        x_ref[here, pl.ds(n * WIDE, WIDE)] = x
        decayed = (x * dot(fe, first_ref[:, cols])).astype(BF16)
        q, off = divmod(chunk * WIDE, quarter)
        inside = pl.ds(off, WIDE)
        carry[q, :, inside] += dot(wt, decayed)

    @pl.when(step == pl.num_programs(0) - 1)
    def _():
        place = place_ref[0]
        for q in range(GROUP):
            slot = lax.bitwise_xor(place, q)
            msg_ref[slot, 0:state, :] = carry[q].astype(BF16)
            decay = jnp.broadcast_to(rows_ref[blocks : blocks + 1, q * quarter : (q + 1) * quarter], (16, quarter))
            msg_ref[slot, state:, :] = split_pair(decay, iota((16, quarter), 0) == 1)


def conv_states(parts, place, halo, features, state_write, state_read, conv_feat, conv_state, fe, first, rows):
    tokens, channels = features.shape
    state = state_write.shape[1]
    quarter = channels // GROUP
    width = fe.shape[1]
    return pl.pallas_call(
        conv_kernel,
        grid=(tokens // ROWS,),
        in_specs=[
            SMEM,
            VMEM,
            pl.BlockSpec((ROWS, channels), lambda i: (i, 0)),
            pl.BlockSpec((ROWS, state), lambda i: (i, 0)),
            pl.BlockSpec((ROWS, state), lambda i: (i, 0)),
            VMEM,
            VMEM,
            pl.BlockSpec((ROWS, width), lambda i: (i, 0)),
            VMEM,
            VMEM,
        ],
        out_specs=[VMEM] * len(parts)
        + [
            pl.BlockSpec((state, ROWS), lambda i: (0, i)),
            pl.BlockSpec((ROWS, state), lambda i: (i, 0)),
            VMEM,
        ],
        out_shape=[pltpu.VMEM((tokens, part), F32) for part in parts]
        + [
            pltpu.VMEM((state, tokens), BF16),
            pltpu.VMEM((tokens, state), BF16),
            jax.ShapeDtypeStruct((GROUP, state + 16, quarter), BF16),
        ],
        scratch_shapes=[
            pltpu.VMEM((ROWS + 8, channels), F32),
            pltpu.VMEM((ROWS + 8, 2 * state), F32),
            pltpu.VMEM((GROUP, state, quarter), F32),
        ],
        compiler_params=pltpu.CompilerParams(vmem_limit_bytes=12 * MIB),
        cost_estimate=pl.CostEstimate(flops=10**10, bytes_accessed=10**7, transcendentals=10**6),
        name="conv_states",
    )(place, halo, features, state_write, state_read, conv_feat, conv_state, fe, first, rows)


def scores_kernel(c_ref, wt_ref, sc_ref):
    state = c_ref.shape[1]
    keep = iota((SUB, SUB), 0) >= iota((SUB, SUB), 1)

    for b in range(c_ref.shape[0] // SUB):
        at = pl.ds(b * SUB, SUB)
        c = c_ref[at, :]
        sc_ref[at, 0:SUB] = jnp.where(keep, dot(c, wt_ref[:, at]), 0.0).astype(BF16)
        sc_ref[at, SUB : SUB + state] = c


def block_scores(c, wt):
    tokens, state = c.shape
    return pl.pallas_call(
        scores_kernel,
        in_specs=[VMEM, VMEM],
        out_specs=VMEM,
        out_shape=pltpu.VMEM((tokens, SUB + state), BF16),
        compiler_params=pltpu.CompilerParams(vmem_limit_bytes=12 * MIB),
        cost_estimate=pl.CostEstimate(flops=10**9, bytes_accessed=2 * 10**6, transcendentals=0),
        name="block_scores",
    )(c, wt)


def within_kernel(offset, _, x_ref, sc_ref, wt_ref, ab_ref, first_ref, second_ref, rows_ref, out_ref, start):
    blocks = x_ref.shape[0] // SUB
    start[...] = jnp.zeros_like(start)

    def block(b, _):
        at = pl.ds(pl.multiple_of(b * SUB, SUB), SUB)
        ab = ab_ref[at, :]
        sc = sc_ref[at, :]
        wt = wt_ref[:, at]
        for n in range(x_ref.shape[1] // WIDE):
            cols = pl.ds(offset + n * WIDE, WIDE)
            here = pl.ds(n * WIDE, WIDE)
            x = x_ref[at, here]
            bx = (x * dot(ab, second_ref[:, cols])).astype(BF16)
            now = start[n]
            inner = dot(sc, jnp.concatenate([bx, now.astype(BF16)], axis=0))
            out_ref[at, here] = dot(ab, first_ref[:, cols]) * inner + rows_ref[blocks + 1 : blocks + 2, cols] * x
            start[n] = rows_ref[pl.ds(b, 1), cols] * (now + dot(wt, bx))
        return 0

    lax.fori_loop(0, blocks, block, 0)


def within(offset, after, x, sc, wt, ab, first, second, rows):
    tokens, part = x.shape
    state = wt.shape[0]
    return pl.pallas_call(
        functools.partial(within_kernel, offset),
        in_specs=[ANY] + [VMEM] * 7,
        out_specs=VMEM,
        out_shape=pltpu.VMEM((tokens, part), F32),
        scratch_shapes=[pltpu.VMEM((part // WIDE, state, WIDE), F32)],
        compiler_params=pltpu.CompilerParams(vmem_limit_bytes=8 * MIB),
        cost_estimate=pl.CostEstimate(flops=2 * 10**9, bytes_accessed=16 * tokens * part, transcendentals=0),
        name="within",
    )(after, x, sc, wt, ab, first, second, rows)


def group_kernel(place_ref, msg_ref, r1_ref, r2_ref, r3_ref, total_ref, prefix_ref, decay_ref, held):
    place = place_ref[0]
    state = prefix_ref.shape[1]
    held[place] = msg_ref[0]
    for k, ref in enumerate((r1_ref, r2_ref, r3_ref)):
        held[lax.bitwise_xor(place, k + 1)] = ref[...]
    sofar = jnp.zeros(prefix_ref.shape[1:], F32)
    decays = jnp.ones((1, sofar.shape[1]), F32)
    for j in range(GROUP):
        tail = held[j, state:, :].astype(F32)
        decay = tail[0:1] + tail[1:2]
        prefix_ref[j] = sofar
        decay_ref[j : j + 1, :] = decays
        sofar = decay * sofar + held[j, 0:state, :].astype(F32)
        decays = decay * decays
    total_ref[0:state, :] = sofar.astype(BF16)
    wide = jnp.broadcast_to(decays, (16, decays.shape[1]))
    total_ref[state:, :] = split_pair(wide, iota(wide.shape, 0) == 1)


def group_prefix(place, msg, received):
    _, rows, quarter = msg.shape
    state = rows - 16
    return pl.pallas_call(
        group_kernel,
        in_specs=[SMEM] + [VMEM] * 4,
        out_specs=[VMEM] * 3,
        out_shape=[
            jax.ShapeDtypeStruct((rows, quarter), BF16),
            pltpu.VMEM((GROUP, state, quarter), F32),
            pltpu.VMEM((8, quarter), F32),
        ],
        scratch_shapes=[pltpu.VMEM((GROUP, rows, quarter), BF16)],
        compiler_params=pltpu.CompilerParams(vmem_limit_bytes=12 * MIB),
        name="group_prefix",
    )(place, msg, *received)


def spread_kernel(place_ref, prefix_ref, decay_ref, carried_ref, *out_refs):
    place = place_ref[0]
    state = prefix_ref.shape[1]
    carried = carried_ref[0:state, :].astype(F32)
    for k, ref in enumerate(out_refs):
        j = lax.bitwise_xor(place, k)
        ref[...] = (prefix_ref[j] + decay_ref[pl.ds(j, 1), :] * carried).astype(BF16)


def spread(place, prefix, decay, carried):
    _, state, quarter = prefix.shape
    return pl.pallas_call(
        spread_kernel,
        in_specs=[SMEM] + [VMEM] * 3,
        out_specs=[VMEM] * GROUP,
        out_shape=[jax.ShapeDtypeStruct((state, quarter), BF16)] * GROUP,
        compiler_params=pltpu.CompilerParams(vmem_limit_bytes=12 * MIB),
        name="spread",
    )(place, prefix, decay, carried)


def state_kernel(count, place_ref, c_ref, fe_ref, second_ref, s0, s1, s2, s3, *refs):
    m_refs, out_refs, (sq_ref, start) = refs[:count], refs[count : 2 * count], refs[2 * count :]
    place = place_ref[0]
    tokens = c_ref.shape[0]
    quarter = s0.shape[1]
    for k, ref in enumerate((s0, s1, s2, s3)):
        start[lax.bitwise_xor(place, k)] = ref[...]
    homes = [(m, o, n) for m, o in zip(m_refs, out_refs) for n in range(m.shape[1] // WIDE)]

    def block(b, _):
        at = pl.ds(pl.multiple_of(b * SUB, SUB), SUB)
        c = c_ref[at, :]
        fe = fe_ref[at, :]
        squares = jnp.zeros((SUB, 128), F32)
        for chunk, (m_ref, out_ref, n) in enumerate(homes):
            cols = pl.ds(chunk * WIDE, WIDE)
            here = pl.ds(n * WIDE, WIDE)
            q, off = divmod(chunk * WIDE, quarter)
            value = m_ref[at, here] + dot(fe, second_ref[:, cols]) * dot(c, start[q, :, off : off + WIDE])
            out_ref[at, here] = value
            for lane in range(0, WIDE, 128):
                piece = value[:, lane : lane + 128]
                squares = squares + piece * piece
        sq_ref[pl.ds(b, 1), :] = jnp.sum(squares.T, axis=0, keepdims=True)
        return 0

    lax.fori_loop(0, tokens // SUB, block, 0)


def add_states(place, ms, c, fe, second, pieces):
    tokens, state = c.shape
    quarter = pieces[0].shape[1]
    blocks = tokens // SUB
    return pl.pallas_call(
        functools.partial(state_kernel, len(ms)),
        in_specs=[SMEM] + [VMEM] * (3 + GROUP + len(ms)),
        out_specs=[VMEM] * (len(ms) + 1),
        out_shape=[pltpu.VMEM(m.shape, F32) for m in ms] + [jax.ShapeDtypeStruct((blocks, SUB), F32)],
        scratch_shapes=[pltpu.VMEM((GROUP, state, quarter), BF16)],
        compiler_params=pltpu.CompilerParams(vmem_limit_bytes=8 * MIB),
        name="add_states",
    )(place, c, fe, second, *pieces, *ms)


def norm_kernel(size, count, gain_ref, *refs):
    m_refs, sq_refs, out_ref = refs[:count], refs[count:-1], refs[-1]
    step = pl.program_id(0)
    rows = out_ref.shape[0]
    homes = [(m, n) for m in m_refs for n in range(m.shape[1] // 128)]
    for sub in range(rows // SUB):
        b = step * (rows // SUB) + sub
        total = sq_refs[0][pl.ds(b, 1), :]
        for ref in sq_refs[1:]:
            total = total + ref[pl.ds(b, 1), :]
        scale = lax.rsqrt(total * (1.0 / size) + EPSILON)
        scale = jnp.broadcast_to(scale, (SUB, SUB)).T
        at = pl.ds(pl.multiple_of(b * SUB, SUB), SUB)
        for tile, (m_ref, n) in enumerate(homes):
            cols = pl.ds(tile * 128, 128)
            value = m_ref[at, pl.ds(n * 128, 128)] * scale * gain_ref[:, cols]
            out_ref[pl.ds(sub * SUB, SUB), cols] = value.astype(BF16)


def norm(size, ms, gain, squares):
    tokens = ms[0].shape[0]
    channels = gain.shape[0]
    rows = 512
    return pl.pallas_call(
        functools.partial(norm_kernel, size, len(ms)),
        grid=(tokens // rows,),
        in_specs=[VMEM] * (1 + len(ms) + len(squares)),
        out_specs=pl.BlockSpec((rows, channels), lambda i: (i, 0)),
        out_shape=jax.ShapeDtypeStruct((tokens, channels), BF16),
        compiler_params=pltpu.CompilerParams(vmem_limit_bytes=8 * MIB),
        name="norm",
    )(gain.reshape(1, channels), *ms, *squares)


def later(value, steps):
    count = lax.axis_size("seq")
    return lax.ppermute(value, "seq", [(i, i + steps) for i in range(count - steps)])


def partner(value, axis, mask):
    return lax.ppermute(value, axis, [(i, i ^ mask) for i in range(lax.axis_size(axis))])


def group_carry(total):
    groups = lax.axis_size("seq") // GROUP
    carried = later(total, GROUP)
    state = total.shape[0] - 16
    reach = 1
    while reach < groups - 1:
        got = later(carried, reach * GROUP).astype(F32)
        mine = carried.astype(F32)
        decay = mine[state : state + 1] + mine[state + 1 : state + 2]
        got_decay = got[state : state + 1] + got[state + 1 : state + 2]
        values = mine[:state] + decay * got[:state]
        both = decay * got_decay
        high = both.astype(BF16)
        rest = (both - high.astype(F32)).astype(BF16)
        carried = jnp.concatenate(
            [values.astype(BF16), high, rest, jnp.zeros((14, both.shape[1]), BF16)], axis=0
        )
        reach *= 2
    return carried


def on_device(
    features, state_write, state_read, conv_feat, conv_state, log_decay, skip_weight, norm_gain
):
    tokens, channels = features.shape
    place = lax.rem(lax.axis_index("seq"), GROUP).astype(jnp.int32).reshape(1)
    tail = jnp.concatenate([features[-16:], state_write[-16:], state_read[-16:]], axis=1)
    halo = later(tail, 1)
    ab, fe, rows, first, second = decay_prep(log_decay, skip_weight, channels)
    chunks = channels // WIDE
    cuts = [0, (3 * chunks) // 8 * WIDE, (5 * chunks) // 8 * WIDE, channels]
    parts = [cuts[n + 1] - cuts[n] for n in range(3)]
    *xs, wt, c, msg = conv_states(
        parts, place, halo, features, state_write, state_read, conv_feat, conv_state, fe, first, rows
    )
    received = [partner(msg[k], "seq", k) for k in range(1, GROUP)]
    sc = block_scores(c, wt)
    shared = (sc, wt, ab, first, second, rows)
    ms = [within(cuts[0], place, xs[0], *shared)]
    total, prefix, decay = group_prefix(place, msg, received)
    carried = group_carry(total)
    ms.append(within(cuts[1], total, xs[1], *shared))
    pieces = spread(place, prefix, decay, carried)
    starts = [pieces[0]] + [partner(pieces[k], "seq", k) for k in range(1, GROUP)]
    ms.append(within(cuts[2], pieces[0], xs[2], *shared))
    *ms, squares = add_states(place, ms, c, fe, second, starts)
    others = [partner(squares, "head", k) for k in range(1, lax.axis_size("head"))]
    size = channels * lax.axis_size("head")
    return norm(size, ms, norm_gain, [squares] + others)


def solution(mesh):
    placed = (
        P("seq", "head"),
        P("seq", None),
        P("seq", None),
        P(None, "head"),
        P(),
        P("seq", "head"),
        P("head"),
        P("head"),
    )
    return jax.shard_map(
        on_device, mesh=mesh, in_specs=placed, out_specs=P("seq", "head"), check_vma=False
    )
```

time: 473 us -> 111 us (0.23)
  the two profiles are of different devices: /device:TPU:28 before, /device:TPU:0 now
where the time goes in v1:
time: 111 us
  Pallas kernels  78.4 us (71%)
  starting transfers between devices  18.4 us (17%)
  local copies, waits for them, and re-layouts  11.9 us (11%)
  waiting for transfers between devices  1.93 us (2%)
    pallas_call x1, Pallas kernels, conv_states(): pl.pallas_call(conv_kernel, grid=(tokens // ROWS,), in_specs=[SMEM, VMEM,...  29.6 us
    pallas_call x3, Pallas kernels, within(): pl.pallas_call(functools.partial(within_kernel, offset), in_specs=[ANY] +...  28.6 us
    pallas_call x1, Pallas kernels, add_states(): pl.pallas_call(functools.partial(state_kernel, len(ms)), in_specs=[SMEM]...  10.2 us
    unnamed x19, local copies, waits for them, and re-layouts  9.64 us
    ppermute x2, starting transfers between devices, later(): lax.ppermute(value, 'seq', [(i, i + steps) for i in range(count - steps)])  9.38 us
    ppermute x9, starting transfers between devices, partner(): lax.ppermute(value, axis, [(i, i ^ mask) for i in range(lax.axis_size(axi...  9.03 us
    pallas_call x1, Pallas kernels, norm(): pl.pallas_call(functools.partial(norm_kernel, size, len(ms)), grid=(token...  5.62 us
    pallas_call x1, Pallas kernels, decay_prep(): pl.pallas_call(functools.partial(decay_kernel, heads), in_specs=[VMEM, VM...  3.65 us
  transfers between devices with their start and end apart: 11, of which 2 were waited for; matrix products, arithmetic and copies ran while one was open for 1% of the time, Pallas kernels for 29%

profile of v1, /device:TPU:0, one launch (start us, length us, event | category | flops | bytes accessed | tf_op | source)
XLA Modules:
  0.0 110.8 jit_solution(15001540354296182626)
XLA Ops:
  0.0 0.7 slice.19
  0.7 0.7 slice.20
  1.4 0.8 slice.18
  2.2 4.9 %collective-permute-start = (bf16[16,2304]{1,0:T(8,128)(2,1)S(1)}, bf16[16,2304]{1,0:T(8,128)(2,1)S(1)}, u32[]{:S(2)}, u32[]{:S(2)}) collective-permute-start(bf16[16,2304]{1,0:T(8,128)(2,1)S(1)} %pad_maximum_fusion), channel_id=1, source_target_pairs={{0,4},{4,8},{8,12},{12,16},{16,20},{20,24},{24,28},{1,5},{5,9},{9,... | collective-permute-start | bytes 221192 | tf_op jit(solution)/shard_map/ppermute | solution.py:423
  7.1 1.4 %copy.9.ld_ref = f32[2560,32]{1,0:T(8,128)S(1)} copy(f32[2560,32]{0,1:T(8,128)} %param.13) | data formatting | bytes 655360 | tf_op args[5]
  8.5 0.0 copy-start.8
  8.5 0.6 copy-done.8
  9.2 3.6 %decay_prep.1 = (bf16[2560,128]{1,0:T(8,128)(2,1)S(1)}, bf16[2560,128]{1,0:T(8,128)(2,1)S(1)}, f32[24,2048]{1,0:T(8,128)S(1)}, bf16[128,2048]{1,0:T(8,128)(2,1)S(1)}, bf16[128,2048]{1,0:T(8,128)(2,1)S(1)}) custom-call(f32[2560,32]{1,0:T(8,128)S(1)} %copy.9.ld_ref, f32[1,32]{1,0:T(1,128)S(1)} %bitcast.10), custom_call_target="tpu_custom_call" | custom-call | flops 1000000000 | bytes 5000000 | tf_op jit(solution)/shard_map/decay_prep/pallas_call | solution.py:99
  12.8 0.0 collective-permute-done.halo_ref
  12.8 0.0 copy-start.3
  12.8 4.0 %copy-done.3 = bf16[2560,2048]{1,0:T(8,128)(2,1)S(1)} copy-done((bf16[2560,2048]{1,0:T(8,128)(2,1)S(1)}, bf16[2560,2048]{1,0:T(8,128)(2,1)}, u32[]{:S(2)}) %copy-start.3) | copy-done | bytes 10485784
  16.8 0.0 copy-start.4
  16.8 1.1 copy-done.4
  17.9 0.0 copy-start.5
  17.9 1.1 copy-done.5
  19.0 0.0 copy-start.6
  19.0 0.8 copy-done.6
  19.7 0.0 copy-start.7
  19.7 0.7 copy-done.7
  20.4 29.6 %conv_states.1 = (f32[2560,768]{1,0:T(8,128)S(1)}, f32[2560,512]{1,0:T(8,128)S(1)}, f32[2560,768]{1,0:T(8,128)S(1)}, bf16[128,2560]{1,0:T(8,128)(2,1)S(1)}, bf16...) custom-call(s32[1]{0:T(128)} %bitcast.1.place_ref._, bf16[16,2304]{1,0:T(8,128)(2,1)S(1)} %collective-permute-done.halo_ref, ...), custom_call_target="tpu_custom_call" | custom-call | flops 10000000000 | bytes 10000000 | tf_op jit(solution)/shard_map/conv_states/pallas_call | solution.py:184
  50.0 0.0 copy-start
  50.1 2.6 %collective-permute-start.3 = (bf16[144,512]{1,0:T(8,128)(2,1)S(1)}, bf16[144,512]{1,0:T(8,128)(2,1)S(1)}, u32[]{:S(2)}, u32[]{:S(2)}) collective-permute-start(bf16[144,512]{1,0:T(8,128)(2,1)S(1)} %get-tuple-element.49), channel_id=1, source_target_pairs={{0,12},{4,8},{8,4},{12,0},{16,28},{20,24},{24,20},{28,16},{1,13},{... | collective-permute-start | bytes 442376 | tf_op jit(solution)/shard_map/ppermute | solution.py:427
  52.7 0.4 collective-permute-start.2
  53.1 0.5 collective-permute-start.1
  53.6 0.4 block_scores.1.sc_ref
  54.0 10.0 %within.3.refs_0_ = f32[2560,768]{1,0:T(8,128)S(1)} custom-call(s32[1]{0:T(128)} %bitcast.1.place_ref._, f32[2560,768]{1,0:T(8,128)S(1)} %get-tuple-element.40.x_ref, bf16[2560,256]{1,0:T(8,128)(2,1)S(1)} %block_scores.1.sc_ref, bf16[128,2560]{1,0:T(8,128)(2,1)S(1)} %get-tuple-element.41.wt_ref, bf16[2560,128]{1,0:T(8,128)(2,1)S(1)} %get-tuple-element.42.ab_ref, ...), custom_call_target="tpu_custom_call" | custom-call | flops 2000000000 | bytes 31457280 | tf_op jit(solution)/shard_map/within/pallas_call | solution.py:272
  64.0 0.0 copy-done
  64.0 0.0 collective-permute-done.3.r3_ref
  64.0 0.0 collective-permute-done.2.r2_ref
  64.0 0.0 collective-permute-done.1.r1_ref
  64.0 0.3 group_prefix.1
  64.3 4.5 %collective-permute-start.4 = (bf16[144,512]{1,0:T(8,128)(2,1)S(1)}, bf16[144,512]{1,0:T(8,128)(2,1)S(1)}, u32[]{:S(2)}, u32[]{:S(2)}) collective-permute-start(bf16[144,512]{1,0:T(8,128)(2,1)S(1)} %get-tuple-element.35._), channel_id=1, source_target_pairs={{0,16},{4,20},{8,24},{12,28},{1,17},{5,21},{9,25},{13,29},{2,18},{... | collective-permute-start | bytes 442376 | tf_op jit(solution)/shard_map/ppermute | solution.py:423
  68.8 8.6 %within.4.refs_1_ = f32[2560,512]{1,0:T(8,128)S(1)} custom-call(bf16[144,512]{1,0:T(8,128)(2,1)S(1)} %get-tuple-element.35._, f32[2560,512]{1,0:T(8,128)S(1)} %get-tuple-element.43.x_ref, bf16[2560,256]{1,0:T(8,128)(2,1)S(1)} %block_scores.1.sc_ref, bf16[128,2560]{1,0:T(8,128)(2,1)S(1)} %get-tuple-element.41.wt_ref, ...), custom_call_target="tpu_custom_call" | custom-call | flops 2000000000 | bytes 20971520 | tf_op jit(solution)/shard_map/within/pallas_call | solution.py:272
  77.4 0.0 collective-permute-done.4.carried_ref
  77.5 0.1 spread.1
  77.6 1.6 %collective-permute-start.5 = (bf16[128,512]{1,0:T(8,128)(2,1)S(1)}, bf16[128,512]{1,0:T(8,128)(2,1)S(1)}, u32[]{:S(2)}, u32[]{:S(2)}) collective-permute-start(bf16[128,512]{1,0:T(8,128)(2,1)S(1)} %get-tuple-element.37), channel_id=1, source_target_pairs={{0,4},{4,0},{8,12},{12,8},{16,20},{20,16},{24,28},{28,24},{1,5},{5... | collective-permute-start | bytes 393224 | tf_op jit(solution)/shard_map/ppermute | solution.py:427
  79.2 0.1 collective-permute-start.6
  79.3 1.8 %collective-permute-start.7 = (bf16[128,512]{1,0:T(8,128)(2,1)S(1)}, bf16[128,512]{1,0:T(8,128)(2,1)S(1)}, u32[]{:S(2)}, u32[]{:S(2)}) collective-permute-start(bf16[128,512]{1,0:T(8,128)(2,1)S(1)} %get-tuple-element.39), channel_id=1, source_target_pairs={{0,12},{4,8},{8,4},{12,0},{16,28},{20,24},{24,20},{28,16},{1,13},{... | collective-permute-start | bytes 393224 | tf_op jit(solution)/shard_map/ppermute | solution.py:427
  81.1 0.0 copy-start.1
  81.1 10.0 %within.5.refs_2_ = f32[2560,768]{1,0:T(8,128)S(1)} custom-call(bf16[128,512]{1,0:T(8,128)(2,1)S(1)} %get-tuple-element.36._.s0, f32[2560,768]{1,0:T(8,128)S(1)} %get-tuple-element.44.x_ref, bf16[2560,256]{1,0:T(8,128)(2,1)S(1)} %block_scores.1.sc_ref, bf16[128,2560]{1,0:T(8,128)(2,1)S(1)} %get-tuple-element.41.wt_ref, ...), custom_call_target="tpu_custom_call" | custom-call | flops 2000000000 | bytes 31457280 | tf_op jit(solution)/shard_map/within/pallas_call | solution.py:272
  91.1 0.0 copy-start.2
  91.1 0.0 collective-permute-done.5.s1
  91.1 0.0 collective-permute-done.6.s2
  91.1 0.0 collective-permute-done.7.s3
  91.1 0.0 copy-done.1
  91.2 10.2 %add_states.1 = (f32[2560,768]{1,0:T(8,128)S(1)}, f32[2560,512]{1,0:T(8,128)S(1)}, f32[2560,768]{1,0:T(8,128)S(1)}, f32[20,128]{1,0:T(8,128)S(1)}) custom-call(s32[1]{0:T(128)} %bitcast.1.place_ref._, bf16[2560,128]{1,0:T(8,128)(2,1)S(1)} %copy-done.1, bf16[2560,128]{1,0:T(8,128)(2,1)S(1)} %get-tuple-element.27.fe_ref, ...), custom_call_target="tpu_custom_call" | custom-call | tf_op jit(solution)/shard_map/add_states/pallas_call | solution.py:376
  101.3 0.1 collective-permute-start.10
  101.4 1.6 %collective-permute-start.9 = (f32[20,128]{1,0:T(8,128)S(1)}, f32[20,128]{1,0:T(8,128)S(1)}, u32[]{:S(2)}, u32[]{:S(2)}) collective-permute-start(f32[20,128]{1,0:T(8,128)S(1)} %get-tuple-element.48.refs_3_), channel_id=1, source_target_pairs={{0,2},{1,3},{2,0},{3,1},{4,6},{5,7},{6,4},{7,5},{8,10},{9,11},{10,... | collective-permute-start | bytes 30728 | tf_op jit(solution)/shard_map/ppermute | solution.py:427
  103.0 0.3 collective-permute-start.8
  103.3 1.3 %collective-permute-done.10.refs_6_ = f32[20,128]{1,0:T(8,128)S(1)} collective-permute-done((f32[20,128]{1,0:T(8,128)S(1)}, f32[20,128]{1,0:T(8,128)S(1)}, u32[]{:S(2)}, u32[]{:S(2)}) %collective-permute-start.10) | collective-permute-done | bytes 10272 | tf_op jit(solution)/shard_map/ppermute | solution.py:427
  104.6 0.6 collective-permute-done.9.refs_5_
  105.2 0.0 collective-permute-done.8.refs_4_
  105.2 0.0 copy-done.2
  105.2 5.6 %norm.1 = bf16[2560,2048]{1,0:T(8,128)(2,1)} custom-call(f32[1,2048]{1,0:T(1,128)S(1)} %bitcast.9, f32[2560,768]{1,0:T(8,128)S(1)} %get-tuple-element.45.refs_0_, f32[2560,512]{1,0:T(8,128)S(1)} %get-tuple-element.46.refs_1_, f32[2560,768]{1,0:T(8,128)S(1)} %get-tuple-element.47.refs_2_, f32[20,128]{1,0:T(8,128)S(1)} %get-tuple-element.48.refs_3_, ...), custom_call_target="tpu_custom_call" | custom-call | tf_op jit(solution)/shard_map/norm/pallas_call | solution.py:410
  (2 shorter events, 0.0 us)
Async XLA Ops:
  2.2 10.6 %collective-permute-start = (bf16[16,2304]{1,0:T(8,128)(2,1)S(1)}, bf16[16,2304]{1,0:T(8,128)(2,1)S(1)}, u32[]{:S(2)}, u32[]{:S(2)}) collective-permute-start(bf16[16,2304]{1,0:T(8,128)(2,1)S(1)} %pad_maximum_fusion), channel_id=1, source_target_pairs={{0,4},{4,8},{8,12},{12,16},{16,20},{20,24},{24,28},{1,5},{5,9},{9,... | collective-permute-start | bytes 221192 | tf_op jit(solution)/shard_map/ppermute | solution.py:423
  8.5 0.7 copy-start.8
  12.8 4.0 %copy-start.3 = (bf16[2560,2048]{1,0:T(8,128)(2,1)S(1)}, bf16[2560,2048]{1,0:T(8,128)(2,1)}, u32[]{:S(2)}) copy-start(bf16[2560,2048]{1,0:T(8,128)(2,1)} %feat_ref.1) | copy-start | bytes 31457284
  16.8 1.1 copy-start.4
  17.9 1.1 copy-start.5
  19.0 0.8 copy-start.6
  19.7 0.7 copy-start.7
  50.0 13.9 %copy-start = (bf16[2560,128]{1,0:T(8,128)(2,1)}, bf16[2560,128]{1,0:T(8,128)(2,1)S(1)}, u32[]{:S(2)}) copy-start(bf16[2560,128]{1,0:T(8,128)(2,1)S(1)} %get-tuple-element.30.c_ref) | copy-start | bytes 1966084
  50.1 13.9 %collective-permute-start.3 = (bf16[144,512]{1,0:T(8,128)(2,1)S(1)}, bf16[144,512]{1,0:T(8,128)(2,1)S(1)}, u32[]{:S(2)}, u32[]{:S(2)}) collective-permute-start(bf16[144,512]{1,0:T(8,128)(2,1)S(1)} %get-tuple-element.49), channel_id=1, source_target_pairs={{0,12},{4,8},{8,4},{12,0},{16,28},{20,24},{24,20},{28,16},{1,13},{... | collective-permute-start | bytes 442376 | tf_op jit(solution)/shard_map/ppermute | solution.py:427
  52.7 11.3 %collective-permute-start.2 = (bf16[144,512]{1,0:T(8,128)(2,1)S(1)}, bf16[144,512]{1,0:T(8,128)(2,1)S(1)}, u32[]{:S(2)}, u32[]{:S(2)}) collective-permute-start(bf16[144,512]{1,0:T(8,128)(2,1)S(1)} %get-tuple-element.50), channel_id=1, source_target_pairs={{0,8},{4,12},{8,0},{12,4},{16,24},{20,28},{24,16},{28,20},{1,9},{5... | collective-permute-start | bytes 442376 | tf_op jit(solution)/shard_map/ppermute | solution.py:427
  53.1 10.9 %collective-permute-start.1 = (bf16[144,512]{1,0:T(8,128)(2,1)S(1)}, bf16[144,512]{1,0:T(8,128)(2,1)S(1)}, u32[]{:S(2)}, u32[]{:S(2)}) collective-permute-start(bf16[144,512]{1,0:T(8,128)(2,1)S(1)} %get-tuple-element.51), channel_id=1, source_target_pairs={{0,4},{4,0},{8,12},{12,8},{16,20},{20,16},{24,28},{28,24},{1,5},{5... | collective-permute-start | bytes 442376 | tf_op jit(solution)/shard_map/ppermute | solution.py:427
  64.3 13.2 %collective-permute-start.4 = (bf16[144,512]{1,0:T(8,128)(2,1)S(1)}, bf16[144,512]{1,0:T(8,128)(2,1)S(1)}, u32[]{:S(2)}, u32[]{:S(2)}) collective-permute-start(bf16[144,512]{1,0:T(8,128)(2,1)S(1)} %get-tuple-element.35._), channel_id=1, source_target_pairs={{0,16},{4,20},{8,24},{12,28},{1,17},{5,21},{9,25},{13,29},{2,18},{... | collective-permute-start | bytes 442376 | tf_op jit(solution)/shard_map/ppermute | solution.py:423
  77.6 13.5 %collective-permute-start.5 = (bf16[128,512]{1,0:T(8,128)(2,1)S(1)}, bf16[128,512]{1,0:T(8,128)(2,1)S(1)}, u32[]{:S(2)}, u32[]{:S(2)}) collective-permute-start(bf16[128,512]{1,0:T(8,128)(2,1)S(1)} %get-tuple-element.37), channel_id=1, source_target_pairs={{0,4},{4,0},{8,12},{12,8},{16,20},{20,16},{24,28},{28,24},{1,5},{5... | collective-permute-start | bytes 393224 | tf_op jit(solution)/shard_map/ppermute | solution.py:427
  79.2 12.0 %collective-permute-start.6 = (bf16[128,512]{1,0:T(8,128)(2,1)S(1)}, bf16[128,512]{1,0:T(8,128)(2,1)S(1)}, u32[]{:S(2)}, u32[]{:S(2)}) collective-permute-start(bf16[128,512]{1,0:T(8,128)(2,1)S(1)} %get-tuple-element.38), channel_id=1, source_target_pairs={{0,8},{4,12},{8,0},{12,4},{16,24},{20,28},{24,16},{28,20},{1,9},{5... | collective-permute-start | bytes 393224 | tf_op jit(solution)/shard_map/ppermute | solution.py:427
  79.3 11.8 %collective-permute-start.7 = (bf16[128,512]{1,0:T(8,128)(2,1)S(1)}, bf16[128,512]{1,0:T(8,128)(2,1)S(1)}, u32[]{:S(2)}, u32[]{:S(2)}) collective-permute-start(bf16[128,512]{1,0:T(8,128)(2,1)S(1)} %get-tuple-element.39), channel_id=1, source_target_pairs={{0,12},{4,8},{8,4},{12,0},{16,28},{20,24},{24,20},{28,16},{1,13},{... | collective-permute-start | bytes 393224 | tf_op jit(solution)/shard_map/ppermute | solution.py:427
  81.1 10.0 %copy-start.1 = (bf16[2560,128]{1,0:T(8,128)(2,1)S(1)}, bf16[2560,128]{1,0:T(8,128)(2,1)}, u32[]{:S(2)}) copy-start(bf16[2560,128]{1,0:T(8,128)(2,1)} %copy-done) | copy-start | bytes 1966084
  91.1 14.1 %copy-start.2 = (f32[2048]{0:T(1024)S(1)}, f32[2048]{0:T(1024)}, u32[]{:S(2)}) copy-start(f32[2048]{0:T(1024)} %param.15) | copy-start | bytes 24580
  101.3 3.3 %collective-permute-start.10 = (f32[20,128]{1,0:T(8,128)S(1)}, f32[20,128]{1,0:T(8,128)S(1)}, u32[]{:S(2)}, u32[]{:S(2)}) collective-permute-start(f32[20,128]{1,0:T(8,128)S(1)} %get-tuple-element.48.refs_3_), channel_id=1, source_target_pairs={{0,3},{1,2},{2,1},{3,0},{4,7},{5,6},{6,5},{7,4},{8,11},{9,10},{10,... | collective-permute-start | bytes 30728 | tf_op jit(solution)/shard_map/ppermute | solution.py:427
  101.4 3.8 %collective-permute-start.9 = (f32[20,128]{1,0:T(8,128)S(1)}, f32[20,128]{1,0:T(8,128)S(1)}, u32[]{:S(2)}, u32[]{:S(2)}) collective-permute-start(f32[20,128]{1,0:T(8,128)S(1)} %get-tuple-element.48.refs_3_), channel_id=1, source_target_pairs={{0,2},{1,3},{2,0},{3,1},{4,6},{5,7},{6,4},{7,5},{8,10},{9,11},{10,... | collective-permute-start | bytes 30728 | tf_op jit(solution)/shard_map/ppermute | solution.py:427
  103.0 2.2 %collective-permute-start.8 = (f32[20,128]{1,0:T(8,128)S(1)}, f32[20,128]{1,0:T(8,128)S(1)}, u32[]{:S(2)}, u32[]{:S(2)}) collective-permute-start(f32[20,128]{1,0:T(8,128)S(1)} %get-tuple-element.48.refs_3_), channel_id=1, source_target_pairs={{0,1},{1,0},{2,3},{3,2},{4,5},{5,4},{6,7},{7,6},{8,9},{9,8},{10,11... | collective-permute-start | bytes 30728 | tf_op jit(solution)/shard_map/ppermute | solution.py:427

commit v2 on v1

v2 whole, which is shorter than its diff:
```python
import functools

import jax
import jax.numpy as jnp
from jax import lax
from jax.experimental import pallas as pl
from jax.experimental.pallas import tpu as pltpu
from jax.sharding import PartitionSpec as P

EPSILON = 1e-05
SUB = 128
WIDE = 256
ROWS = 256
RING = 4
GROUP = 4
UNROLL = 4
F32 = jnp.float32
BF16 = jnp.bfloat16
HIGHEST = lax.Precision.HIGHEST
MIB = 1 << 20

VMEM = pl.BlockSpec(memory_space=pltpu.VMEM)
SMEM = pl.BlockSpec(memory_space=pltpu.SMEM)
ANY = pl.BlockSpec(memory_space=pl.ANY)


def dot(a, b):
    return jnp.dot(a, b, preferred_element_type=F32)


def exact_dot(a, b):
    return jnp.dot(a, b, preferred_element_type=F32, precision=HIGHEST)


def iota(shape, dim):
    return lax.broadcasted_iota(jnp.int32, shape, dim)


def split_pair(value, low):
    high = value.astype(BF16).astype(F32)
    return jnp.where(low, value - high, high).astype(BF16)


def per_head(table, group, heads, head_dim, tile):
    shift = head_dim.bit_length() - 1
    lane = lax.shift_right_logical(iota(table.shape, 1), shift)
    return jnp.take_along_axis(table, lane + (group * heads + tile * (128 // head_dim)), axis=1)


def decay_kernel(heads, ld_ref, skip_ref, table_ref, pair_ref, rows_ref, first_ref, second_ref, cum_ref, sc_ref):
    tokens = ld_ref.shape[0]
    channels = rows_ref.shape[1]
    blocks = tokens // SUB
    dim_shift = (channels // heads).bit_length() - 1
    copies = 128 // heads
    lower = (iota((SUB, SUB), 0) >= iota((SUB, SUB), 1)).astype(F32)
    lane = iota((SUB, 128), 1)
    totals, refs = [], []
    for b in range(blocks):
        at = pl.ds(b * SUB, SUB)
        decay = jnp.concatenate([ld_ref[at, :]] * copies, axis=1)
        cumul = exact_dot(lower, decay)
        y = 2.0 * decay
        series = -y * (1.0 + y * (1 / 2) * (1.0 + y * (1 / 3) * (1.0 + y * (1 / 4) * (1.0 + y * (1 / 5)))))
        cum_ref[at, :] = cumul
        sc_ref[at, :] = jnp.sqrt(jnp.where(y > -0.1, series, 1.0 - jnp.exp(y)))
        totals.append(cumul[SUB - 1 : SUB])
        refs.append(cumul[SUB // 2 - 1 : SUB // 2])
    zero = jnp.zeros_like(totals[0])
    before = [zero]
    for b in range(blocks - 1):
        before.append(before[-1] + totals[b])
    after = [zero] * blocks
    for b in range(blocks - 2, -1, -1):
        after[b] = after[b + 1] + totals[b + 1]
    row_lane = iota((1, 128), 1)
    negative = (row_lane >= heads) & (row_lane < 3 * heads)
    scaled = (lane >= heads) & (lane < 3 * heads)
    low = (lane & heads) != 0
    for b in range(blocks):
        at = pl.ds(b * SUB, SUB)
        cumul = cum_ref[at, :]
        base = jnp.where(
            row_lane < heads,
            -refs[b],
            jnp.where(row_lane < 2 * heads, refs[b], jnp.where(row_lane < 3 * heads, totals[b], before[b])),
        )
        power = base + jnp.where(negative, -cumul, cumul) + jnp.where(negative & (row_lane >= 2 * heads), after[b], 0.0)
        table_ref[at, :] = jnp.exp(power) * jnp.where(scaled, sc_ref[at, :], 1.0)
        value = jnp.exp(cumul + jnp.where(row_lane < 2 * heads, -refs[b], before[b]))
        pair_ref[at, :] = split_pair(value, low)
    rows = [jnp.exp(totals[b] - refs[b] + refs[b + 1]) for b in range(blocks - 1)] + [zero]
    rows.append(jnp.exp(before[-1] + totals[-1]))
    rows.append(jnp.concatenate([skip_ref[...]] * copies, axis=1))
    rows += [zero] * (rows_ref.shape[0] - len(rows))
    head_of = lax.shift_right_logical(iota((128, channels), 1), dim_shift)
    row = iota((128, channels), 0)
    rows_ref[...] = exact_dot(jnp.concatenate(rows, axis=0), (row == head_of).astype(F32))
    match = (row & (heads - 1)) == head_of
    first_ref[...] = (match & (row < 2 * heads)).astype(F32).astype(BF16)
    second_ref[...] = (match & (row >= 2 * heads) & (row < 4 * heads)).astype(F32).astype(BF16)


def decay_prep(log_decay, skip_weight, channels):
    tokens, heads = log_decay.shape
    blocks = tokens // SUB
    rows = -(-(blocks + 2) // 8) * 8
    return pl.pallas_call(
        functools.partial(decay_kernel, heads),
        in_specs=[VMEM, VMEM],
        out_specs=[VMEM] * 5,
        out_shape=[
            pltpu.VMEM((tokens, 128), F32),
            pltpu.VMEM((tokens, 128), BF16),
            pltpu.VMEM((rows, channels), F32),
            pltpu.VMEM((128, channels), BF16),
            pltpu.VMEM((128, channels), BF16),
        ],
        scratch_shapes=[pltpu.VMEM((tokens, 128), F32), pltpu.VMEM((tokens, 128), F32)],
        compiler_params=pltpu.CompilerParams(vmem_limit_bytes=8 * MIB),
        cost_estimate=pl.CostEstimate(flops=10**9, bytes_accessed=5 * 10**6, transcendentals=10**6),
        name="decay_prep",
    )(log_decay, skip_weight.reshape(1, heads))


def tail_kernel(feat_ref, write_ref, read_ref, out_ref):
    channels = feat_ref.shape[1]
    state = write_ref.shape[1]
    out_ref[:, :channels] = feat_ref[...]
    out_ref[:, channels : channels + state] = write_ref[...]
    out_ref[:, channels + state :] = read_ref[...]


def tail_rows(features, state_write, state_read):
    tokens, channels = features.shape
    state = state_write.shape[1]
    last = tokens // 16 - 1
    return pl.pallas_call(
        tail_kernel,
        grid=(1,),
        in_specs=[pl.BlockSpec((16, width), lambda i: (last, 0)) for width in (channels, state, state)],
        out_specs=pl.BlockSpec((16, channels + 2 * state), lambda i: (0, 0)),
        out_shape=jax.ShapeDtypeStruct((16, channels + 2 * state), BF16),
        compiler_params=pltpu.CompilerParams(vmem_limit_bytes=2 * MIB),
        name="tail_rows",
    )(*map(in_hbm, (features, state_write, state_read)))


def in_hbm(value):
    return pltpu.with_memory_space_constraint(value, pltpu.HBM)


def conv_silu(ref, base, rows, taps):
    total = None
    for k in range(4):
        term = ref[pl.ds(base + 5 + k, rows), :] * taps[k : k + 1]
        total = term if total is None else total + term
    return total + total * jnp.tanh(total)


def conv_kernel(
    heads, count, place_ref, halo_ref, feat_ref, write_ref, read_ref, taps_ref, state_taps_ref, table_ref, rows_ref,
    *refs,
):
    *x_refs, wt_ref, c_ref, msg_ref, carry, feat_ring, write_ring, read_ring, sems = refs[:-count]
    bufs = refs[-count:]
    tokens, channels = feat_ref.shape
    head_dim = channels // heads
    state = write_ref.shape[1]
    quarter = channels // GROUP
    blocks = tokens // SUB
    homes = [(ref, n) for ref in x_refs for n in range(ref.shape[1] // 128)]
    tiles = len(homes)
    rings = [(feat_ref, feat_ring), (write_ref, write_ring), (read_ref, read_ring)]
    sources = [(feat_ring, n) for n in range(tiles)] + [(write_ring, 0), (read_ring, 0)]

    def copies(b):
        slot = lax.rem(b, RING)
        at = pl.ds(pl.multiple_of(b * SUB, SUB), SUB)
        return [
            pltpu.make_async_copy(ref.at[at, :], ring.at[slot], sems.at[n, slot])
            for n, (ref, ring) in enumerate(rings)
        ]

    for b in range(RING):
        for copy in copies(jnp.int32(b)):
            copy.start()
    halo = halo_ref[...].astype(F32)[8:16] * place_ref[1].astype(F32)
    for n, buf in enumerate(bufs):
        buf[SUB : SUB + 8, :] = halo[:, n * 128 : (n + 1) * 128]
    carry[...] = jnp.zeros_like(carry)
    zero = place_ref[2]

    def block(b, _):
        here = pl.ds(pl.multiple_of(b * SUB, SUB), SUB)
        slot = lax.rem(b, RING)
        table = table_ref[here, :]
        for copy in copies(b):
            copy.wait()

        def conv(n, taps, tile):
            buf = bufs[n]
            source, spot = sources[n]
            buf[0:8, :] = buf[SUB : SUB + 8, :]
            buf[8:, :] = source[slot, :, pl.ds(spot * 128, 128)].astype(F32)
            return conv_silu(buf, zero, SUB, 0.5 * taps[:, pl.ds(tile * 128, 128)])

        wt = conv(tiles, state_taps_ref, 0).T.astype(BF16)
        wt_ref[:, here] = wt
        c_ref[here, :] = conv(tiles + 1, state_taps_ref, 1).astype(BF16)
        decayed = []
        for n, (x_ref, spot) in enumerate(homes):
            x = conv(n, taps_ref, n)
            x_ref[here, pl.ds(spot * 128, 128)] = x
            decayed.append((x * per_head(table, 2, heads, head_dim, n)).astype(BF16))
            if len(decayed) == WIDE // 128:
                q, off = divmod((n + 1) * 128 - WIDE, quarter)
                carry[q, :, pl.ds(off, WIDE)] += dot(wt, jnp.concatenate(decayed, axis=1))
                decayed = []

        @pl.when(b + RING < blocks)
        def _():
            for copy in copies(b + RING):
                copy.start()

        return 0

    lax.fori_loop(0, blocks, block, 0)
    place = place_ref[0]
    for q in range(GROUP):
        slot = lax.bitwise_xor(place, q)
        msg_ref[slot, 0:state, :] = carry[q].astype(BF16)
        decay = jnp.broadcast_to(rows_ref[blocks : blocks + 1, q * quarter : (q + 1) * quarter], (16, quarter))
        msg_ref[slot, state:, :] = split_pair(decay, iota((16, quarter), 0) == 1)


def conv_states(parts, place, halo, features, state_write, state_read, conv_feat, conv_state, table, rows, heads):
    tokens, channels = features.shape
    state = state_write.shape[1]
    quarter = channels // GROUP
    count = (channels + 2 * state) // 128
    return pl.pallas_call(
        functools.partial(conv_kernel, heads, count),
        in_specs=[SMEM, VMEM] + [ANY] * 3 + [VMEM] * 4,
        out_specs=[VMEM] * (len(parts) + 3),
        out_shape=[pltpu.VMEM((tokens, part), F32) for part in parts]
        + [
            pltpu.VMEM((state, tokens), BF16),
            pltpu.VMEM((tokens, state), BF16),
            jax.ShapeDtypeStruct((GROUP, state + 16, quarter), BF16),
        ],
        scratch_shapes=[
            pltpu.VMEM((GROUP, state, quarter), F32),
            pltpu.VMEM((RING, SUB, channels), BF16),
            pltpu.VMEM((RING, SUB, state), BF16),
            pltpu.VMEM((RING, SUB, state), BF16),
            pltpu.SemaphoreType.DMA((3, RING)),
        ]
        + [pltpu.VMEM((SUB + 8, 128), F32)] * count,
        compiler_params=pltpu.CompilerParams(vmem_limit_bytes=8 * MIB),
        cost_estimate=pl.CostEstimate(flops=10**10, bytes_accessed=10**7, transcendentals=10**6),
        name="conv_states",
    )(place, halo, *map(in_hbm, (features, state_write, state_read)), conv_feat, conv_state, table, rows)


def scores_kernel(c_ref, wt_ref, sc_ref):
    state = c_ref.shape[1]
    keep = iota((SUB, SUB), 0) >= iota((SUB, SUB), 1)

    for b in range(c_ref.shape[0] // SUB):
        at = pl.ds(b * SUB, SUB)
        c = c_ref[at, :]
        sc_ref[at, 0:SUB] = jnp.where(keep, dot(c, wt_ref[:, at]), 0.0).astype(BF16)
        sc_ref[at, SUB : SUB + state] = c


def block_scores(c, wt):
    tokens, state = c.shape
    return pl.pallas_call(
        scores_kernel,
        in_specs=[VMEM, VMEM],
        out_specs=VMEM,
        out_shape=pltpu.VMEM((tokens, SUB + state), BF16),
        compiler_params=pltpu.CompilerParams(vmem_limit_bytes=8 * MIB),
        cost_estimate=pl.CostEstimate(flops=10**9, bytes_accessed=2 * 10**6, transcendentals=0),
        name="block_scores",
    )(c, wt)


def within_kernel(offset, heads, _, x_ref, sc_ref, wt_ref, table_ref, pair_ref, rows_ref, first_ref, out_ref, start):
    blocks = x_ref.shape[0] // SUB
    head_dim = rows_ref.shape[1] // heads
    start[...] = jnp.zeros_like(start)

    def block(b, _):
        at = pl.ds(pl.multiple_of(b * SUB, SUB), SUB)
        table = table_ref[at, :]
        pair = pair_ref[at, :]
        sc = sc_ref[at, :]
        wt = wt_ref[:, at]
        for n in range(x_ref.shape[1] // WIDE):
            cols = pl.ds(offset + n * WIDE, WIDE)
            here = pl.ds(n * WIDE, WIDE)
            tiles = [(offset + n * WIDE + lane) // 128 for lane in range(0, WIDE, 128)]
            x = x_ref[at, here]
            bx = (x * jnp.concatenate([per_head(table, 1, heads, head_dim, t) for t in tiles], axis=1)).astype(BF16)
            now = start[n]
            inner = dot(sc, jnp.concatenate([bx, now.astype(BF16)], axis=0))
            if n % 2:
                outer = jnp.concatenate([per_head(table, 0, heads, head_dim, t) for t in tiles], axis=1)
            else:
                outer = dot(pair, first_ref[:, cols])
            out_ref[at, here] = outer * inner + rows_ref[blocks + 1 : blocks + 2, cols] * x
            start[n] = rows_ref[pl.ds(b, 1), cols] * (now + dot(wt, bx))
        return 0

    lax.fori_loop(0, blocks, block, 0, unroll=UNROLL)


def within(offset, heads, after, x, sc, wt, table, pair, rows, first):
    tokens, part = x.shape
    state = wt.shape[0]
    return pl.pallas_call(
        functools.partial(within_kernel, offset, heads),
        in_specs=[ANY] + [VMEM] * 7,
        out_specs=VMEM,
        out_shape=pltpu.VMEM((tokens, part), F32),
        scratch_shapes=[pltpu.VMEM((part // WIDE, state, WIDE), F32)],
        compiler_params=pltpu.CompilerParams(vmem_limit_bytes=8 * MIB),
        cost_estimate=pl.CostEstimate(flops=2 * 10**9, bytes_accessed=16 * tokens * part, transcendentals=0),
        name="within",
    )(after, x, sc, wt, table, pair, rows, first)


def group_kernel(place_ref, msg_ref, r1_ref, r2_ref, r3_ref, total_ref, prefix_ref, decay_ref, held):
    place = place_ref[0]
    state = prefix_ref.shape[1]
    held[place] = msg_ref[0]
    for k, ref in enumerate((r1_ref, r2_ref, r3_ref)):
        held[lax.bitwise_xor(place, k + 1)] = ref[...]
    sofar = jnp.zeros(prefix_ref.shape[1:], F32)
    decays = jnp.ones((1, sofar.shape[1]), F32)
    for j in range(GROUP):
        tail = held[j, state:, :].astype(F32)
        decay = tail[0:1] + tail[1:2]
        prefix_ref[j] = sofar
        decay_ref[j : j + 1, :] = decays
        sofar = decay * sofar + held[j, 0:state, :].astype(F32)
        decays = decay * decays
    total_ref[0:state, :] = sofar.astype(BF16)
    wide = jnp.broadcast_to(decays, (16, decays.shape[1]))
    total_ref[state:, :] = split_pair(wide, iota(wide.shape, 0) == 1)


def group_prefix(place, msg, received):
    _, rows, quarter = msg.shape
    state = rows - 16
    return pl.pallas_call(
        group_kernel,
        in_specs=[SMEM] + [VMEM] * 4,
        out_specs=[VMEM] * 3,
        out_shape=[
            jax.ShapeDtypeStruct((rows, quarter), BF16),
            pltpu.VMEM((GROUP, state, quarter), F32),
            pltpu.VMEM((8, quarter), F32),
        ],
        scratch_shapes=[pltpu.VMEM((GROUP, rows, quarter), BF16)],
        compiler_params=pltpu.CompilerParams(vmem_limit_bytes=8 * MIB),
        name="group_prefix",
    )(place, msg, *received)


def spread_kernel(place_ref, prefix_ref, decay_ref, carried_ref, *out_refs):
    place = place_ref[0]
    state = prefix_ref.shape[1]
    carried = carried_ref[0:state, :].astype(F32) * place_ref[3].astype(F32)
    for k, ref in enumerate(out_refs):
        j = lax.bitwise_xor(place, k)
        ref[...] = (prefix_ref[j] + decay_ref[pl.ds(j, 1), :] * carried).astype(BF16)


def spread(place, prefix, decay, carried):
    _, state, quarter = prefix.shape
    return pl.pallas_call(
        spread_kernel,
        in_specs=[SMEM] + [VMEM] * 3,
        out_specs=[VMEM] * GROUP,
        out_shape=[jax.ShapeDtypeStruct((state, quarter), BF16)] * GROUP,
        compiler_params=pltpu.CompilerParams(vmem_limit_bytes=8 * MIB),
        name="spread",
    )(place, prefix, decay, carried)


def state_kernel(count, heads, place_ref, c_ref, table_ref, pair_ref, second_ref, s0, s1, s2, s3, *refs):
    m_refs, out_refs, (sq_ref, start) = refs[:count], refs[count : 2 * count], refs[2 * count :]
    place = place_ref[0]
    tokens = c_ref.shape[0]
    quarter = s0.shape[1]
    head_dim = quarter * GROUP // heads
    for k, ref in enumerate((s0, s1, s2, s3)):
        start[lax.bitwise_xor(place, k)] = ref[...]
    homes = [(m, o, n) for m, o in zip(m_refs, out_refs) for n in range(m.shape[1] // WIDE)]

    def block(b, _):
        at = pl.ds(pl.multiple_of(b * SUB, SUB), SUB)
        c = c_ref[at, :]
        table = table_ref[at, :]
        pair = pair_ref[at, :]
        squares = jnp.zeros((SUB, 128), F32)
        for chunk, (m_ref, out_ref, n) in enumerate(homes):
            q, off = divmod(chunk * WIDE, quarter)
            inner = dot(c, start[q, :, off : off + WIDE])
            if chunk % 8 in (0, 3, 6):
                factors = dot(pair, second_ref[:, pl.ds(chunk * WIDE, WIDE)])
            for lane in range(0, WIDE, 128):
                spot = pl.ds(n * WIDE + lane, 128)
                if chunk % 8 in (0, 3, 6):
                    factor = factors[:, lane : lane + 128]
                else:
                    factor = per_head(table, 3, heads, head_dim, (chunk * WIDE + lane) // 128)
                piece = m_ref[at, spot] + factor * inner[:, lane : lane + 128]
                out_ref[at, spot] = piece.astype(BF16)
                squares = squares + piece * piece
        sq_ref[pl.ds(b, 1), :] = jnp.sum(squares.T, axis=0, keepdims=True)
        return 0

    lax.fori_loop(0, tokens // SUB, block, 0, unroll=2)


def add_states(heads, place, ms, c, table, pair, second, pieces):
    tokens, state = c.shape
    quarter = pieces[0].shape[1]
    blocks = tokens // SUB
    return pl.pallas_call(
        functools.partial(state_kernel, len(ms), heads),
        in_specs=[SMEM] + [VMEM] * (4 + GROUP + len(ms)),
        out_specs=[VMEM] * (len(ms) + 1),
        out_shape=[pltpu.VMEM(m.shape, BF16) for m in ms] + [jax.ShapeDtypeStruct((blocks, SUB), F32)],
        scratch_shapes=[pltpu.VMEM((GROUP, state, quarter), BF16)],
        compiler_params=pltpu.CompilerParams(vmem_limit_bytes=8 * MIB),
        name="add_states",
    )(place, c, table, pair, second, *pieces, *ms)


def norm_kernel(size, count, gain_ref, *refs):
    m_refs, sq_refs, (out_ref, ring, sems) = refs[:count], refs[count:-3], refs[-3:]
    homes = [(m, n) for m in m_refs for n in range(m.shape[1] // 128)]
    blocks = out_ref.shape[0] // ROWS

    def copy(b):
        slot = lax.rem(b, RING)
        at = pl.ds(pl.multiple_of(b * ROWS, ROWS), ROWS)
        return pltpu.make_async_copy(ring.at[slot], out_ref.at[at, :], sems.at[slot])

    def block(b, _):
        slot = lax.rem(b, RING)

        @pl.when(b >= RING)
        def _():
            copy(b - RING).wait()

        for sub in range(ROWS // SUB):
            row = b * (ROWS // SUB) + sub
            total = sq_refs[0][pl.ds(row, 1), :]
            for ref in sq_refs[1:]:
                total = total + ref[pl.ds(row, 1), :]
            scale = lax.rsqrt(total * (1.0 / size) + EPSILON)
            scale = jnp.broadcast_to(scale, (SUB, SUB)).T
            at = pl.ds(pl.multiple_of(row * SUB, SUB), SUB)
            for tile, (m_ref, n) in enumerate(homes):
                cols = pl.ds(tile * 128, 128)
                value = m_ref[at, pl.ds(n * 128, 128)].astype(F32) * scale * gain_ref[:, cols]
                ring[slot, pl.ds(sub * SUB, SUB), cols] = value.astype(BF16)
        copy(b).start()
        return 0

    lax.fori_loop(0, blocks, block, 0)
    for b in range(max(0, blocks - RING), blocks):
        copy(jnp.int32(b)).wait()


def norm(size, ms, gain, squares):
    tokens = ms[0].shape[0]
    channels = gain.shape[0]
    return pl.pallas_call(
        functools.partial(norm_kernel, size, len(ms)),
        in_specs=[VMEM] * (1 + len(ms) + len(squares)),
        out_specs=ANY,
        out_shape=jax.ShapeDtypeStruct((tokens, channels), BF16),
        scratch_shapes=[pltpu.VMEM((RING, ROWS, channels), BF16), pltpu.SemaphoreType.DMA((RING,))],
        compiler_params=pltpu.CompilerParams(vmem_limit_bytes=8 * MIB),
        name="norm",
    )(gain.reshape(1, channels), *ms, *squares)


def later(value, steps):
    count = lax.axis_size("seq")
    return lax.ppermute(value, "seq", [(i, (i + steps) % count) for i in range(count)])


def partner(value, axis, mask):
    return lax.ppermute(value, axis, [(i, i ^ mask) for i in range(lax.axis_size(axis))])


def group_carry(total):
    groups = lax.axis_size("seq") // GROUP
    group = lax.axis_index("seq") // GROUP
    carried = later(total, GROUP)
    state = total.shape[0] - 16
    reach = 1
    while reach < groups - 1:
        mine = jnp.where(group >= 1, carried.astype(F32), 0.0)
        got = jnp.where(group >= reach, later(mine.astype(BF16), reach * GROUP).astype(F32), 0.0)
        decay = mine[state : state + 1] + mine[state + 1 : state + 2]
        got_decay = got[state : state + 1] + got[state + 1 : state + 2]
        values = mine[:state] + decay * got[:state]
        both = decay * got_decay
        high = both.astype(BF16)
        rest = (both - high.astype(F32)).astype(BF16)
        carried = jnp.concatenate(
            [values.astype(BF16), high, rest, jnp.zeros((14, both.shape[1]), BF16)], axis=0
        )
        reach *= 2
    return carried


def on_device(
    features, state_write, state_read, conv_feat, conv_state, log_decay, skip_weight, norm_gain
):
    tokens, channels = features.shape
    heads = log_decay.shape[1]
    index = lax.axis_index("seq").astype(jnp.int32)
    place = jnp.stack(
        [lax.rem(index, GROUP), jnp.minimum(index, 1), jnp.zeros_like(index), jnp.minimum(index // GROUP, 1)]
    )
    halo = later(tail_rows(features, state_write, state_read), 1)
    table, pair, rows, first, second = decay_prep(log_decay, skip_weight, channels)
    chunks = channels // WIDE
    cuts = [0, (3 * chunks) // 8 * WIDE, (5 * chunks) // 8 * WIDE, channels]
    parts = [cuts[n + 1] - cuts[n] for n in range(3)]
    *xs, wt, c, msg = conv_states(
        parts, place, halo, features, state_write, state_read, conv_feat, conv_state, table, rows, heads
    )
    received = [partner(msg[k], "seq", k) for k in range(1, GROUP)]
    sc = block_scores(c, wt)
    shared = (sc, wt, table, pair, rows, first)
    ms = [within(cuts[0], heads, place, xs[0], *shared)]
    total, prefix, decay = group_prefix(place, msg, received)
    carried = group_carry(total)
    ms.append(within(cuts[1], heads, total, xs[1], *shared))
    pieces = spread(place, prefix, decay, carried)
    starts = [pieces[0]] + [partner(pieces[k], "seq", k) for k in range(1, GROUP)]
    ms.append(within(cuts[2], heads, pieces[0], xs[2], *shared))
    *ms, squares = add_states(heads, place, ms, c, table, pair, second, starts)
    others = [partner(squares, "head", k) for k in range(1, lax.axis_size("head"))]
    size = channels * lax.axis_size("head")
    return norm(size, ms, norm_gain, [squares] + others)


def solution(mesh):
    placed = (
        P("seq", "head"),
        P("seq", None),
        P("seq", None),
        P(None, "head"),
        P(),
        P("seq", "head"),
        P("head"),
        P("head"),
    )
    return jax.shard_map(
        on_device, mesh=mesh, in_specs=placed, out_specs=P("seq", "head"), check_vma=False
    )
```

time: 111 us -> 73.6 us (0.66)
  Pallas kernels: 78.4 us -> 53.4 us
  local copies, waits for them, and re-layouts: 11.9 us -> 0.45 us
  starting transfers between devices: 18.4 us -> 13.2 us
  waiting for transfers between devices: 1.93 us -> 6.15 us
    pallas_call x6 -> x7, Pallas kernels: 74 us -> 48.3 us  [the longest x1 19 us: conv_states(): pl.pallas_call(functools.partial(conv_kernel, heads, count), in_specs=[SM...]
    unnamed x19 -> x11, local copies, waits for them, and re-layouts: 9.64 us -> 0.42 us
    ppermute x2, starting transfers between devices: 9.38 us -> 4.15 us  [later(): lax.ppermute(value, 'seq', [(i, (i + steps) % count) for i in range(count)])]
    ppermute x2, waiting for transfers between devices: 0.01 us -> 4.22 us  [later(): lax.ppermute(value, 'seq', [(i, (i + steps) % count) for i in range(count)])]
    slice x3 -> x0, local copies, waits for them, and re-layouts: 2.22 us -> none  [the longest x1 0.84 us: on_device(): features[-16:]]
  transfers between devices with their start and end apart: 11 -> 11, of which waited for: 2 -> 4; matrix products, arithmetic and copies ran while one was open for 1% -> 1% of each run, Pallas kernels for 29% -> 27%
where the time goes in v2:
time: 73.6 us; the launch traced here: 73.4 us
  Pallas kernels  53.4 us (73%)
  starting transfers between devices  13.2 us (18%)
  waiting for transfers between devices  6.15 us (8%)
    pallas_call x1, Pallas kernels, conv_states(): pl.pallas_call(functools.partial(conv_kernel, heads, count), in_specs=[SM...  19 us
    pallas_call x3, Pallas kernels, within(): pl.pallas_call(functools.partial(within_kernel, offset, heads), in_specs=...  15.9 us
    ppermute x9, starting transfers between devices, partner(): lax.ppermute(value, axis, [(i, i ^ mask) for i in range(lax.axis_size(axi...  9.03 us
    pallas_call x1, Pallas kernels, add_states(): pl.pallas_call(functools.partial(state_kernel, len(ms), heads), in_specs=...  7.81 us
    pallas_call x1, Pallas kernels, norm(): pl.pallas_call(functools.partial(norm_kernel, size, len(ms)), in_specs=[V...  4.6 us
    ppermute x2, waiting for transfers between devices, later(): lax.ppermute(value, 'seq', [(i, (i + steps) % count) for i in range(count)])  4.22 us
    ppermute x2, starting transfers between devices, later(): lax.ppermute(value, 'seq', [(i, (i + steps) % count) for i in range(count)])  4.15 us
    pallas_call x1, Pallas kernels, decay_prep(): pl.pallas_call(functools.partial(decay_kernel, heads), in_specs=[VMEM, VM...  3.33 us
  transfers between devices with their start and end apart: 11, of which 4 were waited for; matrix products, arithmetic and copies ran while one was open for 1% of the time, Pallas kernels for 27%

profile of v2, /device:TPU:0, one launch (start us, length us, event | category | flops | bytes accessed | tf_op | source)
XLA Modules:
  0.0 73.4 jit_solution(14228867453209810973)
XLA Ops:
  0.0 0.0 copy-start.4
  0.0 0.0 copy-start.3
  0.0 0.9 %tail_rows.1 = bf16[16,2304]{1,0:T(8,128)(2,1)S(1)} custom-call(bf16[2560,2048]{1,0:T(8,128)(2,1)} %feat_ref.3, bf16[2560,128]{1,0:T(8,128)(2,1)} %write_ref.3, bf16[2560,128]{1,0:T(8,128)(2,1)} %read_ref.3), custom_call_target="tpu_custom_call" | custom-call | tf_op jit(solution)/shard_map/tail_rows/pallas_call | solution.py:138
  0.9 0.0 copy-start.1
  0.9 0.0 copy-start.2
  0.9 3.0 %collective-permute-start = (bf16[16,2304]{1,0:T(8,128)(2,1)S(1)}, bf16[16,2304]{1,0:T(8,128)(2,1)S(1)}, u32[]{:S(2)}, u32[]{:S(2)}) collective-permute-start(bf16[16,2304]{1,0:T(8,128)(2,1)S(1)} %tail_rows.1), channel_id=1, source_target_pairs={{0,4},{4,8},{8,12},{12,16},{16,20},{20,24},{24,28},{28,0},{1,5},{5... | collective-permute-start | bytes 221192 | tf_op jit(solution)/shard_map/ppermute | solution.py:498
  4.0 0.0 copy-done.4
  4.0 0.4 copy.9.ld_ref
  4.4 0.1 pad_add_fusion.place_ref._
  4.4 0.0 copy-done.3
  4.4 3.3 %decay_prep.1 = (f32[2560,128]{1,0:T(8,128)S(1)}, bf16[2560,128]{1,0:T(8,128)(2,1)S(1)}, f32[24,2048]{1,0:T(8,128)S(1)}, bf16[128,2048]{1,0:T(8,128)(2,1)S(1)}, bf16[128,2048]{1,0:T(8,128)(2,1)S(1)}) custom-call(f32[2560,32]{1,0:T(8,128)S(1)} %copy.9.ld_ref, f32[1,32]{1,0:T(1,128)S(1)} %bitcast.12), custom_call_target="tpu_custom_call" | custom-call | flops 1000000000 | bytes 5000000 | tf_op jit(solution)/shard_map/decay_prep/pallas_call | solution.py:108
  7.8 1.6 %collective-permute-done.halo_ref = bf16[16,2304]{1,0:T(8,128)(2,1)S(1)} collective-permute-done((bf16[16,2304]{1,0:T(8,128)(2,1)S(1)}, bf16[16,2304]{1,0:T(8,128)(2,1)S(1)}, u32[]{:S(2)}, u32[]{:S(2)}) %collective-permute-start) | collective-permute-done | bytes 73760 | tf_op jit(solution)/shard_map/ppermute | solution.py:498
  9.3 0.0 copy-done.1
  9.3 0.0 copy-done.2
  9.3 19.0 %conv_states.1 = (f32[2560,768]{1,0:T(8,128)S(1)}, f32[2560,512]{1,0:T(8,128)S(1)}, f32[2560,768]{1,0:T(8,128)S(1)}, bf16[128,2560]{1,0:T(8,128)(2,1)S(1)}, bf16...) custom-call(s32[4]{0:T(128)S(1)} %pad_add_fusion.place_ref._, ...), custom_call_target="tpu_custom_call" | custom-call | flops 10000000000 | bytes 10000000 | tf_op jit(solution)/shard_map/conv_states/pallas_call | solution.py:242
  28.4 1.1 %collective-permute-start.3 = (bf16[144,512]{1,0:T(8,128)(2,1)S(1)}, bf16[144,512]{1,0:T(8,128)(2,1)S(1)}, u32[]{:S(2)}, u32[]{:S(2)}) collective-permute-start(bf16[144,512]{1,0:T(8,128)(2,1)S(1)} %get-tuple-element.49), channel_id=1, source_target_pairs={{0,12},{4,8},{8,4},{12,0},{16,28},{20,24},{24,20},{28,16},{1,13},{... | collective-permute-start | bytes 442376 | tf_op jit(solution)/shard_map/ppermute | solution.py:502
  29.5 0.4 collective-permute-start.2
  29.9 2.0 %collective-permute-start.1 = (bf16[144,512]{1,0:T(8,128)(2,1)S(1)}, bf16[144,512]{1,0:T(8,128)(2,1)S(1)}, u32[]{:S(2)}, u32[]{:S(2)}) collective-permute-start(bf16[144,512]{1,0:T(8,128)(2,1)S(1)} %get-tuple-element.51), channel_id=1, source_target_pairs={{0,4},{4,0},{8,12},{12,8},{16,20},{20,16},{24,28},{28,24},{1,5},{5... | collective-permute-start | bytes 442376 | tf_op jit(solution)/shard_map/ppermute | solution.py:502
  32.0 0.4 block_scores.1.sc_ref
  32.3 5.7 %within.3.refs_0_ = f32[2560,768]{1,0:T(8,128)S(1)} custom-call(s32[4]{0:T(128)S(1)} %pad_add_fusion.place_ref._, f32[2560,768]{1,0:T(8,128)S(1)} %get-tuple-element.40.x_ref, bf16[2560,256]{1,0:T(8,128)(2,1)S(1)} %block_scores.1.sc_ref, bf16[128,2560]{1,0:T(8,128)(2,1)S(1)} %get-tuple-element.41.wt_ref, f32[2560,128]{1,0:T(8,128)S(1)} %get-tuple-element.27.table_ref, ...), custom_call_target="tpu_custom_call" | custom-call | flops 2000000000 | bytes 31457280 | tf_op jit(solution)/shard_map/within/pallas_call | solution.py:323
  38.1 0.0 collective-permute-done.3.r3_ref
  38.1 0.0 collective-permute-done.2.r2_ref
  38.1 0.0 collective-permute-done.1.r1_ref
  38.1 0.8 %group_prefix.1 = (bf16[144,512]{1,0:T(8,128)(2,1)S(1)}, f32[4,128,512]{2,1,0:T(8,128)S(1)}, f32[8,512]{1,0:T(8,128)S(1)}) custom-call(s32[4]{0:T(128)S(1)} %pad_add_fusion.place_ref._, bf16[4,144,512]{2,1,0:T(8,128)(2,1)S(1)} %get-tuple-element.32.msg_ref, bf16[144,512]{1,0:T(8,128)(2,1)S(1)} %collective-permute-done.1.r1_ref, ...), custom_call_target="tpu_custom_call" | custom-call | tf_op jit(solution)/shard_map/group_prefix/pallas_call | solution.py:358
  38.9 1.1 %collective-permute-start.4 = (bf16[144,512]{1,0:T(8,128)(2,1)S(1)}, bf16[144,512]{1,0:T(8,128)(2,1)S(1)}, u32[]{:S(2)}, u32[]{:S(2)}) collective-permute-start(bf16[144,512]{1,0:T(8,128)(2,1)S(1)} %get-tuple-element.35._), channel_id=1, source_target_pairs={{0,16},{4,20},{8,24},{12,28},{16,0},{20,4},{24,8},{28,12},{1,17},{... | collective-permute-start | bytes 442376 | tf_op jit(solution)/shard_map/ppermute | solution.py:498
  40.0 4.5 %within.4.refs_1_ = f32[2560,512]{1,0:T(8,128)S(1)} custom-call(bf16[144,512]{1,0:T(8,128)(2,1)S(1)} %get-tuple-element.35._, f32[2560,512]{1,0:T(8,128)S(1)} %get-tuple-element.43.x_ref, bf16[2560,256]{1,0:T(8,128)(2,1)S(1)} %block_scores.1.sc_ref, bf16[128,2560]{1,0:T(8,128)(2,1)S(1)} %get-tuple-element.41.wt_ref, ...), custom_call_target="tpu_custom_call" | custom-call | flops 2000000000 | bytes 20971520 | tf_op jit(solution)/shard_map/within/pallas_call | solution.py:323
  44.6 2.7 %collective-permute-done.4.carried_ref = bf16[144,512]{1,0:T(8,128)(2,1)S(1)} collective-permute-done((bf16[144,512]{1,0:T(8,128)(2,1)S(1)}, bf16[144,512]{1,0:T(8,128)(2,1)S(1)}, u32[]{:S(2)}, u32[]{:S(2)}) %collective-permute-start.4) | collective-permute-done | bytes 147488 | tf_op jit(solution)/shard_map/ppermute | solution.py:498
  47.2 0.7 spread.1
  47.9 0.9 %collective-permute-start.5 = (bf16[128,512]{1,0:T(8,128)(2,1)S(1)}, bf16[128,512]{1,0:T(8,128)(2,1)S(1)}, u32[]{:S(2)}, u32[]{:S(2)}) collective-permute-start(bf16[128,512]{1,0:T(8,128)(2,1)S(1)} %get-tuple-element.37), channel_id=1, source_target_pairs={{0,4},{4,0},{8,12},{12,8},{16,20},{20,16},{24,28},{28,24},{1,5},{5... | collective-permute-start | bytes 393224 | tf_op jit(solution)/shard_map/ppermute | solution.py:502
  48.8 0.0 collective-permute-start.6
  48.8 2.6 %collective-permute-start.7 = (bf16[128,512]{1,0:T(8,128)(2,1)S(1)}, bf16[128,512]{1,0:T(8,128)(2,1)S(1)}, u32[]{:S(2)}, u32[]{:S(2)}) collective-permute-start(bf16[128,512]{1,0:T(8,128)(2,1)S(1)} %get-tuple-element.39), channel_id=1, source_target_pairs={{0,12},{4,8},{8,4},{12,0},{16,28},{20,24},{24,20},{28,16},{1,13},{... | collective-permute-start | bytes 393224 | tf_op jit(solution)/shard_map/ppermute | solution.py:502
  51.4 5.7 %within.5.refs_2_ = f32[2560,768]{1,0:T(8,128)S(1)} custom-call(bf16[128,512]{1,0:T(8,128)(2,1)S(1)} %get-tuple-element.36._.s0, f32[2560,768]{1,0:T(8,128)S(1)} %get-tuple-element.44.x_ref, bf16[2560,256]{1,0:T(8,128)(2,1)S(1)} %block_scores.1.sc_ref, bf16[128,2560]{1,0:T(8,128)(2,1)S(1)} %get-tuple-element.41.wt_ref, ...), custom_call_target="tpu_custom_call" | custom-call | flops 2000000000 | bytes 31457280 | tf_op jit(solution)/shard_map/within/pallas_call | solution.py:323
  57.1 0.0 collective-permute-done.5.s1
  57.2 0.0 collective-permute-done.6.s2
  57.2 0.0 collective-permute-done.7.s3
  57.2 0.0 copy-start
  57.2 7.8 %add_states.1 = (bf16[2560,768]{1,0:T(8,128)(2,1)S(1)}, bf16[2560,512]{1,0:T(8,128)(2,1)S(1)}, bf16[2560,768]{1,0:T(8,128)(2,1)S(1)}, f32[20,128]{1,0:T(8,128)S(1)}) custom-call(s32[4]{0:T(128)S(1)} %pad_add_fusion.place_ref._, bf16[2560,128]{1,0:T(8,128)(2,1)S(1)} %get-tuple-element.29.c_ref, f32[2560,128]{1,0:T(8,128)S(1)} %get-tuple-element.27.table_ref, ...), custom_call_target="tpu_custom_call" | custom-call | tf_op jit(solution)/shard_map/add_states/pallas_call | solution.py:434
  65.0 0.1 collective-permute-start.10
  65.1 1.4 %collective-permute-start.9 = (f32[20,128]{1,0:T(8,128)S(1)}, f32[20,128]{1,0:T(8,128)S(1)}, u32[]{:S(2)}, u32[]{:S(2)}) collective-permute-start(f32[20,128]{1,0:T(8,128)S(1)} %get-tuple-element.48.refs_3_), channel_id=1, source_target_pairs={{0,2},{1,3},{2,0},{3,1},{4,6},{5,7},{6,4},{7,5},{8,10},{9,11},{10,... | collective-permute-start | bytes 30728 | tf_op jit(solution)/shard_map/ppermute | solution.py:502
  66.5 0.4 collective-permute-start.8
  66.9 1.3 %collective-permute-done.10.refs_6_ = f32[20,128]{1,0:T(8,128)S(1)} collective-permute-done((f32[20,128]{1,0:T(8,128)S(1)}, f32[20,128]{1,0:T(8,128)S(1)}, u32[]{:S(2)}, u32[]{:S(2)}) %collective-permute-start.10) | collective-permute-done | bytes 10272 | tf_op jit(solution)/shard_map/ppermute | solution.py:502
  68.2 0.6 collective-permute-done.9.refs_5_
  68.8 0.0 collective-permute-done.8.refs_4_
  68.8 0.0 copy-done
  68.8 4.6 %norm.1 = bf16[2560,2048]{1,0:T(8,128)(2,1)} custom-call(f32[1,2048]{1,0:T(1,128)S(1)} %bitcast.11, bf16[2560,768]{1,0:T(8,128)(2,1)S(1)} %get-tuple-element.45.refs_0_, bf16[2560,512]{1,0:T(8,128)(2,1)S(1)} %get-tuple-element.46.refs_1_, bf16[2560,768]{1,0:T(8,128)(2,1)S(1)} %get-tuple-element.47.refs_2_, f32[20,128]{1,0:T(8,128)S(1)} %get-tuple-element.48.refs_3_, ...), custom_call_target="tpu_custom_call" | custom-call | tf_op jit(solution)/shard_map/norm/pallas_call | solution.py:485
  (1 shorter events, 0.0 us)
Async XLA Ops:
  0.0 4.0 %copy-start.4 = (f32[2560,32]{0,1:T(8,128)S(1)}, f32[2560,32]{0,1:T(8,128)}, u32[]{:S(2)}) copy-start(f32[2560,32]{0,1:T(8,128)} %param.13) | copy-start | bytes 983044
  0.0 4.4 %copy-start.3 = (f32[32]{0:T(128)S(1)}, f32[32]{0:T(128)}, u32[]{:S(2)}) copy-start(f32[32]{0:T(128)} %param.14) | copy-start | bytes 388
  0.9 8.4 %copy-start.1 = (f32[4,2048]{1,0:T(4,128)S(1)}, f32[4,2048]{1,0:T(4,128)}, u32[]{:S(2)}) copy-start(f32[4,2048]{1,0:T(4,128)} %taps_ref.1) | copy-start | bytes 98308
  0.9 8.4 %copy-start.2 = (f32[4,256]{1,0:T(4,128)S(1)}, f32[4,256]{1,0:T(4,128)}, u32[]{:S(2)}) copy-start(f32[4,256]{1,0:T(4,128)} %state_taps_ref.1) | copy-start | bytes 12292
  0.9 8.4 %collective-permute-start = (bf16[16,2304]{1,0:T(8,128)(2,1)S(1)}, bf16[16,2304]{1,0:T(8,128)(2,1)S(1)}, u32[]{:S(2)}, u32[]{:S(2)}) collective-permute-start(bf16[16,2304]{1,0:T(8,128)(2,1)S(1)} %tail_rows.1), channel_id=1, source_target_pairs={{0,4},{4,8},{8,12},{12,16},{16,20},{20,24},{24,28},{28,0},{1,5},{5... | collective-permute-start | bytes 221192 | tf_op jit(solution)/shard_map/ppermute | solution.py:498
  28.4 9.6 %collective-permute-start.3 = (bf16[144,512]{1,0:T(8,128)(2,1)S(1)}, bf16[144,512]{1,0:T(8,128)(2,1)S(1)}, u32[]{:S(2)}, u32[]{:S(2)}) collective-permute-start(bf16[144,512]{1,0:T(8,128)(2,1)S(1)} %get-tuple-element.49), channel_id=1, source_target_pairs={{0,12},{4,8},{8,4},{12,0},{16,28},{20,24},{24,20},{28,16},{1,13},{... | collective-permute-start | bytes 442376 | tf_op jit(solution)/shard_map/ppermute | solution.py:502
  29.5 8.6 %collective-permute-start.2 = (bf16[144,512]{1,0:T(8,128)(2,1)S(1)}, bf16[144,512]{1,0:T(8,128)(2,1)S(1)}, u32[]{:S(2)}, u32[]{:S(2)}) collective-permute-start(bf16[144,512]{1,0:T(8,128)(2,1)S(1)} %get-tuple-element.50), channel_id=1, source_target_pairs={{0,8},{4,12},{8,0},{12,4},{16,24},{20,28},{24,16},{28,20},{1,9},{5... | collective-permute-start | bytes 442376 | tf_op jit(solution)/shard_map/ppermute | solution.py:502
  29.9 8.1 %collective-permute-start.1 = (bf16[144,512]{1,0:T(8,128)(2,1)S(1)}, bf16[144,512]{1,0:T(8,128)(2,1)S(1)}, u32[]{:S(2)}, u32[]{:S(2)}) collective-permute-start(bf16[144,512]{1,0:T(8,128)(2,1)S(1)} %get-tuple-element.51), channel_id=1, source_target_pairs={{0,4},{4,0},{8,12},{12,8},{16,20},{20,16},{24,28},{28,24},{1,5},{5... | collective-permute-start | bytes 442376 | tf_op jit(solution)/shard_map/ppermute | solution.py:502
  38.9 8.3 %collective-permute-start.4 = (bf16[144,512]{1,0:T(8,128)(2,1)S(1)}, bf16[144,512]{1,0:T(8,128)(2,1)S(1)}, u32[]{:S(2)}, u32[]{:S(2)}) collective-permute-start(bf16[144,512]{1,0:T(8,128)(2,1)S(1)} %get-tuple-element.35._), channel_id=1, source_target_pairs={{0,16},{4,20},{8,24},{12,28},{16,0},{20,4},{24,8},{28,12},{1,17},{... | collective-permute-start | bytes 442376 | tf_op jit(solution)/shard_map/ppermute | solution.py:498
  47.9 9.2 %collective-permute-start.5 = (bf16[128,512]{1,0:T(8,128)(2,1)S(1)}, bf16[128,512]{1,0:T(8,128)(2,1)S(1)}, u32[]{:S(2)}, u32[]{:S(2)}) collective-permute-start(bf16[128,512]{1,0:T(8,128)(2,1)S(1)} %get-tuple-element.37), channel_id=1, source_target_pairs={{0,4},{4,0},{8,12},{12,8},{16,20},{20,16},{24,28},{28,24},{1,5},{5... | collective-permute-start | bytes 393224 | tf_op jit(solution)/shard_map/ppermute | solution.py:502
  48.8 8.3 %collective-permute-start.6 = (bf16[128,512]{1,0:T(8,128)(2,1)S(1)}, bf16[128,512]{1,0:T(8,128)(2,1)S(1)}, u32[]{:S(2)}, u32[]{:S(2)}) collective-permute-start(bf16[128,512]{1,0:T(8,128)(2,1)S(1)} %get-tuple-element.38), channel_id=1, source_target_pairs={{0,8},{4,12},{8,0},{12,4},{16,24},{20,28},{24,16},{28,20},{1,9},{5... | collective-permute-start | bytes 393224 | tf_op jit(solution)/shard_map/ppermute | solution.py:502
  48.8 8.3 %collective-permute-start.7 = (bf16[128,512]{1,0:T(8,128)(2,1)S(1)}, bf16[128,512]{1,0:T(8,128)(2,1)S(1)}, u32[]{:S(2)}, u32[]{:S(2)}) collective-permute-start(bf16[128,512]{1,0:T(8,128)(2,1)S(1)} %get-tuple-element.39), channel_id=1, source_target_pairs={{0,12},{4,8},{8,4},{12,0},{16,28},{20,24},{24,20},{28,16},{1,13},{... | collective-permute-start | bytes 393224 | tf_op jit(solution)/shard_map/ppermute | solution.py:502
  57.2 11.7 %copy-start = (f32[2048]{0:T(1024)S(1)}, f32[2048]{0:T(1024)}, u32[]{:S(2)}) copy-start(f32[2048]{0:T(1024)} %param.15) | copy-start | bytes 24580
  65.0 3.2 %collective-permute-start.10 = (f32[20,128]{1,0:T(8,128)S(1)}, f32[20,128]{1,0:T(8,128)S(1)}, u32[]{:S(2)}, u32[]{:S(2)}) collective-permute-start(f32[20,128]{1,0:T(8,128)S(1)} %get-tuple-element.48.refs_3_), channel_id=1, source_target_pairs={{0,3},{1,2},{2,1},{3,0},{4,7},{5,6},{6,5},{7,4},{8,11},{9,10},{10,... | collective-permute-start | bytes 30728 | tf_op jit(solution)/shard_map/ppermute | solution.py:502
  65.1 3.8 %collective-permute-start.9 = (f32[20,128]{1,0:T(8,128)S(1)}, f32[20,128]{1,0:T(8,128)S(1)}, u32[]{:S(2)}, u32[]{:S(2)}) collective-permute-start(f32[20,128]{1,0:T(8,128)S(1)} %get-tuple-element.48.refs_3_), channel_id=1, source_target_pairs={{0,2},{1,3},{2,0},{3,1},{4,6},{5,7},{6,4},{7,5},{8,10},{9,11},{10,... | collective-permute-start | bytes 30728 | tf_op jit(solution)/shard_map/ppermute | solution.py:502
  66.5 2.4 %collective-permute-start.8 = (f32[20,128]{1,0:T(8,128)S(1)}, f32[20,128]{1,0:T(8,128)S(1)}, u32[]{:S(2)}, u32[]{:S(2)}) collective-permute-start(f32[20,128]{1,0:T(8,128)S(1)} %get-tuple-element.48.refs_3_), channel_id=1, source_target_pairs={{0,1},{1,0},{2,3},{3,2},{4,5},{5,4},{6,7},{7,6},{8,9},{9,8},{10,11... | collective-permute-start | bytes 30728 | tf_op jit(solution)/shard_map/ppermute | solution.py:502

commit v3 on v2

--- a/solution.py
+++ b/solution.py
@@ -8,6 +8,7 @@
 from jax.sharding import PartitionSpec as P
 
 EPSILON = 1e-05
+SPREAD = 16
 SUB = 128
 WIDE = 256
 ROWS = 256
@@ -36,6 +37,19 @@
     return lax.broadcasted_iota(jnp.int32, shape, dim)
 
 
+def token_of(row):
+    return lax.shift_left(row & 7, SPREAD.bit_length() - 1) | lax.shift_right_logical(row, 3)
+
+
+def row_of(token):
+    return 8 * (token % SPREAD) + token // SPREAD
+
+
+def ordering():
+    shape = (SUB, SUB)
+    return token_of(iota(shape, 0)) == iota(shape, 1)
+
+
 def split_pair(value, low):
     high = value.astype(BF16).astype(F32)
     return jnp.where(low, value - high, high).astype(BF16)
@@ -53,19 +67,21 @@
     blocks = tokens // SUB
     dim_shift = (channels // heads).bit_length() - 1
     copies = 128 // heads
-    lower = (iota((SUB, SUB), 0) >= iota((SUB, SUB), 1)).astype(F32)
+    lower = (token_of(iota((SUB, SUB), 0)) >= iota((SUB, SUB), 1)).astype(F32)
+    both = jnp.concatenate([ordering().astype(F32), lower], axis=0)
     lane = iota((SUB, 128), 1)
     totals, refs = [], []
     for b in range(blocks):
         at = pl.ds(b * SUB, SUB)
-        decay = jnp.concatenate([ld_ref[at, :]] * copies, axis=1)
-        cumul = exact_dot(lower, decay)
+        sums = jnp.concatenate([exact_dot(both, ld_ref[at, :])] * copies, axis=1)
+        decay, cumul = sums[:SUB], sums[SUB:]
         y = 2.0 * decay
         series = -y * (1.0 + y * (1 / 2) * (1.0 + y * (1 / 3) * (1.0 + y * (1 / 4) * (1.0 + y * (1 / 5)))))
         cum_ref[at, :] = cumul
         sc_ref[at, :] = jnp.sqrt(jnp.where(y > -0.1, series, 1.0 - jnp.exp(y)))
         totals.append(cumul[SUB - 1 : SUB])
-        refs.append(cumul[SUB // 2 - 1 : SUB // 2])
+        middle = row_of(SUB // 2 - 1)
+        refs.append(cumul[middle : middle + 1])
     zero = jnp.zeros_like(totals[0])
     before = [zero]
     for b in range(blocks - 1):
@@ -150,11 +166,18 @@
     return pltpu.with_memory_space_constraint(value, pltpu.HBM)
 
 
-def conv_silu(ref, base, rows, taps):
-    total = None
-    for k in range(4):
-        term = ref[pl.ds(base + 5 + k, rows), :] * taps[k : k + 1]
-        total = term if total is None else total + term
+def conv_silu(now, buf, top, taps):
+    size = now.shape[0]
+    for k in range(3):
+        last = pltpu.roll(now[size - 24 + 8 * k : size - 16 + 8 * k], 1, 0)
+        edge = pl.ds(8 * k, 8)
+        before = buf[size + 24 + 8 * k : size + 32 + 8 * k, :]
+        buf[edge, :] = jnp.where(top, before, last)
+        buf[size + 24 + 8 * k : size + 32 + 8 * k, :] = last
+    buf[24 : size + 24, :] = now
+    total = now * taps[3:4]
+    for k in (1, 2, 3):
+        total = total + buf[24 - 8 * k : size + 24 - 8 * k, :] * taps[3 - k : 4 - k]
     return total + total * jnp.tanh(total)
 
 
@@ -162,8 +185,9 @@
     heads, count, place_ref, halo_ref, feat_ref, write_ref, read_ref, taps_ref, state_taps_ref, table_ref, rows_ref,
     *refs,
 ):
-    *x_refs, wt_ref, c_ref, msg_ref, carry, feat_ring, write_ring, read_ring, sems = refs[:-count]
-    bufs = refs[-count:]
+    parts = taps_ref.shape[1] // WIDE
+    held, bufs = refs[-parts:], refs[-parts - count : -parts]
+    *x_refs, wt_ref, c_ref, msg_ref, carry, wt_held, feat_ring, write_ring, read_ring, sems = refs[: -parts - count]
     tokens, channels = feat_ref.shape
     head_dim = channels // heads
     state = write_ref.shape[1]
@@ -172,60 +196,86 @@
     homes = [(ref, n) for ref in x_refs for n in range(ref.shape[1] // 128)]
     tiles = len(homes)
     rings = [(feat_ref, feat_ring), (write_ref, write_ring), (read_ref, read_ring)]
-    sources = [(feat_ring, n) for n in range(tiles)] + [(write_ring, 0), (read_ring, 0)]
-
-    def copies(b):
+
+    def copies(b, source=0):
         slot = lax.rem(b, RING)
-        at = pl.ds(pl.multiple_of(b * SUB, SUB), SUB)
+        at = pl.ds(pl.multiple_of(source * SUB, SUB), SUB)
         return [
             pltpu.make_async_copy(ref.at[at, :], ring.at[slot], sems.at[n, slot])
             for n, (ref, ring) in enumerate(rings)
         ]
 
+    def start(b, source):
+        for copy in copies(b, source):
+            copy.start()
+
     for b in range(RING):
-        for copy in copies(jnp.int32(b)):
-            copy.start()
-    halo = halo_ref[...].astype(F32)[8:16] * place_ref[1].astype(F32)
+        start(jnp.int32(b), b)
+    halo = halo_ref[...].astype(F32) * place_ref[1].astype(F32)
     for n, buf in enumerate(bufs):
-        buf[SUB : SUB + 8, :] = halo[:, n * 128 : (n + 1) * 128]
+        for k in range(3):
+            at = pl.ds(SUB + 24 + 8 * k, 8)
+            buf[at, :] = jnp.broadcast_to(halo[13 + k : 14 + k, n * 128 : (n + 1) * 128], (8, 128))
     carry[...] = jnp.zeros_like(carry)
-    zero = place_ref[2]
-
-    def block(b, _):
+    order = ordering().astype(F32).astype(BF16)
+    eye = (iota((SUB, SUB), 0) == iota((SUB, SUB), 1)).astype(F32).astype(BF16)
+    top = iota((8, 128), 0) == 0
+
+    for ref in (wt_held, *held):
+        ref[...] = jnp.zeros_like(ref)
+
+    def add_part(part, wt):
+        q, off = divmod(part * WIDE, quarter)
+        carry[q, :, pl.ds(off, WIDE)] += dot(wt, held[part][...])
+
+    def block(b, half, wt_before):
         here = pl.ds(pl.multiple_of(b * SUB, SUB), SUB)
+        inside = pl.ds(half * SUB, SUB)
         slot = lax.rem(b, RING)
         table = table_ref[here, :]
-        for copy in copies(b):
+
+        def conv(now, n, taps, tile):
+            return conv_silu(now, bufs[n], top, 0.5 * taps[:, pl.ds(tile * 128, 128)])
+
+        def states():
+            written = conv(dot(order, write_ring[slot]), tiles, state_taps_ref, 0).astype(BF16)
+            contract = (((1,), (1,)), ((), ()))
+            wt = lax.dot_general(eye, written, contract, preferred_element_type=F32).astype(BF16)
+            wt_ref[:, here] = wt
+            wt_held[:, inside] = wt
+            c_ref[here, :] = conv(dot(order, read_ring[slot]), tiles + 1, state_taps_ref, 1).astype(BF16)
+
+        for n, (x_ref, spot) in enumerate(homes):
+            part, lane = divmod(n * 128, WIDE)
+            if lane == 0:
+                wide = dot(order, feat_ring[slot, :, pl.ds(part * WIDE, WIDE)])
+                if half == 0:
+                    add_part(part, wt_before)
+                if part == parts // 2:
+                    states()
+            x = conv(wide[:, lane : lane + 128], n, taps_ref, n)
+            x_ref[here, pl.ds(spot * 128, 128)] = x
+            held[part][inside, pl.ds(lane, 128)] = (x * per_head(table, 2, heads, head_dim, n)).astype(BF16)
+
+    def pair(i, _):
+        first = 2 * i
+        for b in (first, first + 1):
+            for copy in copies(b):
+                copy.wait()
+        wt_before = wt_held[...]
+        block(first, 0, wt_before)
+        block(first + 1, 1, None)
+        for b in (first, first + 1):
+            start(b, jnp.minimum(b + RING, blocks - 1))
+        return 0
+
+    lax.fori_loop(0, blocks // 2, pair, 0)
+    for b in range(blocks, blocks + RING):
+        for copy in copies(jnp.int32(b)):
             copy.wait()
-
-        def conv(n, taps, tile):
-            buf = bufs[n]
-            source, spot = sources[n]
-            buf[0:8, :] = buf[SUB : SUB + 8, :]
-            buf[8:, :] = source[slot, :, pl.ds(spot * 128, 128)].astype(F32)
-            return conv_silu(buf, zero, SUB, 0.5 * taps[:, pl.ds(tile * 128, 128)])
-
-        wt = conv(tiles, state_taps_ref, 0).T.astype(BF16)
-        wt_ref[:, here] = wt
-        c_ref[here, :] = conv(tiles + 1, state_taps_ref, 1).astype(BF16)
-        decayed = []
-        for n, (x_ref, spot) in enumerate(homes):
-            x = conv(n, taps_ref, n)
-            x_ref[here, pl.ds(spot * 128, 128)] = x
-            decayed.append((x * per_head(table, 2, heads, head_dim, n)).astype(BF16))
-            if len(decayed) == WIDE // 128:
-                q, off = divmod((n + 1) * 128 - WIDE, quarter)
-                carry[q, :, pl.ds(off, WIDE)] += dot(wt, jnp.concatenate(decayed, axis=1))
-                decayed = []
-
-        @pl.when(b + RING < blocks)
-        def _():
-            for copy in copies(b + RING):
-                copy.start()
-
-        return 0
-
-    lax.fori_loop(0, blocks, block, 0)
+    wt = wt_held[...]
+    for part in range(parts):
+        add_part(part, wt)
     place = place_ref[0]
     for q in range(GROUP):
         slot = lax.bitwise_xor(place, q)
@@ -251,12 +301,14 @@
         ],
         scratch_shapes=[
             pltpu.VMEM((GROUP, state, quarter), F32),
+            pltpu.VMEM((state, 2 * SUB), BF16),
             pltpu.VMEM((RING, SUB, channels), BF16),
             pltpu.VMEM((RING, SUB, state), BF16),
             pltpu.VMEM((RING, SUB, state), BF16),
             pltpu.SemaphoreType.DMA((3, RING)),
         ]
-        + [pltpu.VMEM((SUB + 8, 128), F32)] * count,
+        + [pltpu.VMEM((SUB + 48, 128), F32)] * count
+        + [pltpu.VMEM((2 * SUB, WIDE), BF16)] * (channels // WIDE),
         compiler_params=pltpu.CompilerParams(vmem_limit_bytes=8 * MIB),
         cost_estimate=pl.CostEstimate(flops=10**10, bytes_accessed=10**7, transcendentals=10**6),
         name="conv_states",
@@ -265,7 +317,7 @@
 
 def scores_kernel(c_ref, wt_ref, sc_ref):
     state = c_ref.shape[1]
-    keep = iota((SUB, SUB), 0) >= iota((SUB, SUB), 1)
+    keep = token_of(iota((SUB, SUB), 0)) >= token_of(iota((SUB, SUB), 1))
 
     for b in range(c_ref.shape[0] // SUB):
         at = pl.ds(b * SUB, SUB)
@@ -424,7 +476,7 @@
         sq_ref[pl.ds(b, 1), :] = jnp.sum(squares.T, axis=0, keepdims=True)
         return 0
 
-    lax.fori_loop(0, tokens // SUB, block, 0, unroll=2)
+    lax.fori_loop(0, tokens // SUB, block, 0, unroll=UNROLL)
 
 
 def add_states(heads, place, ms, c, table, pair, second, pieces):
@@ -443,40 +495,36 @@
 
 
 def norm_kernel(size, count, gain_ref, *refs):
-    m_refs, sq_refs, (out_ref, ring, sems) = refs[:count], refs[count:-3], refs[-3:]
-    homes = [(m, n) for m in m_refs for n in range(m.shape[1] // 128)]
+    m_refs, sq_refs, (out_ref, ring, sems, scales) = refs[:count], refs[count:-4], refs[-4:]
+    homes = [(m, n) for m in m_refs for n in range(m.shape[1] // WIDE)]
     blocks = out_ref.shape[0] // ROWS
+    total = sq_refs[0][...]
+    for ref in sq_refs[1:]:
+        total = total + ref[...]
+    scales[...] = lax.rsqrt(exact_dot(total, ordering().astype(F32)) * (1.0 / size) + EPSILON)
+    back_rows = (iota((SUB, SUB), 0) == token_of(iota((SUB, SUB), 1))).astype(F32).astype(BF16)
 
     def copy(b):
-        slot = lax.rem(b, RING)
-        at = pl.ds(pl.multiple_of(b * ROWS, ROWS), ROWS)
-        return pltpu.make_async_copy(ring.at[slot], out_ref.at[at, :], sems.at[slot])
-
-    def block(b, _):
-        slot = lax.rem(b, RING)
-
-        @pl.when(b >= RING)
-        def _():
+        slot = b % RING
+        return pltpu.make_async_copy(ring.at[slot], out_ref.at[pl.ds(b * ROWS, ROWS), :], sems.at[slot])
+
+    for b in range(blocks):
+        slot = b % RING
+        if b >= RING:
             copy(b - RING).wait()
-
         for sub in range(ROWS // SUB):
             row = b * (ROWS // SUB) + sub
-            total = sq_refs[0][pl.ds(row, 1), :]
-            for ref in sq_refs[1:]:
-                total = total + ref[pl.ds(row, 1), :]
-            scale = lax.rsqrt(total * (1.0 / size) + EPSILON)
-            scale = jnp.broadcast_to(scale, (SUB, SUB)).T
-            at = pl.ds(pl.multiple_of(row * SUB, SUB), SUB)
-            for tile, (m_ref, n) in enumerate(homes):
-                cols = pl.ds(tile * 128, 128)
-                value = m_ref[at, pl.ds(n * 128, 128)].astype(F32) * scale * gain_ref[:, cols]
-                ring[slot, pl.ds(sub * SUB, SUB), cols] = value.astype(BF16)
+            scale = jnp.broadcast_to(scales[row : row + 1, :], (SUB, SUB)).T
+            at = pl.ds(row * SUB, SUB)
+            for chunk, (m_ref, n) in enumerate(homes):
+                rows = dot(back_rows, m_ref[at, pl.ds(n * WIDE, WIDE)])
+                for lane in range(0, WIDE, 128):
+                    cols = pl.ds(chunk * WIDE + lane, 128)
+                    value = rows[:, lane : lane + 128] * scale * gain_ref[:, cols]
+                    ring[slot, pl.ds(sub * SUB, SUB), cols] = value.astype(BF16)
         copy(b).start()
-        return 0
-
-    lax.fori_loop(0, blocks, block, 0)
     for b in range(max(0, blocks - RING), blocks):
-        copy(jnp.int32(b)).wait()
+        copy(b).wait()
 
 
 def norm(size, ms, gain, squares):
@@ -487,7 +535,11 @@
         in_specs=[VMEM] * (1 + len(ms) + len(squares)),
         out_specs=ANY,
         out_shape=jax.ShapeDtypeStruct((tokens, channels), BF16),
-        scratch_shapes=[pltpu.VMEM((RING, ROWS, channels), BF16), pltpu.SemaphoreType.DMA((RING,))],
+        scratch_shapes=[
+            pltpu.VMEM((RING, ROWS, channels), BF16),
+            pltpu.SemaphoreType.DMA((RING,)),
+            pltpu.VMEM(squares[0].shape, F32),
+        ],
         compiler_params=pltpu.CompilerParams(vmem_limit_bytes=8 * MIB),
         name="norm",
     )(gain.reshape(1, channels), *ms, *squares)
@@ -536,7 +588,7 @@
     halo = later(tail_rows(features, state_write, state_read), 1)
     table, pair, rows, first, second = decay_prep(log_decay, skip_weight, channels)
     chunks = channels // WIDE
-    cuts = [0, (3 * chunks) // 8 * WIDE, (5 * chunks) // 8 * WIDE, channels]
+    cuts = [0, (3 * chunks) // 8 * WIDE, (6 * chunks) // 8 * WIDE, channels]
     parts = [cuts[n + 1] - cuts[n] for n in range(3)]
     *xs, wt, c, msg = conv_states(
         parts, place, halo, features, state_write, state_read, conv_feat, conv_state, table, rows, heads

time: 73.6 us -> 72 us (0.978)
  waiting for transfers between devices: 6.15 us -> 3.86 us
    ppermute x2, waiting for transfers between devices: 4.22 us -> 1.61 us  [later(): lax.ppermute(value, 'seq', [(i, (i + steps) % count) for i in range(count)])]
  transfers between devices with their start and end apart: 11 -> 11, of which waited for: 4 -> 5; matrix products, arithmetic and copies ran while one was open for 1% -> 1% of each run, Pallas kernels for 27% -> 28%
where the time goes in v3:
time: 72 us; the launch traced here: 71.8 us
  Pallas kernels  53.3 us (74%)
  starting transfers between devices  13.8 us (19%)
  waiting for transfers between devices  3.86 us (5%)
    pallas_call x1, Pallas kernels, conv_states(): pl.pallas_call(functools.partial(conv_kernel, heads, count), in_specs=[SM...  18.5 us
    pallas_call x3, Pallas kernels, within(): pl.pallas_call(functools.partial(within_kernel, offset, heads), in_specs=...  16 us
    ppermute x9, starting transfers between devices, partner(): lax.ppermute(value, axis, [(i, i ^ mask) for i in range(lax.axis_size(axi...  9.03 us
    pallas_call x1, Pallas kernels, add_states(): pl.pallas_call(functools.partial(state_kernel, len(ms), heads), in_specs=...  7.09 us
    pallas_call x1, Pallas kernels, norm(): pl.pallas_call(functools.partial(norm_kernel, size, len(ms)), in_specs=[V...  5.12 us
    ppermute x2, starting transfers between devices, later(): lax.ppermute(value, 'seq', [(i, (i + steps) % count) for i in range(count)])  4.76 us
    pallas_call x1, Pallas kernels, decay_prep(): pl.pallas_call(functools.partial(decay_kernel, heads), in_specs=[VMEM, VM...  3.95 us
    ppermute x9, waiting for transfers between devices, partner(): lax.ppermute(value, axis, [(i, i ^ mask) for i in range(lax.axis_size(axi...  2.25 us
  transfers between devices with their start and end apart: 11, of which 5 were waited for; matrix products, arithmetic and copies ran while one was open for 1% of the time, Pallas kernels for 28%

profile of v3, /device:TPU:0, one launch (start us, length us, event | category | flops | bytes accessed | tf_op | source)
XLA Modules:
  0.0 71.8 jit_solution(3468319376821171334)
XLA Ops:
  0.0 0.0 copy-start.4
  0.0 0.0 copy-start.3
  0.0 0.9 %tail_rows.1 = bf16[16,2304]{1,0:T(8,128)(2,1)S(1)} custom-call(bf16[2560,2048]{1,0:T(8,128)(2,1)} %feat_ref.3, bf16[2560,128]{1,0:T(8,128)(2,1)} %write_ref.3, bf16[2560,128]{1,0:T(8,128)(2,1)} %read_ref.3), custom_call_target="tpu_custom_call" | custom-call | tf_op jit(solution)/shard_map/tail_rows/pallas_call | solution.py:154
  0.9 0.0 copy-start.1
  0.9 0.0 copy-start.2
  0.9 3.0 %collective-permute-start = (bf16[16,2304]{1,0:T(8,128)(2,1)S(1)}, bf16[16,2304]{1,0:T(8,128)(2,1)S(1)}, u32[]{:S(2)}, u32[]{:S(2)}) collective-permute-start(bf16[16,2304]{1,0:T(8,128)(2,1)S(1)} %tail_rows.1), channel_id=1, source_target_pairs={{0,4},{4,8},{8,12},{12,16},{16,20},{20,24},{24,28},{28,0},{1,5},{5... | collective-permute-start | bytes 221192 | tf_op jit(solution)/shard_map/ppermute | solution.py:550
  4.0 0.0 copy-done.4
  4.0 0.4 copy.9.ld_ref
  4.4 0.1 pad_add_fusion.place_ref._
  4.4 0.0 copy-done.3
  4.4 4.0 %decay_prep.1 = (f32[2560,128]{1,0:T(8,128)S(1)}, bf16[2560,128]{1,0:T(8,128)(2,1)S(1)}, f32[24,2048]{1,0:T(8,128)S(1)}, bf16[128,2048]{1,0:T(8,128)(2,1)S(1)}, bf16[128,2048]{1,0:T(8,128)(2,1)S(1)}) custom-call(f32[2560,32]{1,0:T(8,128)S(1)} %copy.9.ld_ref, f32[1,32]{1,0:T(1,128)S(1)} %bitcast.12), custom_call_target="tpu_custom_call" | custom-call | flops 1000000000 | bytes 5000000 | tf_op jit(solution)/shard_map/decay_prep/pallas_call | solution.py:124
  8.4 0.9 %collective-permute-done.halo_ref = bf16[16,2304]{1,0:T(8,128)(2,1)S(1)} collective-permute-done((bf16[16,2304]{1,0:T(8,128)(2,1)S(1)}, bf16[16,2304]{1,0:T(8,128)(2,1)S(1)}, u32[]{:S(2)}, u32[]{:S(2)}) %collective-permute-start) | collective-permute-done | bytes 73760 | tf_op jit(solution)/shard_map/ppermute | solution.py:550
  9.3 0.0 copy-done.1
  9.3 0.0 copy-done.2
  9.3 18.5 %conv_states.1 = (f32[2560,768]{1,0:T(8,128)S(1)}, f32[2560,768]{1,0:T(8,128)S(1)}, f32[2560,512]{1,0:T(8,128)S(1)}, bf16[128,2560]{1,0:T(8,128)(2,1)S(1)}, bf16...) custom-call(s32[4]{0:T(128)S(1)} %pad_add_fusion.place_ref._, ...), custom_call_target="tpu_custom_call" | custom-call | flops 10000000000 | bytes 10000000 | tf_op jit(solution)/shard_map/conv_states/pallas_call | solution.py:292
  27.9 1.7 %collective-permute-start.3 = (bf16[144,512]{1,0:T(8,128)(2,1)S(1)}, bf16[144,512]{1,0:T(8,128)(2,1)S(1)}, u32[]{:S(2)}, u32[]{:S(2)}) collective-permute-start(bf16[144,512]{1,0:T(8,128)(2,1)S(1)} %get-tuple-element.49), channel_id=1, source_target_pairs={{0,12},{4,8},{8,4},{12,0},{16,28},{20,24},{24,20},{28,16},{1,13},{... | collective-permute-start | bytes 442376 | tf_op jit(solution)/shard_map/ppermute | solution.py:554
  29.5 0.4 collective-permute-start.2
  30.0 1.4 %collective-permute-start.1 = (bf16[144,512]{1,0:T(8,128)(2,1)S(1)}, bf16[144,512]{1,0:T(8,128)(2,1)S(1)}, u32[]{:S(2)}, u32[]{:S(2)}) collective-permute-start(bf16[144,512]{1,0:T(8,128)(2,1)S(1)} %get-tuple-element.51), channel_id=1, source_target_pairs={{0,4},{4,0},{8,12},{12,8},{16,20},{20,16},{24,28},{28,24},{1,5},{5... | collective-permute-start | bytes 442376 | tf_op jit(solution)/shard_map/ppermute | solution.py:554
  31.4 0.4 block_scores.1.sc_ref
  31.8 5.7 %within.3.refs_0_ = f32[2560,768]{1,0:T(8,128)S(1)} custom-call(s32[4]{0:T(128)S(1)} %pad_add_fusion.place_ref._, f32[2560,768]{1,0:T(8,128)S(1)} %get-tuple-element.40.x_ref, bf16[2560,256]{1,0:T(8,128)(2,1)S(1)} %block_scores.1.sc_ref, bf16[128,2560]{1,0:T(8,128)(2,1)S(1)} %get-tuple-element.41.wt_ref, f32[2560,128]{1,0:T(8,128)S(1)} %get-tuple-element.27.table_ref, ...), custom_call_target="tpu_custom_call" | custom-call | flops 2000000000 | bytes 31457280 | tf_op jit(solution)/shard_map/within/pallas_call | solution.py:375
  37.5 0.0 collective-permute-done.3.r3_ref
  37.5 0.0 collective-permute-done.2.r2_ref
  37.5 0.0 collective-permute-done.1.r1_ref
  37.5 0.8 %group_prefix.1 = (bf16[144,512]{1,0:T(8,128)(2,1)S(1)}, f32[4,128,512]{2,1,0:T(8,128)S(1)}, f32[8,512]{1,0:T(8,128)S(1)}) custom-call(s32[4]{0:T(128)S(1)} %pad_add_fusion.place_ref._, bf16[4,144,512]{2,1,0:T(8,128)(2,1)S(1)} %get-tuple-element.32.msg_ref, bf16[144,512]{1,0:T(8,128)(2,1)S(1)} %collective-permute-done.1.r1_ref, ...), custom_call_target="tpu_custom_call" | custom-call | tf_op jit(solution)/shard_map/group_prefix/pallas_call | solution.py:410
  38.3 1.7 %collective-permute-start.4 = (bf16[144,512]{1,0:T(8,128)(2,1)S(1)}, bf16[144,512]{1,0:T(8,128)(2,1)S(1)}, u32[]{:S(2)}, u32[]{:S(2)}) collective-permute-start(bf16[144,512]{1,0:T(8,128)(2,1)S(1)} %get-tuple-element.35._), channel_id=1, source_target_pairs={{0,16},{4,20},{8,24},{12,28},{16,0},{20,4},{24,8},{28,12},{1,17},{... | collective-permute-start | bytes 442376 | tf_op jit(solution)/shard_map/ppermute | solution.py:550
  40.1 5.7 %within.4.refs_1_ = f32[2560,768]{1,0:T(8,128)S(1)} custom-call(bf16[144,512]{1,0:T(8,128)(2,1)S(1)} %get-tuple-element.35._, f32[2560,768]{1,0:T(8,128)S(1)} %get-tuple-element.43.x_ref, bf16[2560,256]{1,0:T(8,128)(2,1)S(1)} %block_scores.1.sc_ref, bf16[128,2560]{1,0:T(8,128)(2,1)S(1)} %get-tuple-element.41.wt_ref, ...), custom_call_target="tpu_custom_call" | custom-call | flops 2000000000 | bytes 31457280 | tf_op jit(solution)/shard_map/within/pallas_call | solution.py:375
  45.8 0.7 collective-permute-done.4.carried_ref
  46.4 0.6 spread.1
  47.1 1.8 %collective-permute-start.5 = (bf16[128,512]{1,0:T(8,128)(2,1)S(1)}, bf16[128,512]{1,0:T(8,128)(2,1)S(1)}, u32[]{:S(2)}, u32[]{:S(2)}) collective-permute-start(bf16[128,512]{1,0:T(8,128)(2,1)S(1)} %get-tuple-element.37), channel_id=1, source_target_pairs={{0,4},{4,0},{8,12},{12,8},{16,20},{20,16},{24,28},{28,24},{1,5},{5... | collective-permute-start | bytes 393224 | tf_op jit(solution)/shard_map/ppermute | solution.py:554
  48.9 0.0 collective-permute-start.6
  48.9 1.7 %collective-permute-start.7 = (bf16[128,512]{1,0:T(8,128)(2,1)S(1)}, bf16[128,512]{1,0:T(8,128)(2,1)S(1)}, u32[]{:S(2)}, u32[]{:S(2)}) collective-permute-start(bf16[128,512]{1,0:T(8,128)(2,1)S(1)} %get-tuple-element.39), channel_id=1, source_target_pairs={{0,12},{4,8},{8,4},{12,0},{16,28},{20,24},{24,20},{28,16},{1,13},{... | collective-permute-start | bytes 393224 | tf_op jit(solution)/shard_map/ppermute | solution.py:554
  50.6 4.6 %within.5.refs_2_ = f32[2560,512]{1,0:T(8,128)S(1)} custom-call(bf16[128,512]{1,0:T(8,128)(2,1)S(1)} %get-tuple-element.36._.s0, f32[2560,512]{1,0:T(8,128)S(1)} %get-tuple-element.44.x_ref, bf16[2560,256]{1,0:T(8,128)(2,1)S(1)} %block_scores.1.sc_ref, bf16[128,2560]{1,0:T(8,128)(2,1)S(1)} %get-tuple-element.41.wt_ref, ...), custom_call_target="tpu_custom_call" | custom-call | flops 2000000000 | bytes 20971520 | tf_op jit(solution)/shard_map/within/pallas_call | solution.py:375
  55.2 0.0 collective-permute-done.5.s1
  55.2 0.0 collective-permute-done.6.s2
  55.2 0.3 collective-permute-done.7.s3
  55.6 0.0 copy-start
  55.6 7.1 %add_states.1 = (bf16[2560,768]{1,0:T(8,128)(2,1)S(1)}, bf16[2560,768]{1,0:T(8,128)(2,1)S(1)}, bf16[2560,512]{1,0:T(8,128)(2,1)S(1)}, f32[20,128]{1,0:T(8,128)S(1)}) custom-call(s32[4]{0:T(128)S(1)} %pad_add_fusion.place_ref._, bf16[2560,128]{1,0:T(8,128)(2,1)S(1)} %get-tuple-element.29.c_ref, f32[2560,128]{1,0:T(8,128)S(1)} %get-tuple-element.27.table_ref, ...), custom_call_target="tpu_custom_call" | custom-call | tf_op jit(solution)/shard_map/add_states/pallas_call | solution.py:486
  62.7 0.1 collective-permute-start.10
  62.7 1.5 %collective-permute-start.9 = (f32[20,128]{1,0:T(8,128)S(1)}, f32[20,128]{1,0:T(8,128)S(1)}, u32[]{:S(2)}, u32[]{:S(2)}) collective-permute-start(f32[20,128]{1,0:T(8,128)S(1)} %get-tuple-element.48.refs_3_), channel_id=1, source_target_pairs={{0,2},{1,3},{2,0},{3,1},{4,6},{5,7},{6,4},{7,5},{8,10},{9,11},{10,... | collective-permute-start | bytes 30728 | tf_op jit(solution)/shard_map/ppermute | solution.py:554
  64.2 0.4 collective-permute-start.8
  64.6 1.4 %collective-permute-done.10.refs_6_ = f32[20,128]{1,0:T(8,128)S(1)} collective-permute-done((f32[20,128]{1,0:T(8,128)S(1)}, f32[20,128]{1,0:T(8,128)S(1)}, u32[]{:S(2)}, u32[]{:S(2)}) %collective-permute-start.10) | collective-permute-done | bytes 10272 | tf_op jit(solution)/shard_map/ppermute | solution.py:554
  65.9 0.6 collective-permute-done.9.refs_5_
  66.5 0.0 collective-permute-done.8.refs_4_
  66.5 0.0 copy-done
  66.5 5.1 %norm.1 = bf16[2560,2048]{1,0:T(8,128)(2,1)} custom-call(f32[1,2048]{1,0:T(1,128)S(1)} %bitcast.11, bf16[2560,768]{1,0:T(8,128)(2,1)S(1)} %get-tuple-element.45.refs_0_, bf16[2560,768]{1,0:T(8,128)(2,1)S(1)} %get-tuple-element.46.refs_1_, bf16[2560,512]{1,0:T(8,128)(2,1)S(1)} %get-tuple-element.47.refs_2_, f32[20,128]{1,0:T(8,128)S(1)} %get-tuple-element.48.refs_3_, ...), custom_call_target="tpu_custom_call" | custom-call | tf_op jit(solution)/shard_map/norm/pallas_call | solution.py:533
  (1 shorter events, 0.0 us)
Async XLA Ops:
  0.0 4.0 %copy-start.4 = (f32[2560,32]{0,1:T(8,128)S(1)}, f32[2560,32]{0,1:T(8,128)}, u32[]{:S(2)}) copy-start(f32[2560,32]{0,1:T(8,128)} %param.13) | copy-start | bytes 983044
  0.0 4.4 %copy-start.3 = (f32[32]{0:T(128)S(1)}, f32[32]{0:T(128)}, u32[]{:S(2)}) copy-start(f32[32]{0:T(128)} %param.14) | copy-start | bytes 388
  0.9 8.4 %copy-start.1 = (f32[4,2048]{1,0:T(4,128)S(1)}, f32[4,2048]{1,0:T(4,128)}, u32[]{:S(2)}) copy-start(f32[4,2048]{1,0:T(4,128)} %taps_ref.1) | copy-start | bytes 98308
  0.9 8.4 %copy-start.2 = (f32[4,256]{1,0:T(4,128)S(1)}, f32[4,256]{1,0:T(4,128)}, u32[]{:S(2)}) copy-start(f32[4,256]{1,0:T(4,128)} %state_taps_ref.1) | copy-start | bytes 12292
  0.9 8.4 %collective-permute-start = (bf16[16,2304]{1,0:T(8,128)(2,1)S(1)}, bf16[16,2304]{1,0:T(8,128)(2,1)S(1)}, u32[]{:S(2)}, u32[]{:S(2)}) collective-permute-start(bf16[16,2304]{1,0:T(8,128)(2,1)S(1)} %tail_rows.1), channel_id=1, source_target_pairs={{0,4},{4,8},{8,12},{12,16},{16,20},{20,24},{24,28},{28,0},{1,5},{5... | collective-permute-start | bytes 221192 | tf_op jit(solution)/shard_map/ppermute | solution.py:550
  27.9 9.6 %collective-permute-start.3 = (bf16[144,512]{1,0:T(8,128)(2,1)S(1)}, bf16[144,512]{1,0:T(8,128)(2,1)S(1)}, u32[]{:S(2)}, u32[]{:S(2)}) collective-permute-start(bf16[144,512]{1,0:T(8,128)(2,1)S(1)} %get-tuple-element.49), channel_id=1, source_target_pairs={{0,12},{4,8},{8,4},{12,0},{16,28},{20,24},{24,20},{28,16},{1,13},{... | collective-permute-start | bytes 442376 | tf_op jit(solution)/shard_map/ppermute | solution.py:554
  29.5 8.0 %collective-permute-start.2 = (bf16[144,512]{1,0:T(8,128)(2,1)S(1)}, bf16[144,512]{1,0:T(8,128)(2,1)S(1)}, u32[]{:S(2)}, u32[]{:S(2)}) collective-permute-start(bf16[144,512]{1,0:T(8,128)(2,1)S(1)} %get-tuple-element.50), channel_id=1, source_target_pairs={{0,8},{4,12},{8,0},{12,4},{16,24},{20,28},{24,16},{28,20},{1,9},{5... | collective-permute-start | bytes 442376 | tf_op jit(solution)/shard_map/ppermute | solution.py:554
  30.0 7.5 %collective-permute-start.1 = (bf16[144,512]{1,0:T(8,128)(2,1)S(1)}, bf16[144,512]{1,0:T(8,128)(2,1)S(1)}, u32[]{:S(2)}, u32[]{:S(2)}) collective-permute-start(bf16[144,512]{1,0:T(8,128)(2,1)S(1)} %get-tuple-element.51), channel_id=1, source_target_pairs={{0,4},{4,0},{8,12},{12,8},{16,20},{20,16},{24,28},{28,24},{1,5},{5... | collective-permute-start | bytes 442376 | tf_op jit(solution)/shard_map/ppermute | solution.py:554
  38.3 8.1 %collective-permute-start.4 = (bf16[144,512]{1,0:T(8,128)(2,1)S(1)}, bf16[144,512]{1,0:T(8,128)(2,1)S(1)}, u32[]{:S(2)}, u32[]{:S(2)}) collective-permute-start(bf16[144,512]{1,0:T(8,128)(2,1)S(1)} %get-tuple-element.35._), channel_id=1, source_target_pairs={{0,16},{4,20},{8,24},{12,28},{16,0},{20,4},{24,8},{28,12},{1,17},{... | collective-permute-start | bytes 442376 | tf_op jit(solution)/shard_map/ppermute | solution.py:550
  47.1 8.1 %collective-permute-start.5 = (bf16[128,512]{1,0:T(8,128)(2,1)S(1)}, bf16[128,512]{1,0:T(8,128)(2,1)S(1)}, u32[]{:S(2)}, u32[]{:S(2)}) collective-permute-start(bf16[128,512]{1,0:T(8,128)(2,1)S(1)} %get-tuple-element.37), channel_id=1, source_target_pairs={{0,4},{4,0},{8,12},{12,8},{16,20},{20,16},{24,28},{28,24},{1,5},{5... | collective-permute-start | bytes 393224 | tf_op jit(solution)/shard_map/ppermute | solution.py:554
  48.9 6.3 %collective-permute-start.6 = (bf16[128,512]{1,0:T(8,128)(2,1)S(1)}, bf16[128,512]{1,0:T(8,128)(2,1)S(1)}, u32[]{:S(2)}, u32[]{:S(2)}) collective-permute-start(bf16[128,512]{1,0:T(8,128)(2,1)S(1)} %get-tuple-element.38), channel_id=1, source_target_pairs={{0,8},{4,12},{8,0},{12,4},{16,24},{20,28},{24,16},{28,20},{1,9},{5... | collective-permute-start | bytes 393224 | tf_op jit(solution)/shard_map/ppermute | solution.py:554
  48.9 6.6 %collective-permute-start.7 = (bf16[128,512]{1,0:T(8,128)(2,1)S(1)}, bf16[128,512]{1,0:T(8,128)(2,1)S(1)}, u32[]{:S(2)}, u32[]{:S(2)}) collective-permute-start(bf16[128,512]{1,0:T(8,128)(2,1)S(1)} %get-tuple-element.39), channel_id=1, source_target_pairs={{0,12},{4,8},{8,4},{12,0},{16,28},{20,24},{24,20},{28,16},{1,13},{... | collective-permute-start | bytes 393224 | tf_op jit(solution)/shard_map/ppermute | solution.py:554
  55.6 10.9 %copy-start = (f32[2048]{0:T(1024)S(1)}, f32[2048]{0:T(1024)}, u32[]{:S(2)}) copy-start(f32[2048]{0:T(1024)} %param.15) | copy-start | bytes 24580
  62.7 3.3 %collective-permute-start.10 = (f32[20,128]{1,0:T(8,128)S(1)}, f32[20,128]{1,0:T(8,128)S(1)}, u32[]{:S(2)}, u32[]{:S(2)}) collective-permute-start(f32[20,128]{1,0:T(8,128)S(1)} %get-tuple-element.48.refs_3_), channel_id=1, source_target_pairs={{0,3},{1,2},{2,1},{3,0},{4,7},{5,6},{6,5},{7,4},{8,11},{9,10},{10,... | collective-permute-start | bytes 30728 | tf_op jit(solution)/shard_map/ppermute | solution.py:554
  62.7 3.8 %collective-permute-start.9 = (f32[20,128]{1,0:T(8,128)S(1)}, f32[20,128]{1,0:T(8,128)S(1)}, u32[]{:S(2)}, u32[]{:S(2)}) collective-permute-start(f32[20,128]{1,0:T(8,128)S(1)} %get-tuple-element.48.refs_3_), channel_id=1, source_target_pairs={{0,2},{1,3},{2,0},{3,1},{4,6},{5,7},{6,4},{7,5},{8,10},{9,11},{10,... | collective-permute-start | bytes 30728 | tf_op jit(solution)/shard_map/ppermute | solution.py:554
  64.2 2.3 %collective-permute-start.8 = (f32[20,128]{1,0:T(8,128)S(1)}, f32[20,128]{1,0:T(8,128)S(1)}, u32[]{:S(2)}, u32[]{:S(2)}) collective-permute-start(f32[20,128]{1,0:T(8,128)S(1)} %get-tuple-element.48.refs_3_), channel_id=1, source_target_pairs={{0,1},{1,0},{2,3},{3,2},{4,5},{5,4},{6,7},{7,6},{8,9},{9,8},{10,11... | collective-permute-start | bytes 30728 | tf_op jit(solution)/shard_map/ppermute | solution.py:554

commit v4 on v3

--- a/solution.py
+++ b/solution.py
@@ -11,10 +11,11 @@
 SPREAD = 16
 SUB = 128
 WIDE = 256
-ROWS = 256
+ROWS = 512
 RING = 4
 GROUP = 4
 UNROLL = 4
+MXU_CHUNKS = (1,3,5,7)
 F32 = jnp.float32
 BF16 = jnp.bfloat16
 HIGHEST = lax.Precision.HIGHEST
@@ -209,7 +210,7 @@
         for copy in copies(b, source):
             copy.start()
 
-    for b in range(RING):
+    for b in range(2):
         start(jnp.int32(b), b)
     halo = halo_ref[...].astype(F32) * place_ref[1].astype(F32)
     for n, buf in enumerate(bufs):
@@ -262,15 +263,15 @@
         for b in (first, first + 1):
             for copy in copies(b):
                 copy.wait()
+        for b in (first + 2, first + 3):
+            start(b, jnp.minimum(b, blocks - 1))
         wt_before = wt_held[...]
         block(first, 0, wt_before)
         block(first + 1, 1, None)
-        for b in (first, first + 1):
-            start(b, jnp.minimum(b + RING, blocks - 1))
         return 0
 
     lax.fori_loop(0, blocks // 2, pair, 0)
-    for b in range(blocks, blocks + RING):
+    for b in range(blocks, blocks + 2):
         for copy in copies(jnp.int32(b)):
             copy.wait()
     wt = wt_held[...]
@@ -462,11 +463,11 @@
         for chunk, (m_ref, out_ref, n) in enumerate(homes):
             q, off = divmod(chunk * WIDE, quarter)
             inner = dot(c, start[q, :, off : off + WIDE])
-            if chunk % 8 in (0, 3, 6):
+            if chunk % 8 in MXU_CHUNKS:
                 factors = dot(pair, second_ref[:, pl.ds(chunk * WIDE, WIDE)])
             for lane in range(0, WIDE, 128):
                 spot = pl.ds(n * WIDE + lane, 128)
-                if chunk % 8 in (0, 3, 6):
+                if chunk % 8 in MXU_CHUNKS:
                     factor = factors[:, lane : lane + 128]
                 else:
                     factor = per_head(table, 3, heads, head_dim, (chunk * WIDE + lane) // 128)
@@ -476,7 +477,7 @@
         sq_ref[pl.ds(b, 1), :] = jnp.sum(squares.T, axis=0, keepdims=True)
         return 0
 
-    lax.fori_loop(0, tokens // SUB, block, 0, unroll=UNROLL)
+    lax.fori_loop(0, tokens // SUB, block, 0, unroll=5)
 
 
 def add_states(heads, place, ms, c, table, pair, second, pieces):
@@ -540,7 +541,7 @@
             pltpu.SemaphoreType.DMA((RING,)),
             pltpu.VMEM(squares[0].shape, F32),
         ],
-        compiler_params=pltpu.CompilerParams(vmem_limit_bytes=8 * MIB),
+        compiler_params=pltpu.CompilerParams(vmem_limit_bytes=12 * MIB),
         name="norm",
     )(gain.reshape(1, channels), *ms, *squares)
 

time: 72 us -> 70.6 us (0.981)
  Pallas kernels: 53.3 us -> 52 us
  transfers between devices with their start and end apart: 11 -> 11, of which waited for: 5 -> 5; matrix products, arithmetic and copies ran while one was open for 1% -> 1% of each run, Pallas kernels for 28% -> 29%
where the time goes in v4:
time: 70.6 us; the launch traced here: 70.4 us
  Pallas kernels  52 us (74%)
  starting transfers between devices  13.8 us (20%)
  waiting for transfers between devices  3.8 us (5%)
    pallas_call x1, Pallas kernels, conv_states(): pl.pallas_call(functools.partial(conv_kernel, heads, count), in_specs=[SM...  17.8 us
    pallas_call x3, Pallas kernels, within(): pl.pallas_call(functools.partial(within_kernel, offset, heads), in_specs=...  16 us
    ppermute x9, starting transfers between devices, partner(): lax.ppermute(value, axis, [(i, i ^ mask) for i in range(lax.axis_size(axi...  9.03 us
    pallas_call x1, Pallas kernels, add_states(): pl.pallas_call(functools.partial(state_kernel, len(ms), heads), in_specs=...  6.64 us
    pallas_call x1, Pallas kernels, norm(): pl.pallas_call(functools.partial(norm_kernel, size, len(ms)), in_specs=[V...  4.91 us
    ppermute x2, starting transfers between devices, later(): lax.ppermute(value, 'seq', [(i, (i + steps) % count) for i in range(count)])  4.79 us
    pallas_call x1, Pallas kernels, decay_prep(): pl.pallas_call(functools.partial(decay_kernel, heads), in_specs=[VMEM, VM...  3.95 us
    ppermute x9, waiting for transfers between devices, partner(): lax.ppermute(value, axis, [(i, i ^ mask) for i in range(lax.axis_size(axi...  2.25 us
  transfers between devices with their start and end apart: 11, of which 5 were waited for; matrix products, arithmetic and copies ran while one was open for 1% of the time, Pallas kernels for 29%

profile of v4, /device:TPU:0, one launch (start us, length us, event | category | flops | bytes accessed | tf_op | source)
XLA Modules:
  0.0 70.4 jit_solution(5389611598357343059)
XLA Ops:
  0.0 0.0 copy-start.4
  0.0 0.0 copy-start.3
  0.0 0.9 %tail_rows.1 = bf16[16,2304]{1,0:T(8,128)(2,1)S(1)} custom-call(bf16[2560,2048]{1,0:T(8,128)(2,1)} %feat_ref.3, bf16[2560,128]{1,0:T(8,128)(2,1)} %write_ref.3, bf16[2560,128]{1,0:T(8,128)(2,1)} %read_ref.3), custom_call_target="tpu_custom_call" | custom-call | tf_op jit(solution)/shard_map/tail_rows/pallas_call | solution.py:155
  0.9 0.0 copy-start.1
  0.9 0.0 copy-start.2
  0.9 3.0 %collective-permute-start = (bf16[16,2304]{1,0:T(8,128)(2,1)S(1)}, bf16[16,2304]{1,0:T(8,128)(2,1)S(1)}, u32[]{:S(2)}, u32[]{:S(2)}) collective-permute-start(bf16[16,2304]{1,0:T(8,128)(2,1)S(1)} %tail_rows.1), channel_id=1, source_target_pairs={{0,4},{4,8},{8,12},{12,16},{16,20},{20,24},{24,28},{28,0},{1,5},{5... | collective-permute-start | bytes 221192 | tf_op jit(solution)/shard_map/ppermute | solution.py:551
  4.0 0.0 copy-done.4
  4.0 0.4 copy.9.ld_ref
  4.4 0.1 pad_add_fusion.place_ref._
  4.4 0.0 copy-done.3
  4.4 4.0 %decay_prep.1 = (f32[2560,128]{1,0:T(8,128)S(1)}, bf16[2560,128]{1,0:T(8,128)(2,1)S(1)}, f32[24,2048]{1,0:T(8,128)S(1)}, bf16[128,2048]{1,0:T(8,128)(2,1)S(1)}, bf16[128,2048]{1,0:T(8,128)(2,1)S(1)}) custom-call(f32[2560,32]{1,0:T(8,128)S(1)} %copy.9.ld_ref, f32[1,32]{1,0:T(1,128)S(1)} %bitcast.12), custom_call_target="tpu_custom_call" | custom-call | flops 1000000000 | bytes 5000000 | tf_op jit(solution)/shard_map/decay_prep/pallas_call | solution.py:125
  8.4 0.9 %collective-permute-done.halo_ref = bf16[16,2304]{1,0:T(8,128)(2,1)S(1)} collective-permute-done((bf16[16,2304]{1,0:T(8,128)(2,1)S(1)}, bf16[16,2304]{1,0:T(8,128)(2,1)S(1)}, u32[]{:S(2)}, u32[]{:S(2)}) %collective-permute-start) | collective-permute-done | bytes 73760 | tf_op jit(solution)/shard_map/ppermute | solution.py:551
  9.3 0.0 copy-done.1
  9.3 0.0 copy-done.2
  9.3 17.8 %conv_states.1 = (f32[2560,768]{1,0:T(8,128)S(1)}, f32[2560,768]{1,0:T(8,128)S(1)}, f32[2560,512]{1,0:T(8,128)S(1)}, bf16[128,2560]{1,0:T(8,128)(2,1)S(1)}, bf16...) custom-call(s32[4]{0:T(128)S(1)} %pad_add_fusion.place_ref._, ...), custom_call_target="tpu_custom_call" | custom-call | flops 10000000000 | bytes 10000000 | tf_op jit(solution)/shard_map/conv_states/pallas_call | solution.py:293
  27.2 1.7 %collective-permute-start.3 = (bf16[144,512]{1,0:T(8,128)(2,1)S(1)}, bf16[144,512]{1,0:T(8,128)(2,1)S(1)}, u32[]{:S(2)}, u32[]{:S(2)}) collective-permute-start(bf16[144,512]{1,0:T(8,128)(2,1)S(1)} %get-tuple-element.49), channel_id=1, source_target_pairs={{0,12},{4,8},{8,4},{12,0},{16,28},{20,24},{24,20},{28,16},{1,13},{... | collective-permute-start | bytes 442376 | tf_op jit(solution)/shard_map/ppermute | solution.py:555
  28.9 0.4 collective-permute-start.2
  29.4 1.4 %collective-permute-start.1 = (bf16[144,512]{1,0:T(8,128)(2,1)S(1)}, bf16[144,512]{1,0:T(8,128)(2,1)S(1)}, u32[]{:S(2)}, u32[]{:S(2)}) collective-permute-start(bf16[144,512]{1,0:T(8,128)(2,1)S(1)} %get-tuple-element.51), channel_id=1, source_target_pairs={{0,4},{4,0},{8,12},{12,8},{16,20},{20,16},{24,28},{28,24},{1,5},{5... | collective-permute-start | bytes 442376 | tf_op jit(solution)/shard_map/ppermute | solution.py:555
  30.8 0.4 block_scores.1.sc_ref
  31.1 5.7 %within.3.refs_0_ = f32[2560,768]{1,0:T(8,128)S(1)} custom-call(s32[4]{0:T(128)S(1)} %pad_add_fusion.place_ref._, f32[2560,768]{1,0:T(8,128)S(1)} %get-tuple-element.40.x_ref, bf16[2560,256]{1,0:T(8,128)(2,1)S(1)} %block_scores.1.sc_ref, bf16[128,2560]{1,0:T(8,128)(2,1)S(1)} %get-tuple-element.41.wt_ref, f32[2560,128]{1,0:T(8,128)S(1)} %get-tuple-element.27.table_ref, ...), custom_call_target="tpu_custom_call" | custom-call | flops 2000000000 | bytes 31457280 | tf_op jit(solution)/shard_map/within/pallas_call | solution.py:376
  36.8 0.0 collective-permute-done.3.r3_ref
  36.8 0.0 collective-permute-done.2.r2_ref
  36.9 0.0 collective-permute-done.1.r1_ref
  36.9 0.8 %group_prefix.1 = (bf16[144,512]{1,0:T(8,128)(2,1)S(1)}, f32[4,128,512]{2,1,0:T(8,128)S(1)}, f32[8,512]{1,0:T(8,128)S(1)}) custom-call(s32[4]{0:T(128)S(1)} %pad_add_fusion.place_ref._, bf16[4,144,512]{2,1,0:T(8,128)(2,1)S(1)} %get-tuple-element.32.msg_ref, bf16[144,512]{1,0:T(8,128)(2,1)S(1)} %collective-permute-done.1.r1_ref, ...), custom_call_target="tpu_custom_call" | custom-call | tf_op jit(solution)/shard_map/group_prefix/pallas_call | solution.py:411
  37.7 1.8 %collective-permute-start.4 = (bf16[144,512]{1,0:T(8,128)(2,1)S(1)}, bf16[144,512]{1,0:T(8,128)(2,1)S(1)}, u32[]{:S(2)}, u32[]{:S(2)}) collective-permute-start(bf16[144,512]{1,0:T(8,128)(2,1)S(1)} %get-tuple-element.35._), channel_id=1, source_target_pairs={{0,16},{4,20},{8,24},{12,28},{16,0},{20,4},{24,8},{28,12},{1,17},{... | collective-permute-start | bytes 442376 | tf_op jit(solution)/shard_map/ppermute | solution.py:551
  39.4 5.7 %within.4.refs_1_ = f32[2560,768]{1,0:T(8,128)S(1)} custom-call(bf16[144,512]{1,0:T(8,128)(2,1)S(1)} %get-tuple-element.35._, f32[2560,768]{1,0:T(8,128)S(1)} %get-tuple-element.43.x_ref, bf16[2560,256]{1,0:T(8,128)(2,1)S(1)} %block_scores.1.sc_ref, bf16[128,2560]{1,0:T(8,128)(2,1)S(1)} %get-tuple-element.41.wt_ref, ...), custom_call_target="tpu_custom_call" | custom-call | flops 2000000000 | bytes 31457280 | tf_op jit(solution)/shard_map/within/pallas_call | solution.py:376
  45.1 0.6 collective-permute-done.4.carried_ref
  45.7 0.6 spread.1
  46.4 1.8 %collective-permute-start.5 = (bf16[128,512]{1,0:T(8,128)(2,1)S(1)}, bf16[128,512]{1,0:T(8,128)(2,1)S(1)}, u32[]{:S(2)}, u32[]{:S(2)}) collective-permute-start(bf16[128,512]{1,0:T(8,128)(2,1)S(1)} %get-tuple-element.37), channel_id=1, source_target_pairs={{0,4},{4,0},{8,12},{12,8},{16,20},{20,16},{24,28},{28,24},{1,5},{5... | collective-permute-start | bytes 393224 | tf_op jit(solution)/shard_map/ppermute | solution.py:555
  48.2 0.0 collective-permute-start.6
  48.3 1.7 %collective-permute-start.7 = (bf16[128,512]{1,0:T(8,128)(2,1)S(1)}, bf16[128,512]{1,0:T(8,128)(2,1)S(1)}, u32[]{:S(2)}, u32[]{:S(2)}) collective-permute-start(bf16[128,512]{1,0:T(8,128)(2,1)S(1)} %get-tuple-element.39), channel_id=1, source_target_pairs={{0,12},{4,8},{8,4},{12,0},{16,28},{20,24},{24,20},{28,16},{1,13},{... | collective-permute-start | bytes 393224 | tf_op jit(solution)/shard_map/ppermute | solution.py:555
  50.0 4.6 %within.5.refs_2_ = f32[2560,512]{1,0:T(8,128)S(1)} custom-call(bf16[128,512]{1,0:T(8,128)(2,1)S(1)} %get-tuple-element.36._.s0, f32[2560,512]{1,0:T(8,128)S(1)} %get-tuple-element.44.x_ref, bf16[2560,256]{1,0:T(8,128)(2,1)S(1)} %block_scores.1.sc_ref, bf16[128,2560]{1,0:T(8,128)(2,1)S(1)} %get-tuple-element.41.wt_ref, ...), custom_call_target="tpu_custom_call" | custom-call | flops 2000000000 | bytes 20971520 | tf_op jit(solution)/shard_map/within/pallas_call | solution.py:376
  54.5 0.0 collective-permute-done.5.s1
  54.5 0.0 collective-permute-done.6.s2
  54.5 0.3 collective-permute-done.7.s3
  54.9 0.0 copy-start
  54.9 6.6 %add_states.1 = (bf16[2560,768]{1,0:T(8,128)(2,1)S(1)}, bf16[2560,768]{1,0:T(8,128)(2,1)S(1)}, bf16[2560,512]{1,0:T(8,128)(2,1)S(1)}, f32[20,128]{1,0:T(8,128)S(1)}) custom-call(s32[4]{0:T(128)S(1)} %pad_add_fusion.place_ref._, bf16[2560,128]{1,0:T(8,128)(2,1)S(1)} %get-tuple-element.29.c_ref, f32[2560,128]{1,0:T(8,128)S(1)} %get-tuple-element.27.table_ref, ...), custom_call_target="tpu_custom_call" | custom-call | tf_op jit(solution)/shard_map/add_states/pallas_call | solution.py:487
  61.5 0.1 collective-permute-start.10
  61.6 1.5 %collective-permute-start.9 = (f32[20,128]{1,0:T(8,128)S(1)}, f32[20,128]{1,0:T(8,128)S(1)}, u32[]{:S(2)}, u32[]{:S(2)}) collective-permute-start(f32[20,128]{1,0:T(8,128)S(1)} %get-tuple-element.48.refs_3_), channel_id=1, source_target_pairs={{0,2},{1,3},{2,0},{3,1},{4,6},{5,7},{6,4},{7,5},{8,10},{9,11},{10,... | collective-permute-start | bytes 30728 | tf_op jit(solution)/shard_map/ppermute | solution.py:555
  63.1 0.3 collective-permute-start.8
  63.4 1.4 %collective-permute-done.10.refs_6_ = f32[20,128]{1,0:T(8,128)S(1)} collective-permute-done((f32[20,128]{1,0:T(8,128)S(1)}, f32[20,128]{1,0:T(8,128)S(1)}, u32[]{:S(2)}, u32[]{:S(2)}) %collective-permute-start.10) | collective-permute-done | bytes 10272 | tf_op jit(solution)/shard_map/ppermute | solution.py:555
  64.8 0.5 collective-permute-done.9.refs_5_
  65.3 0.0 collective-permute-done.8.refs_4_
  65.3 0.0 copy-done
  65.4 4.9 %norm.1 = bf16[2560,2048]{1,0:T(8,128)(2,1)} custom-call(f32[1,2048]{1,0:T(1,128)S(1)} %bitcast.11, bf16[2560,768]{1,0:T(8,128)(2,1)S(1)} %get-tuple-element.45.refs_0_, bf16[2560,768]{1,0:T(8,128)(2,1)S(1)} %get-tuple-element.46.refs_1_, bf16[2560,512]{1,0:T(8,128)(2,1)S(1)} %get-tuple-element.47.refs_2_, f32[20,128]{1,0:T(8,128)S(1)} %get-tuple-element.48.refs_3_, ...), custom_call_target="tpu_custom_call" | custom-call | tf_op jit(solution)/shard_map/norm/pallas_call | solution.py:534
  (1 shorter events, 0.0 us)
Async XLA Ops:
  0.0 4.0 %copy-start.4 = (f32[2560,32]{0,1:T(8,128)S(1)}, f32[2560,32]{0,1:T(8,128)}, u32[]{:S(2)}) copy-start(f32[2560,32]{0,1:T(8,128)} %param.13) | copy-start | bytes 983044
  0.0 4.4 %copy-start.3 = (f32[32]{0:T(128)S(1)}, f32[32]{0:T(128)}, u32[]{:S(2)}) copy-start(f32[32]{0:T(128)} %param.14) | copy-start | bytes 388
  0.9 8.4 %copy-start.1 = (f32[4,2048]{1,0:T(4,128)S(1)}, f32[4,2048]{1,0:T(4,128)}, u32[]{:S(2)}) copy-start(f32[4,2048]{1,0:T(4,128)} %taps_ref.1) | copy-start | bytes 98308
  0.9 8.4 %copy-start.2 = (f32[4,256]{1,0:T(4,128)S(1)}, f32[4,256]{1,0:T(4,128)}, u32[]{:S(2)}) copy-start(f32[4,256]{1,0:T(4,128)} %state_taps_ref.1) | copy-start | bytes 12292
  0.9 8.4 %collective-permute-start = (bf16[16,2304]{1,0:T(8,128)(2,1)S(1)}, bf16[16,2304]{1,0:T(8,128)(2,1)S(1)}, u32[]{:S(2)}, u32[]{:S(2)}) collective-permute-start(bf16[16,2304]{1,0:T(8,128)(2,1)S(1)} %tail_rows.1), channel_id=1, source_target_pairs={{0,4},{4,8},{8,12},{12,16},{16,20},{20,24},{24,28},{28,0},{1,5},{5... | collective-permute-start | bytes 221192 | tf_op jit(solution)/shard_map/ppermute | solution.py:551
  27.2 9.6 %collective-permute-start.3 = (bf16[144,512]{1,0:T(8,128)(2,1)S(1)}, bf16[144,512]{1,0:T(8,128)(2,1)S(1)}, u32[]{:S(2)}, u32[]{:S(2)}) collective-permute-start(bf16[144,512]{1,0:T(8,128)(2,1)S(1)} %get-tuple-element.49), channel_id=1, source_target_pairs={{0,12},{4,8},{8,4},{12,0},{16,28},{20,24},{24,20},{28,16},{1,13},{... | collective-permute-start | bytes 442376 | tf_op jit(solution)/shard_map/ppermute | solution.py:555
  28.9 7.9 %collective-permute-start.2 = (bf16[144,512]{1,0:T(8,128)(2,1)S(1)}, bf16[144,512]{1,0:T(8,128)(2,1)S(1)}, u32[]{:S(2)}, u32[]{:S(2)}) collective-permute-start(bf16[144,512]{1,0:T(8,128)(2,1)S(1)} %get-tuple-element.50), channel_id=1, source_target_pairs={{0,8},{4,12},{8,0},{12,4},{16,24},{20,28},{24,16},{28,20},{1,9},{5... | collective-permute-start | bytes 442376 | tf_op jit(solution)/shard_map/ppermute | solution.py:555
  29.4 7.5 %collective-permute-start.1 = (bf16[144,512]{1,0:T(8,128)(2,1)S(1)}, bf16[144,512]{1,0:T(8,128)(2,1)S(1)}, u32[]{:S(2)}, u32[]{:S(2)}) collective-permute-start(bf16[144,512]{1,0:T(8,128)(2,1)S(1)} %get-tuple-element.51), channel_id=1, source_target_pairs={{0,4},{4,0},{8,12},{12,8},{16,20},{20,16},{24,28},{28,24},{1,5},{5... | collective-permute-start | bytes 442376 | tf_op jit(solution)/shard_map/ppermute | solution.py:555
  37.7 8.1 %collective-permute-start.4 = (bf16[144,512]{1,0:T(8,128)(2,1)S(1)}, bf16[144,512]{1,0:T(8,128)(2,1)S(1)}, u32[]{:S(2)}, u32[]{:S(2)}) collective-permute-start(bf16[144,512]{1,0:T(8,128)(2,1)S(1)} %get-tuple-element.35._), channel_id=1, source_target_pairs={{0,16},{4,20},{8,24},{12,28},{16,0},{20,4},{24,8},{28,12},{1,17},{... | collective-permute-start | bytes 442376 | tf_op jit(solution)/shard_map/ppermute | solution.py:551
  46.4 8.1 %collective-permute-start.5 = (bf16[128,512]{1,0:T(8,128)(2,1)S(1)}, bf16[128,512]{1,0:T(8,128)(2,1)S(1)}, u32[]{:S(2)}, u32[]{:S(2)}) collective-permute-start(bf16[128,512]{1,0:T(8,128)(2,1)S(1)} %get-tuple-element.37), channel_id=1, source_target_pairs={{0,4},{4,0},{8,12},{12,8},{16,20},{20,16},{24,28},{28,24},{1,5},{5... | collective-permute-start | bytes 393224 | tf_op jit(solution)/shard_map/ppermute | solution.py:555
  48.2 6.3 %collective-permute-start.6 = (bf16[128,512]{1,0:T(8,128)(2,1)S(1)}, bf16[128,512]{1,0:T(8,128)(2,1)S(1)}, u32[]{:S(2)}, u32[]{:S(2)}) collective-permute-start(bf16[128,512]{1,0:T(8,128)(2,1)S(1)} %get-tuple-element.38), channel_id=1, source_target_pairs={{0,8},{4,12},{8,0},{12,4},{16,24},{20,28},{24,16},{28,20},{1,9},{5... | collective-permute-start | bytes 393224 | tf_op jit(solution)/shard_map/ppermute | solution.py:555
  48.3 6.6 %collective-permute-start.7 = (bf16[128,512]{1,0:T(8,128)(2,1)S(1)}, bf16[128,512]{1,0:T(8,128)(2,1)S(1)}, u32[]{:S(2)}, u32[]{:S(2)}) collective-permute-start(bf16[128,512]{1,0:T(8,128)(2,1)S(1)} %get-tuple-element.39), channel_id=1, source_target_pairs={{0,12},{4,8},{8,4},{12,0},{16,28},{20,24},{24,20},{28,16},{1,13},{... | collective-permute-start | bytes 393224 | tf_op jit(solution)/shard_map/ppermute | solution.py:555
  54.9 10.5 %copy-start = (f32[2048]{0:T(1024)S(1)}, f32[2048]{0:T(1024)}, u32[]{:S(2)}) copy-start(f32[2048]{0:T(1024)} %param.15) | copy-start | bytes 24580
  61.5 3.3 %collective-permute-start.10 = (f32[20,128]{1,0:T(8,128)S(1)}, f32[20,128]{1,0:T(8,128)S(1)}, u32[]{:S(2)}, u32[]{:S(2)}) collective-permute-start(f32[20,128]{1,0:T(8,128)S(1)} %get-tuple-element.48.refs_3_), channel_id=1, source_target_pairs={{0,3},{1,2},{2,1},{3,0},{4,7},{5,6},{6,5},{7,4},{8,11},{9,10},{10,... | collective-permute-start | bytes 30728 | tf_op jit(solution)/shard_map/ppermute | solution.py:555
  61.6 3.8 %collective-permute-start.9 = (f32[20,128]{1,0:T(8,128)S(1)}, f32[20,128]{1,0:T(8,128)S(1)}, u32[]{:S(2)}, u32[]{:S(2)}) collective-permute-start(f32[20,128]{1,0:T(8,128)S(1)} %get-tuple-element.48.refs_3_), channel_id=1, source_target_pairs={{0,2},{1,3},{2,0},{3,1},{4,6},{5,7},{6,4},{7,5},{8,10},{9,11},{10,... | collective-permute-start | bytes 30728 | tf_op jit(solution)/shard_map/ppermute | solution.py:555
  63.1 2.2 %collective-permute-start.8 = (f32[20,128]{1,0:T(8,128)S(1)}, f32[20,128]{1,0:T(8,128)S(1)}, u32[]{:S(2)}, u32[]{:S(2)}) collective-permute-start(f32[20,128]{1,0:T(8,128)S(1)} %get-tuple-element.48.refs_3_), channel_id=1, source_target_pairs={{0,1},{1,0},{2,3},{3,2},{4,5},{5,4},{6,7},{7,6},{8,9},{9,8},{10,11... | collective-permute-start | bytes 30728 | tf_op jit(solution)/shard_map/ppermute | solution.py:555

commit v5 on v4

--- a/solution.py
+++ b/solution.py
@@ -15,6 +15,7 @@
 RING = 4
 GROUP = 4
 UNROLL = 4
+TOGETHER = 4
 MXU_CHUNKS = (1,3,5,7)
 F32 = jnp.float32
 BF16 = jnp.bfloat16
@@ -199,7 +200,7 @@
     rings = [(feat_ref, feat_ring), (write_ref, write_ring), (read_ref, read_ring)]
 
     def copies(b, source=0):
-        slot = lax.rem(b, RING)
+        slot = lax.rem(b, 2 * TOGETHER)
         at = pl.ds(pl.multiple_of(source * SUB, SUB), SUB)
         return [
             pltpu.make_async_copy(ref.at[at, :], ring.at[slot], sems.at[n, slot])
@@ -210,7 +211,7 @@
         for copy in copies(b, source):
             copy.start()
 
-    for b in range(2):
+    for b in range(TOGETHER):
         start(jnp.int32(b), b)
     halo = halo_ref[...].astype(F32) * place_ref[1].astype(F32)
     for n, buf in enumerate(bufs):
@@ -232,7 +233,7 @@
     def block(b, half, wt_before):
         here = pl.ds(pl.multiple_of(b * SUB, SUB), SUB)
         inside = pl.ds(half * SUB, SUB)
-        slot = lax.rem(b, RING)
+        slot = lax.rem(b, 2 * TOGETHER)
         table = table_ref[here, :]
 
         def conv(now, n, taps, tile):
@@ -255,23 +256,23 @@
                 if part == parts // 2:
                     states()
             x = conv(wide[:, lane : lane + 128], n, taps_ref, n)
-            x_ref[here, pl.ds(spot * 128, 128)] = x
+            x_ref[here, pl.ds(spot * 128, 128)] = x.astype(x_ref.dtype)
             held[part][inside, pl.ds(lane, 128)] = (x * per_head(table, 2, heads, head_dim, n)).astype(BF16)
 
-    def pair(i, _):
-        first = 2 * i
-        for b in (first, first + 1):
-            for copy in copies(b):
+    def step(i, _):
+        first = TOGETHER * i
+        for k in range(TOGETHER):
+            for copy in copies(first + k):
                 copy.wait()
-        for b in (first + 2, first + 3):
-            start(b, jnp.minimum(b, blocks - 1))
+        for k in range(TOGETHER, 2 * TOGETHER):
+            start(first + k, jnp.minimum(first + k, blocks - 1))
         wt_before = wt_held[...]
-        block(first, 0, wt_before)
-        block(first + 1, 1, None)
+        for k in range(TOGETHER):
+            block(first + k, k, wt_before)
         return 0
 
-    lax.fori_loop(0, blocks // 2, pair, 0)
-    for b in range(blocks, blocks + 2):
+    lax.fori_loop(0, blocks // TOGETHER, step, 0)
+    for b in range(blocks, blocks + TOGETHER):
         for copy in copies(jnp.int32(b)):
             copy.wait()
     wt = wt_held[...]
@@ -294,7 +295,7 @@
         functools.partial(conv_kernel, heads, count),
         in_specs=[SMEM, VMEM] + [ANY] * 3 + [VMEM] * 4,
         out_specs=[VMEM] * (len(parts) + 3),
-        out_shape=[pltpu.VMEM((tokens, part), F32) for part in parts]
+        out_shape=[pltpu.VMEM((tokens, part), F32 if n == 2 else BF16) for n, part in enumerate(parts)]
         + [
             pltpu.VMEM((state, tokens), BF16),
             pltpu.VMEM((tokens, state), BF16),
@@ -302,15 +303,15 @@
         ],
         scratch_shapes=[
             pltpu.VMEM((GROUP, state, quarter), F32),
-            pltpu.VMEM((state, 2 * SUB), BF16),
-            pltpu.VMEM((RING, SUB, channels), BF16),
-            pltpu.VMEM((RING, SUB, state), BF16),
-            pltpu.VMEM((RING, SUB, state), BF16),
-            pltpu.SemaphoreType.DMA((3, RING)),
+            pltpu.VMEM((state, TOGETHER * SUB), BF16),
+            pltpu.VMEM((2 * TOGETHER, SUB, channels), BF16),
+            pltpu.VMEM((2 * TOGETHER, SUB, state), BF16),
+            pltpu.VMEM((2 * TOGETHER, SUB, state), BF16),
+            pltpu.SemaphoreType.DMA((3, 2 * TOGETHER)),
         ]
         + [pltpu.VMEM((SUB + 48, 128), F32)] * count
-        + [pltpu.VMEM((2 * SUB, WIDE), BF16)] * (channels // WIDE),
-        compiler_params=pltpu.CompilerParams(vmem_limit_bytes=8 * MIB),
+        + [pltpu.VMEM((TOGETHER * SUB, WIDE), BF16)] * (channels // WIDE),
+        compiler_params=pltpu.CompilerParams(vmem_limit_bytes=14 * MIB),
         cost_estimate=pl.CostEstimate(flops=10**10, bytes_accessed=10**7, transcendentals=10**6),
         name="conv_states",
     )(place, halo, *map(in_hbm, (features, state_write, state_read)), conv_feat, conv_state, table, rows)
@@ -355,7 +356,7 @@
             cols = pl.ds(offset + n * WIDE, WIDE)
             here = pl.ds(n * WIDE, WIDE)
             tiles = [(offset + n * WIDE + lane) // 128 for lane in range(0, WIDE, 128)]
-            x = x_ref[at, here]
+            x = x_ref[at, here].astype(F32)
             bx = (x * jnp.concatenate([per_head(table, 1, heads, head_dim, t) for t in tiles], axis=1)).astype(BF16)
             now = start[n]
             inner = dot(sc, jnp.concatenate([bx, now.astype(BF16)], axis=0))

time: 70.6 us -> 70.3 us (level)
  no operation moved by 1% of the time
where the time goes in v5:
time: 70.3 us; the launch traced here: 70.1 us
  Pallas kernels  51.9 us (74%)
  starting transfers between devices  13.8 us (20%)
  waiting for transfers between devices  3.5 us (5%)
    pallas_call x1, Pallas kernels, conv_states(): pl.pallas_call(functools.partial(conv_kernel, heads, count), in_specs=[SM...  17.2 us
    pallas_call x3, Pallas kernels, within(): pl.pallas_call(functools.partial(within_kernel, offset, heads), in_specs=...  16.3 us
    ppermute x9, starting transfers between devices, partner(): lax.ppermute(value, axis, [(i, i ^ mask) for i in range(lax.axis_size(axi...  9.03 us
    pallas_call x1, Pallas kernels, add_states(): pl.pallas_call(functools.partial(state_kernel, len(ms), heads), in_specs=...  6.85 us
    pallas_call x1, Pallas kernels, norm(): pl.pallas_call(functools.partial(norm_kernel, size, len(ms)), in_specs=[V...  4.89 us
    ppermute x2, starting transfers between devices, later(): lax.ppermute(value, 'seq', [(i, (i + steps) % count) for i in range(count)])  4.78 us
    pallas_call x1, Pallas kernels, decay_prep(): pl.pallas_call(functools.partial(decay_kernel, heads), in_specs=[VMEM, VM...  3.95 us
    ppermute x9, waiting for transfers between devices, partner(): lax.ppermute(value, axis, [(i, i ^ mask) for i in range(lax.axis_size(axi...  2.2 us
  transfers between devices with their start and end apart: 11, of which 5 were waited for; matrix products, arithmetic and copies ran while one was open for 1% of the time, Pallas kernels for 29%

profile of v5, /device:TPU:0, one launch (start us, length us, event | category | flops | bytes accessed | tf_op | source)
XLA Modules:
  0.0 70.1 jit_solution(576653555709901807)
XLA Ops:
  0.0 0.0 copy-start.4
  0.0 0.0 copy-start.3
  0.0 0.9 %tail_rows.1 = bf16[16,2304]{1,0:T(8,128)(2,1)S(1)} custom-call(bf16[2560,2048]{1,0:T(8,128)(2,1)} %feat_ref.3, bf16[2560,128]{1,0:T(8,128)(2,1)} %write_ref.3, bf16[2560,128]{1,0:T(8,128)(2,1)} %read_ref.3), custom_call_target="tpu_custom_call" | custom-call | tf_op jit(solution)/shard_map/tail_rows/pallas_call | solution.py:156
  0.9 0.0 copy-start.1
  0.9 0.0 copy-start.2
  0.9 3.0 %collective-permute-start = (bf16[16,2304]{1,0:T(8,128)(2,1)S(1)}, bf16[16,2304]{1,0:T(8,128)(2,1)S(1)}, u32[]{:S(2)}, u32[]{:S(2)}) collective-permute-start(bf16[16,2304]{1,0:T(8,128)(2,1)S(1)} %tail_rows.1), channel_id=1, source_target_pairs={{0,4},{4,8},{8,12},{12,16},{16,20},{20,24},{24,28},{28,0},{1,5},{5... | collective-permute-start | bytes 221192 | tf_op jit(solution)/shard_map/ppermute | solution.py:552
  4.0 0.0 copy-done.4
  4.0 0.4 copy.9.ld_ref
  4.4 0.1 pad_add_fusion.place_ref._
  4.4 0.0 copy-done.3
  4.4 4.0 %decay_prep.1 = (f32[2560,128]{1,0:T(8,128)S(1)}, bf16[2560,128]{1,0:T(8,128)(2,1)S(1)}, f32[24,2048]{1,0:T(8,128)S(1)}, bf16[128,2048]{1,0:T(8,128)(2,1)S(1)}, bf16[128,2048]{1,0:T(8,128)(2,1)S(1)}) custom-call(f32[2560,32]{1,0:T(8,128)S(1)} %copy.9.ld_ref, f32[1,32]{1,0:T(1,128)S(1)} %bitcast.12), custom_call_target="tpu_custom_call" | custom-call | flops 1000000000 | bytes 5000000 | tf_op jit(solution)/shard_map/decay_prep/pallas_call | solution.py:126
  8.4 0.9 %collective-permute-done.halo_ref = bf16[16,2304]{1,0:T(8,128)(2,1)S(1)} collective-permute-done((bf16[16,2304]{1,0:T(8,128)(2,1)S(1)}, bf16[16,2304]{1,0:T(8,128)(2,1)S(1)}, u32[]{:S(2)}, u32[]{:S(2)}) %collective-permute-start) | collective-permute-done | bytes 73760 | tf_op jit(solution)/shard_map/ppermute | solution.py:552
  9.3 0.0 copy-done.1
  9.3 0.0 copy-done.2
  9.3 17.2 %conv_states.1 = (bf16[2560,768]{1,0:T(8,128)(2,1)S(1)}, bf16[2560,768]{1,0:T(8,128)(2,1)S(1)}, f32[2560,512]{1,0:T(8,128)S(1)}, bf16[128,2560]{1,0:T(8,128)(2,1...) custom-call(s32[4]{0:T(128)S(1)} %pad_add_fusion.place_ref._, ...), custom_call_target="tpu_custom_call" | custom-call | flops 10000000000 | bytes 10000000 | tf_op jit(solution)/shard_map/conv_states/pallas_call | solution.py:294
  26.6 1.7 %collective-permute-start.3 = (bf16[144,512]{1,0:T(8,128)(2,1)S(1)}, bf16[144,512]{1,0:T(8,128)(2,1)S(1)}, u32[]{:S(2)}, u32[]{:S(2)}) collective-permute-start(bf16[144,512]{1,0:T(8,128)(2,1)S(1)} %get-tuple-element.49), channel_id=1, source_target_pairs={{0,12},{4,8},{8,4},{12,0},{16,28},{20,24},{24,20},{28,16},{1,13},{... | collective-permute-start | bytes 442376 | tf_op jit(solution)/shard_map/ppermute | solution.py:556
  28.3 0.4 collective-permute-start.2
  28.8 1.4 %collective-permute-start.1 = (bf16[144,512]{1,0:T(8,128)(2,1)S(1)}, bf16[144,512]{1,0:T(8,128)(2,1)S(1)}, u32[]{:S(2)}, u32[]{:S(2)}) collective-permute-start(bf16[144,512]{1,0:T(8,128)(2,1)S(1)} %get-tuple-element.51), channel_id=1, source_target_pairs={{0,4},{4,0},{8,12},{12,8},{16,20},{20,16},{24,28},{28,24},{1,5},{5... | collective-permute-start | bytes 442376 | tf_op jit(solution)/shard_map/ppermute | solution.py:556
  30.2 0.4 block_scores.1.sc_ref
  30.5 5.9 %within.3.refs_0_ = f32[2560,768]{1,0:T(8,128)S(1)} custom-call(s32[4]{0:T(128)S(1)} %pad_add_fusion.place_ref._, bf16[2560,768]{1,0:T(8,128)(2,1)S(1)} %get-tuple-element.40.x_ref, bf16[2560,256]{1,0:T(8,128)(2,1)S(1)} %block_scores.1.sc_ref, bf16[128,2560]{1,0:T(8,128)(2,1)S(1)} %get-tuple-element.41.wt_ref, f32[2560,128]{1,0:T(8,128)S(1)} %get-tuple-element.27.table_ref, ...), custom_call_target="tpu_custom_call" | custom-call | flops 2000000000 | bytes 31457280 | tf_op jit(solution)/shard_map/within/pallas_call | solution.py:377
  36.4 0.0 collective-permute-done.3.r3_ref
  36.4 0.0 collective-permute-done.2.r2_ref
  36.4 0.0 collective-permute-done.1.r1_ref
  36.4 0.8 %group_prefix.1 = (bf16[144,512]{1,0:T(8,128)(2,1)S(1)}, f32[4,128,512]{2,1,0:T(8,128)S(1)}, f32[8,512]{1,0:T(8,128)S(1)}) custom-call(s32[4]{0:T(128)S(1)} %pad_add_fusion.place_ref._, bf16[4,144,512]{2,1,0:T(8,128)(2,1)S(1)} %get-tuple-element.32.msg_ref, bf16[144,512]{1,0:T(8,128)(2,1)S(1)} %collective-permute-done.1.r1_ref, ...), custom_call_target="tpu_custom_call" | custom-call | tf_op jit(solution)/shard_map/group_prefix/pallas_call | solution.py:412
  37.2 1.8 %collective-permute-start.4 = (bf16[144,512]{1,0:T(8,128)(2,1)S(1)}, bf16[144,512]{1,0:T(8,128)(2,1)S(1)}, u32[]{:S(2)}, u32[]{:S(2)}) collective-permute-start(bf16[144,512]{1,0:T(8,128)(2,1)S(1)} %get-tuple-element.35._), channel_id=1, source_target_pairs={{0,16},{4,20},{8,24},{12,28},{16,0},{20,4},{24,8},{28,12},{1,17},{... | collective-permute-start | bytes 442376 | tf_op jit(solution)/shard_map/ppermute | solution.py:552
  39.0 5.8 %within.4.refs_1_ = f32[2560,768]{1,0:T(8,128)S(1)} custom-call(bf16[144,512]{1,0:T(8,128)(2,1)S(1)} %get-tuple-element.35._, bf16[2560,768]{1,0:T(8,128)(2,1)S(1)} %get-tuple-element.43.x_ref, bf16[2560,256]{1,0:T(8,128)(2,1)S(1)} %block_scores.1.sc_ref, bf16[128,2560]{1,0:T(8,128)(2,1)S(1)} %get-tuple-element.41.wt_ref, ...), custom_call_target="tpu_custom_call" | custom-call | flops 2000000000 | bytes 31457280 | tf_op jit(solution)/shard_map/within/pallas_call | solution.py:377
  44.8 0.4 collective-permute-done.4.carried_ref
  45.2 0.7 spread.1
  45.9 1.8 %collective-permute-start.5 = (bf16[128,512]{1,0:T(8,128)(2,1)S(1)}, bf16[128,512]{1,0:T(8,128)(2,1)S(1)}, u32[]{:S(2)}, u32[]{:S(2)}) collective-permute-start(bf16[128,512]{1,0:T(8,128)(2,1)S(1)} %get-tuple-element.37), channel_id=1, source_target_pairs={{0,4},{4,0},{8,12},{12,8},{16,20},{20,16},{24,28},{28,24},{1,5},{5... | collective-permute-start | bytes 393224 | tf_op jit(solution)/shard_map/ppermute | solution.py:556
  47.7 0.0 collective-permute-start.6
  47.7 1.8 %collective-permute-start.7 = (bf16[128,512]{1,0:T(8,128)(2,1)S(1)}, bf16[128,512]{1,0:T(8,128)(2,1)S(1)}, u32[]{:S(2)}, u32[]{:S(2)}) collective-permute-start(bf16[128,512]{1,0:T(8,128)(2,1)S(1)} %get-tuple-element.39), channel_id=1, source_target_pairs={{0,12},{4,8},{8,4},{12,0},{16,28},{20,24},{24,20},{28,16},{1,13},{... | collective-permute-start | bytes 393224 | tf_op jit(solution)/shard_map/ppermute | solution.py:556
  49.4 4.6 %within.5.refs_2_ = f32[2560,512]{1,0:T(8,128)S(1)} custom-call(bf16[128,512]{1,0:T(8,128)(2,1)S(1)} %get-tuple-element.36._.s0, f32[2560,512]{1,0:T(8,128)S(1)} %get-tuple-element.44.x_ref, bf16[2560,256]{1,0:T(8,128)(2,1)S(1)} %block_scores.1.sc_ref, bf16[128,2560]{1,0:T(8,128)(2,1)S(1)} %get-tuple-element.41.wt_ref, ...), custom_call_target="tpu_custom_call" | custom-call | flops 2000000000 | bytes 20971520 | tf_op jit(solution)/shard_map/within/pallas_call | solution.py:377
  54.0 0.0 collective-permute-done.5.s1
  54.0 0.0 collective-permute-done.6.s2
  54.0 0.3 collective-permute-done.7.s3
  54.3 0.0 copy-start
  54.3 6.8 %add_states.1 = (bf16[2560,768]{1,0:T(8,128)(2,1)S(1)}, bf16[2560,768]{1,0:T(8,128)(2,1)S(1)}, bf16[2560,512]{1,0:T(8,128)(2,1)S(1)}, f32[20,128]{1,0:T(8,128)S(1)}) custom-call(s32[4]{0:T(128)S(1)} %pad_add_fusion.place_ref._, bf16[2560,128]{1,0:T(8,128)(2,1)S(1)} %get-tuple-element.29.c_ref, f32[2560,128]{1,0:T(8,128)S(1)} %get-tuple-element.27.table_ref, ...), custom_call_target="tpu_custom_call" | custom-call | tf_op jit(solution)/shard_map/add_states/pallas_call | solution.py:488
  61.2 0.1 collective-permute-start.10
  61.3 1.5 %collective-permute-start.9 = (f32[20,128]{1,0:T(8,128)S(1)}, f32[20,128]{1,0:T(8,128)S(1)}, u32[]{:S(2)}, u32[]{:S(2)}) collective-permute-start(f32[20,128]{1,0:T(8,128)S(1)} %get-tuple-element.48.refs_3_), channel_id=1, source_target_pairs={{0,2},{1,3},{2,0},{3,1},{4,6},{5,7},{6,4},{7,5},{8,10},{9,11},{10,... | collective-permute-start | bytes 30728 | tf_op jit(solution)/shard_map/ppermute | solution.py:556
  62.8 0.3 collective-permute-start.8
  63.1 1.4 %collective-permute-done.10.refs_6_ = f32[20,128]{1,0:T(8,128)S(1)} collective-permute-done((f32[20,128]{1,0:T(8,128)S(1)}, f32[20,128]{1,0:T(8,128)S(1)}, u32[]{:S(2)}, u32[]{:S(2)}) %collective-permute-start.10) | collective-permute-done | bytes 10272 | tf_op jit(solution)/shard_map/ppermute | solution.py:556
  64.5 0.5 collective-permute-done.9.refs_5_
  65.0 0.0 collective-permute-done.8.refs_4_
  65.0 0.0 copy-done
  65.0 4.9 %norm.1 = bf16[2560,2048]{1,0:T(8,128)(2,1)} custom-call(f32[1,2048]{1,0:T(1,128)S(1)} %bitcast.11, bf16[2560,768]{1,0:T(8,128)(2,1)S(1)} %get-tuple-element.45.refs_0_, bf16[2560,768]{1,0:T(8,128)(2,1)S(1)} %get-tuple-element.46.refs_1_, bf16[2560,512]{1,0:T(8,128)(2,1)S(1)} %get-tuple-element.47.refs_2_, f32[20,128]{1,0:T(8,128)S(1)} %get-tuple-element.48.refs_3_, ...), custom_call_target="tpu_custom_call" | custom-call | tf_op jit(solution)/shard_map/norm/pallas_call | solution.py:535
  (1 shorter events, 0.0 us)
Async XLA Ops:
  0.0 4.0 %copy-start.4 = (f32[2560,32]{0,1:T(8,128)S(1)}, f32[2560,32]{0,1:T(8,128)}, u32[]{:S(2)}) copy-start(f32[2560,32]{0,1:T(8,128)} %param.13) | copy-start | bytes 983044
  0.0 4.4 %copy-start.3 = (f32[32]{0:T(128)S(1)}, f32[32]{0:T(128)}, u32[]{:S(2)}) copy-start(f32[32]{0:T(128)} %param.14) | copy-start | bytes 388
  0.9 8.4 %copy-start.1 = (f32[4,2048]{1,0:T(4,128)S(1)}, f32[4,2048]{1,0:T(4,128)}, u32[]{:S(2)}) copy-start(f32[4,2048]{1,0:T(4,128)} %taps_ref.1) | copy-start | bytes 98308
  0.9 8.4 %copy-start.2 = (f32[4,256]{1,0:T(4,128)S(1)}, f32[4,256]{1,0:T(4,128)}, u32[]{:S(2)}) copy-start(f32[4,256]{1,0:T(4,128)} %state_taps_ref.1) | copy-start | bytes 12292
  0.9 8.4 %collective-permute-start = (bf16[16,2304]{1,0:T(8,128)(2,1)S(1)}, bf16[16,2304]{1,0:T(8,128)(2,1)S(1)}, u32[]{:S(2)}, u32[]{:S(2)}) collective-permute-start(bf16[16,2304]{1,0:T(8,128)(2,1)S(1)} %tail_rows.1), channel_id=1, source_target_pairs={{0,4},{4,8},{8,12},{12,16},{16,20},{20,24},{24,28},{28,0},{1,5},{5... | collective-permute-start | bytes 221192 | tf_op jit(solution)/shard_map/ppermute | solution.py:552
  26.6 9.8 %collective-permute-start.3 = (bf16[144,512]{1,0:T(8,128)(2,1)S(1)}, bf16[144,512]{1,0:T(8,128)(2,1)S(1)}, u32[]{:S(2)}, u32[]{:S(2)}) collective-permute-start(bf16[144,512]{1,0:T(8,128)(2,1)S(1)} %get-tuple-element.49), channel_id=1, source_target_pairs={{0,12},{4,8},{8,4},{12,0},{16,28},{20,24},{24,20},{28,16},{1,13},{... | collective-permute-start | bytes 442376 | tf_op jit(solution)/shard_map/ppermute | solution.py:556
  28.3 8.1 %collective-permute-start.2 = (bf16[144,512]{1,0:T(8,128)(2,1)S(1)}, bf16[144,512]{1,0:T(8,128)(2,1)S(1)}, u32[]{:S(2)}, u32[]{:S(2)}) collective-permute-start(bf16[144,512]{1,0:T(8,128)(2,1)S(1)} %get-tuple-element.50), channel_id=1, source_target_pairs={{0,8},{4,12},{8,0},{12,4},{16,24},{20,28},{24,16},{28,20},{1,9},{5... | collective-permute-start | bytes 442376 | tf_op jit(solution)/shard_map/ppermute | solution.py:556
  28.8 7.6 %collective-permute-start.1 = (bf16[144,512]{1,0:T(8,128)(2,1)S(1)}, bf16[144,512]{1,0:T(8,128)(2,1)S(1)}, u32[]{:S(2)}, u32[]{:S(2)}) collective-permute-start(bf16[144,512]{1,0:T(8,128)(2,1)S(1)} %get-tuple-element.51), channel_id=1, source_target_pairs={{0,4},{4,0},{8,12},{12,8},{16,20},{20,16},{24,28},{28,24},{1,5},{5... | collective-permute-start | bytes 442376 | tf_op jit(solution)/shard_map/ppermute | solution.py:556
  37.2 8.0 %collective-permute-start.4 = (bf16[144,512]{1,0:T(8,128)(2,1)S(1)}, bf16[144,512]{1,0:T(8,128)(2,1)S(1)}, u32[]{:S(2)}, u32[]{:S(2)}) collective-permute-start(bf16[144,512]{1,0:T(8,128)(2,1)S(1)} %get-tuple-element.35._), channel_id=1, source_target_pairs={{0,16},{4,20},{8,24},{12,28},{16,0},{20,4},{24,8},{28,12},{1,17},{... | collective-permute-start | bytes 442376 | tf_op jit(solution)/shard_map/ppermute | solution.py:552
  45.9 8.1 %collective-permute-start.5 = (bf16[128,512]{1,0:T(8,128)(2,1)S(1)}, bf16[128,512]{1,0:T(8,128)(2,1)S(1)}, u32[]{:S(2)}, u32[]{:S(2)}) collective-permute-start(bf16[128,512]{1,0:T(8,128)(2,1)S(1)} %get-tuple-element.37), channel_id=1, source_target_pairs={{0,4},{4,0},{8,12},{12,8},{16,20},{20,16},{24,28},{28,24},{1,5},{5... | collective-permute-start | bytes 393224 | tf_op jit(solution)/shard_map/ppermute | solution.py:556
  47.7 6.4 %collective-permute-start.6 = (bf16[128,512]{1,0:T(8,128)(2,1)S(1)}, bf16[128,512]{1,0:T(8,128)(2,1)S(1)}, u32[]{:S(2)}, u32[]{:S(2)}) collective-permute-start(bf16[128,512]{1,0:T(8,128)(2,1)S(1)} %get-tuple-element.38), channel_id=1, source_target_pairs={{0,8},{4,12},{8,0},{12,4},{16,24},{20,28},{24,16},{28,20},{1,9},{5... | collective-permute-start | bytes 393224 | tf_op jit(solution)/shard_map/ppermute | solution.py:556
  47.7 6.7 %collective-permute-start.7 = (bf16[128,512]{1,0:T(8,128)(2,1)S(1)}, bf16[128,512]{1,0:T(8,128)(2,1)S(1)}, u32[]{:S(2)}, u32[]{:S(2)}) collective-permute-start(bf16[128,512]{1,0:T(8,128)(2,1)S(1)} %get-tuple-element.39), channel_id=1, source_target_pairs={{0,12},{4,8},{8,4},{12,0},{16,28},{20,24},{24,20},{28,16},{1,13},{... | collective-permute-start | bytes 393224 | tf_op jit(solution)/shard_map/ppermute | solution.py:556
  54.3 10.7 %copy-start = (f32[2048]{0:T(1024)S(1)}, f32[2048]{0:T(1024)}, u32[]{:S(2)}) copy-start(f32[2048]{0:T(1024)} %param.15) | copy-start | bytes 24580
  61.2 3.3 %collective-permute-start.10 = (f32[20,128]{1,0:T(8,128)S(1)}, f32[20,128]{1,0:T(8,128)S(1)}, u32[]{:S(2)}, u32[]{:S(2)}) collective-permute-start(f32[20,128]{1,0:T(8,128)S(1)} %get-tuple-element.48.refs_3_), channel_id=1, source_target_pairs={{0,3},{1,2},{2,1},{3,0},{4,7},{5,6},{6,5},{7,4},{8,11},{9,10},{10,... | collective-permute-start | bytes 30728 | tf_op jit(solution)/shard_map/ppermute | solution.py:556
  61.3 3.8 %collective-permute-start.9 = (f32[20,128]{1,0:T(8,128)S(1)}, f32[20,128]{1,0:T(8,128)S(1)}, u32[]{:S(2)}, u32[]{:S(2)}) collective-permute-start(f32[20,128]{1,0:T(8,128)S(1)} %get-tuple-element.48.refs_3_), channel_id=1, source_target_pairs={{0,2},{1,3},{2,0},{3,1},{4,6},{5,7},{6,4},{7,5},{8,10},{9,11},{10,... | collective-permute-start | bytes 30728 | tf_op jit(solution)/shard_map/ppermute | solution.py:556
  62.8 2.2 %collective-permute-start.8 = (f32[20,128]{1,0:T(8,128)S(1)}, f32[20,128]{1,0:T(8,128)S(1)}, u32[]{:S(2)}, u32[]{:S(2)}) collective-permute-start(f32[20,128]{1,0:T(8,128)S(1)} %get-tuple-element.48.refs_3_), channel_id=1, source_target_pairs={{0,1},{1,0},{2,3},{3,2},{4,5},{5,4},{6,7},{7,6},{8,9},{9,8},{10,11... | collective-permute-start | bytes 30728 | tf_op jit(solution)/shard_map/ppermute | solution.py:556
